TPU v7x, 512 devices: a whole 4x8x8 slice. The times are simulated.
512 devices in a mesh: seq: 8 (over x, core), expert: 64 (over z, y).
Axes of the slice: x: 4, y: 8, z: 8, core: 2. Of those that a mesh axis runs over, the one named last changes fastest.
Arguments:
- dy_values: bfloat16 [64, 128, 4096], P('expert', None, 'seq'), may hold values from -6 to 6
- dy_scales: float32 [64, 128, 32], P('expert', None, 'seq'), may hold values from 0.3 to 3
- route_expert: int32 [64, 128, 8], P('expert'), may hold values from 0 to 63, all different within a row; in each aligned block of 128 rows (0 to 127, 128 to 255, ..., all dimensions but the last counted through in order) at most 20 rows name the same one
- gate_weight: float32 [64, 128, 8], P('expert'), may hold values from 0.05 to 0.5
- saved_pre: bfloat16 [64, 1280, 2, 1024], P('expert', 'seq'), may hold values from -6 to 6
- w_gate: bfloat16 [64, 4096, 1024], P('expert', 'seq'), may hold values from -0.09375 to 0.09375
- w_up: bfloat16 [64, 4096, 1024], P('expert', 'seq'), may hold values from -0.09375 to 0.09375
- w_down: bfloat16 [64, 1024, 4096], P('expert', None, 'seq'), may hold values from -0.1875 to 0.1875
- w_scale: float32 [3, 64, 32, 8], P(None, 'expert', 'seq'), may hold values from 0.5 to 2
Outputs:
- input_grad: bfloat16 [64, 128, 4096], P('expert', None, 'seq')
- down_grad: bfloat16 [64, 1024, 4096], P('expert', None, 'seq')
Inputs may be any that keep to these rules, and one draw needn't show every extreme that they name: `route_expert`: each row names 8 different experts and every expert is named somewhere. Within one group no expert is named by more than 20 entries, and in every draw some expert is named by exactly 20 entries of some group.
All inputs are finite; a program needn't handle non-finite values.
Results may differ from a plain program's by a relative error of at most 0.023.
Values may be sent and summed in bfloat16 or wider, within the bound.
No kernel may reach another device: no remote copies, remote signals or barrier semaphores. Data moves between devices by JAX's collectives and lax.ppermute only.
A program may use at most 64 MiB of HBM per device.

v0:
```python
import jax
import jax.numpy as jnp
from jax import lax
from jax.sharding import PartitionSpec as P


def dequant_rows(values, scales):
    lead = values.shape[:-1]
    blocks = scales.shape[-1]
    width = values.shape[-1]
    grid = values.astype(jnp.float32).reshape(lead + (blocks, width // blocks))
    return (grid * scales[..., None]).reshape(lead + (width,)).astype(jnp.bfloat16)


def dequant_matrix(values, scales):
    rows_in, cols_in = values.shape
    row_blocks, col_blocks = scales.shape
    grid = values.astype(jnp.float32).reshape(
        row_blocks, rows_in // row_blocks, col_blocks, cols_in // col_blocks
    )
    return (grid * scales[:, None, :, None]).reshape(rows_in, cols_in).astype(jnp.bfloat16)


def slot_table(routes, expert_count):
    labels = jnp.arange(expert_count, dtype=jnp.int32)
    onehot = (routes[:, :, None] == labels[None, None, :]).astype(jnp.int32)
    per_token = jnp.sum(onehot, axis=1)
    earlier = jnp.cumsum(per_token, axis=0) - per_token
    return jnp.sum(onehot * earlier[:, None, :], axis=2)


def selection(routes, weights, expert_count, cap_slots):
    slots = slot_table(routes, expert_count)
    target = routes * cap_slots + slots
    places = jnp.arange(expert_count * cap_slots, dtype=jnp.int32)
    match_all = target[None, :, :] == places[:, None, None]
    picked = jnp.sum(
        jnp.where(match_all, weights[None, :, :], jnp.zeros_like(weights)[None, :, :]), axis=2
    )
    plain = jnp.sum(match_all.astype(jnp.float32), axis=2)
    return (picked, plain)


def activations(hidden_grad, saved):
    gate_pre = saved[:, 0, :].astype(jnp.float32)
    up_pre = saved[:, 1, :].astype(jnp.float32)
    gate_sig = jax.nn.sigmoid(gate_pre)
    silu_gate = gate_pre * gate_sig
    hidden_act = (silu_gate * up_pre).astype(jnp.bfloat16)
    up_grad = (hidden_grad * silu_gate).astype(jnp.bfloat16)
    gate_grad = (hidden_grad * up_pre * gate_sig * (1.0 + gate_pre * (1.0 - gate_sig))).astype(
        jnp.bfloat16
    )
    return (gate_grad, up_grad, hidden_act)


def project_back(gate_grad, up_grad, w_gate_eff, w_up_eff):
    contract = (((1,), (1,)), ((), ()))
    result = lax.dot_general(gate_grad, w_gate_eff, contract, preferred_element_type=jnp.float32)
    return result + lax.dot_general(up_grad, w_up_eff, contract, preferred_element_type=jnp.float32)


def shards(
    dy_values, dy_scales, route_expert, gate_weight, saved_pre, w_gate, w_up, w_down, w_scale
):
    seq_count = lax.axis_size("seq")
    expert_count = lax.axis_size("expert")
    cols_dev = dy_values.shape[2]
    rows_dev = saved_pre.shape[1]
    rows_all = rows_dev * seq_count
    cap_slots = rows_all // expert_count
    dy_local = dequant_rows(dy_values[0], dy_scales[0])
    picked, plain = selection(route_expert[0], gate_weight[0], expert_count, cap_slots)
    outgoing = jnp.dot(picked, dy_local.astype(jnp.float32), precision=lax.Precision.HIGHEST)
    outgoing = outgoing.astype(jnp.bfloat16).reshape(expert_count, cap_slots, cols_dev)
    incoming = lax.all_to_all(outgoing, "expert", split_axis=0, concat_axis=0, tiled=True)
    rows = incoming.reshape(rows_all, cols_dev)
    scales = w_scale[:, 0]
    w_gate_eff = dequant_matrix(w_gate[0], scales[0])
    w_up_eff = dequant_matrix(w_up[0], scales[1])
    w_down_eff = dequant_matrix(w_down[0], scales[2].T)
    across = (((1,), (1,)), ((), ()))
    block = rows
    value = lax.dot_general(block, w_down_eff, across, preferred_element_type=jnp.float32)
    hidden_grad = lax.psum_scatter(
        lax.optimization_barrier(value.astype(jnp.bfloat16))
        .astype(jnp.float32)
        .astype(jnp.bfloat16),
        "seq",
        scatter_dimension=0,
        tiled=True,
    ).astype(jnp.float32)
    gate_grad, up_grad, hidden_act = activations(hidden_grad, saved_pre[0])
    stacked = jnp.stack([gate_grad, up_grad, hidden_act])
    piece = lax.all_gather(stacked, "seq", axis=1, tiled=True)
    block = rows
    value = project_back(piece[0], piece[1], w_gate_eff, w_up_eff)
    down_total = lax.dot_general(
        piece[2], block, (((0,), (0,)), ((), ())), preferred_element_type=jnp.float32
    )
    input_rows, down_total = (value, down_total)
    sending = input_rows.astype(jnp.bfloat16).reshape(expert_count, cap_slots, cols_dev)
    returned = lax.all_to_all(sending, "expert", split_axis=0, concat_axis=0, tiled=True)
    combined = jnp.dot(
        plain.T.astype(jnp.bfloat16),
        returned.reshape(expert_count * cap_slots, cols_dev),
        preferred_element_type=jnp.float32,
    )
    return (combined.astype(jnp.bfloat16)[None], down_total.astype(jnp.bfloat16)[None])


def solution(mesh):
    in_specs = (
        P("expert", None, "seq"),
        P("expert", None, "seq"),
        P("expert", None, None),
        P("expert", None, None),
        P("expert", "seq", None, None),
        P("expert", "seq", None),
        P("expert", "seq", None),
        P("expert", None, "seq"),
        P(None, "expert", "seq", None),
    )
    out_specs = (P("expert", None, "seq"), P("expert", None, "seq"))
    return jax.shard_map(shards, mesh=mesh, in_specs=in_specs, out_specs=out_specs, check_vma=False)
```

profile of v0, /device:TPU:1, one launch (start us, length us, event | category | flops | bytes accessed | tf_op | source)
XLA Modules:
  0.0 243.9 jit_solution(10408367651731041336)
XLA Ops:
  7.2 0.0 copy-start.4
  7.2 0.8 convert_reduce_fusion.1
  7.9 0.1 copy.23
  8.0 0.2 reduce_window_sum.11
  8.2 0.1 copy.25
  8.3 0.7 select_reduce_fusion.1
  9.0 0.7 fusion.38
  9.7 0.8 copy.26
  10.5 7.0 %convert_reduce_fusion = (bf16[1280,128]{1,0:T(8,128)(2,1)S(1)}, f32[1280,128]{1,0:T(8,128)S(1)}) fusion(s32[128,8]{0,1:T(8,128)S(1)} %fusion.38, f32[128,8]{0,1:T(8,128)} %bitcast.156), kind=kLoop, calls=%fused_computation.1 | loop fusion | flops 6225920 | bytes 991232 | tf_op jit(solution)/shard_map/reduce_sum | solution.py:40
  17.6 0.2 mul.122
  17.7 0.0 copy-done.4
  17.8 1.2 convolution_convert_fusion.1
  18.9 1.3 reshape.156
  20.3 0.0 copy-start.5
  20.3 17.5 %all-to-all-start = ((bf16[64,20,512]{2,1,0:T(8,128)(2,1)}), bf16[64,20,512]{2,1,0:T(8,128)(2,1)}, u32[]{:S(2)}, u32[]{:S(2)}) async-start(bf16[64,20,512]{2,1,0:T(8,128)(2,1)} %reshape.156), calls=%async_computation | async-start | bytes 3145728 | tf_op jit(solution)/shard_map/all_to_all | solution.py:76
  37.8 0.0 reduce-scatter.2.cloned.1.call-start
  37.8 0.0 copy-done.5
  37.8 0.1 copy.27
  37.9 1.7 reshape.161
  39.7 1.4 multiply_convert_fusion
  41.1 0.0 copy-start.1
  41.1 35.5 %all-to-all-done = bf16[64,20,512]{2,1,0:T(8,128)(2,1)} async-done(((bf16[64,20,512]{2,1,0:T(8,128)(2,1)}), bf16[64,20,512]{2,1,0:T(8,128)(2,1)}, u32[]{:S(2)}, u32[]{:S(2)}) %all-to-all-start) | async-done | bytes 1310752 | tf_op jit(solution)/shard_map/all_to_all | solution.py:76
  76.6 2.3 reshape.157
  78.9 0.0 copy-done.1
  78.9 3.1 %convolution_convert_fusion = bf16[1280,1024]{1,0:T(8,128)(2,1)} fusion(bf16[1280,512]{1,0:T(8,128)(2,1)S(1)} %reshape.157, bf16[128,8,4,128]{3,2,1,0:T(4,128)(2,1)S(1)} %bitcast.151), kind=kOutput, calls=%fused_computation.3 | convolution fusion | flops 1343488000 | bytes 4980736 | tf_op jit(solution)/shard_map/dot_general | solution.py:84
  82.0 0.0 copy-start.3
  82.0 0.0 reduce-scatter.2.cloned.1.call-update
  82.0 0.2 all-gather.2.cloned.1.call-start
  82.2 0.8 copy-done.3
  83.1 0.2 copy.50
  83.2 0.2 fusion.24
  83.5 35.1 %reduce-scatter.2.cloned.1.call-done = bf16[160,1024]{1,0:T(8,128)(2,1)} async-done(((bf16[1280,1024]{1,0:T(8,128)(2,1)}), bf16[160,1024]{1,0:T(8,128)(2,1)}) %reduce-scatter.2.cloned.1.call-update) | async-done | bytes 327696 | tf_op jit(solution)/shard_map/reduce_scatter | solution.py:85
  118.5 1.4 fusion.34
  119.9 1.2 pad_maximum_fusion
  121.0 0.0 all-gather.2.cloned.1.call-update
  121.1 1.5 convert_bitcast_fusion.1
  122.5 0.0 copy-start
  122.6 0.5 copy.31
  123.0 0.7 copy-done
  123.8 0.2 convert_bitcast_fusion
  124.0 0.5 copy.33
  124.5 1.4 fusion.3
  125.9 49.4 %all-gather.2.cloned.1.call-done = bf16[3,1280,1024]{2,1,0:T(8,128)(2,1)} async-done(((bf16[3,160,1024]{2,1,0:T(8,128)(2,1)}), bf16[3,1280,1024]{2,1,0:T(8,128)(2,1)}) %all-gather.2.cloned.1.call-update) | async-done | bytes 7864336 | tf_op jit(solution)/shard_map/all_gather | solution.py:95
  175.3 0.0 copy-start.2
  175.3 3.4 %fusion.2 = f32[1280,512]{1,0:T(8,128)S(1)} fusion(bf16[3,1280,1024]{2,1,0:T(8,128)(2,1)} %all-gather.2.cloned.1.call-done, bf16[64,8,8,128]{3,2,1,0:T(8,128)(2,1)S(1)} %bitcast.153), kind=kOutput, calls=%fused_computation.11 | convolution fusion | flops 1342177280 | bytes 6291456 | tf_op jit(solution)/shard_map/dot_general | solution.py:59
  178.7 0.0 copy-done.2
  178.7 3.4 %fusion = bf16[1280,512]{1,0:T(8,128)(2,1)S(1)} fusion(f32[1280,512]{1,0:T(8,128)S(1)} %fusion.2, bf16[3,1280,1024]{2,1,0:T(8,128)(2,1)} %all-gather.2.cloned.1.call-done, bf16[64,8,8,128]{3,2,1,0:T(8,128)(2,1)S(1)} %bitcast.152), kind=kOutput, calls=%fused_computation.5 | convolution fusion | flops 1343488000 | bytes 7602176 | tf_op jit(solution)/shard_map/dot_general | solution.py:60
  182.1 1.4 reshape.158
  183.5 13.0 %all-to-all-start.1 = ((bf16[64,20,512]{2,1,0:T(8,128)(2,1)}), bf16[64,20,512]{2,1,0:T(8,128)(2,1)S(1)}, u32[]{:S(2)}, u32[]{:S(2)}) async-start(bf16[64,20,512]{2,1,0:T(8,128)(2,1)} %reshape.158), calls=%async_computation.2 | async-start | bytes 3145728 | tf_op jit(solution)/shard_map/all_to_all | solution.py:103
  196.5 4.3 %fusion.6 = bf16[1,1024,512]{2,1,0:T(8,128)(2,1)} fusion(bf16[1280,512]{1,0:T(8,128)(2,1)S(1)} %reshape.157, bf16[3,1280,1024]{2,1,0:T(8,128)(2,1)} %all-gather.2.cloned.1.call-done), kind=kOutput, calls=%fused_computation.20 | convolution fusion | flops 1342701568 | bytes 4980736 | tf_op jit(solution)/shard_map/dot_general | solution.py:98
  200.8 35.0 %all-to-all-done.1 = bf16[64,20,512]{2,1,0:T(8,128)(2,1)S(1)} async-done(((bf16[64,20,512]{2,1,0:T(8,128)(2,1)}), bf16[64,20,512]{2,1,0:T(8,128)(2,1)S(1)}, u32[]{:S(2)}, u32[]{:S(2)}) %all-to-all-start.1) | async-done | bytes 1310752 | tf_op jit(solution)/shard_map/all_to_all | solution.py:103
  235.8 0.3 reshape.159
  236.1 1.0 fusion.7
  (2 shorter events, 0.0 us)
Async XLA Ops:
  7.2 10.6 %copy-start.4 = (bf16[1,128,512]{2,1,0:T(8,128)(2,1)S(1)}, bf16[1,128,512]{2,1,0:T(8,128)(2,1)}, u32[]{:S(2)}) copy-start(bf16[1,128,512]{2,1,0:T(8,128)(2,1)} %param.9) | copy-start | bytes 393220
  20.3 17.6 %copy-start.5 = (f32[3,1,4,8]{3,2,1,0:T(4,128)S(1)}, f32[3,1,4,8]{3,2,1,0:T(4,128)}, u32[]{:S(2)}) copy-start(f32[3,1,4,8]{3,2,1,0:T(4,128)} %param.17) | copy-start | bytes 1156
  20.3 56.4 %all-to-all-start = ((bf16[64,20,512]{2,1,0:T(8,128)(2,1)}), bf16[64,20,512]{2,1,0:T(8,128)(2,1)}, u32[]{:S(2)}, u32[]{:S(2)}) async-start(bf16[64,20,512]{2,1,0:T(8,128)(2,1)} %reshape.156), calls=%async_computation | async-start | bytes 3145728 | tf_op jit(solution)/shard_map/all_to_all | solution.py:76
  37.8 80.8 %reduce-scatter.2.cloned.1.call-start = ((), (), s32[]{:S(2)}) async-start(), calls=%async_computation.3 | async-start | bytes 2949120 | tf_op jit(solution)/shard_map/reduce_scatter | solution.py:85
  41.1 37.8 %copy-start.1 = (bf16[8,128,4,128]{3,2,1,0:T(4,128)(2,1)S(1)}, bf16[8,128,4,128]{3,2,1,0:T(4,128)(2,1)}, u32[]{:S(2)}) copy-start(bf16[8,128,4,128]{3,2,1,0:T(4,128)(2,1)} %multiply_convert_fusion) | copy-start | bytes 3145732
  82.0 1.1 copy-start.3
  82.0 93.3 %all-gather.2.cloned.1.call-start = ((), (), s32[]{:S(2)}) async-start(), calls=%async_computation.4 | async-start | bytes 8847360 | tf_op jit(solution)/shard_map/all_gather | solution.py:95
  122.5 1.2 copy-start
  175.3 3.4 %copy-start.2 = (bf16[4,128,8,128]{3,2,1,0:T(8,128)(2,1)S(1)}, bf16[4,128,8,128]{3,2,1,0:T(8,128)(2,1)}, u32[]{:S(2)}) copy-start(bf16[4,128,8,128]{3,2,1,0:T(8,128)(2,1)} %get-tuple-element.9) | copy-start | bytes 3145732
  183.5 52.3 %all-to-all-start.1 = ((bf16[64,20,512]{2,1,0:T(8,128)(2,1)}), bf16[64,20,512]{2,1,0:T(8,128)(2,1)S(1)}, u32[]{:S(2)}, u32[]{:S(2)}) async-start(bf16[64,20,512]{2,1,0:T(8,128)(2,1)} %reshape.158), calls=%async_computation.2 | async-start | bytes 3145728 | tf_op jit(solution)/shard_map/all_to_all | solution.py:103
Sparse Core Ops, SparseCore 0:
  82.1 36.3 reduce-scatter.1
  121.2 54.0 all-gather.1
where the time goes:
time: 246 us; the launch traced here: 244 us
  waiting for transfers between devices  155 us (63%)
  starting transfers between devices  30.8 us (13%)
  other arithmetic  16.7 us (7%)
  matrix products  16.3 us (7%)
  between operations  14.2 us (6%)
  local copies, waits for them, and re-layouts  10.9 us (4%)
    all_gather x1, waiting for transfers between devices, shards(): piece = lax.all_gather(stacked, 'seq', axis=1, tiled=True)  49.4 us
    all_to_all x1, waiting for transfers between devices, shards(): lax.all_to_all(outgoing, 'expert', split_axis=0, concat_axis=0, tiled=True)  35.5 us
    reduce_scatter x1, waiting for transfers between devices, shards(): lax.psum_scatter(lax.optimization_barrier(value.astype(jnp.bfloat16)).ast...  35.1 us
    all_to_all x1, waiting for transfers between devices, shards(): lax.all_to_all(sending, 'expert', split_axis=0, concat_axis=0, tiled=True)  35 us
    all_to_all x1, starting transfers between devices, shards(): lax.all_to_all(outgoing, 'expert', split_axis=0, concat_axis=0, tiled=True)  17.5 us
    all_to_all x1, starting transfers between devices, shards(): lax.all_to_all(sending, 'expert', split_axis=0, concat_axis=0, tiled=True)  13 us
    reduce_sum x1, other arithmetic, selection(): plain = jnp.sum(match_all.astype(jnp.float32), axis=2)  7.03 us
  transfers between devices with their start and end apart: 4, of which 4 were waited for; matrix products, arithmetic and copies ran while one was open for 5% of the time, Pallas kernels for 0%

commit v1 on v0

v1 whole, which is shorter than its diff:
```python
import functools

import jax
import jax.numpy as jnp
from jax import lax
from jax.experimental import pallas as pl
from jax.experimental.pallas import tpu as pltpu
from jax.sharding import Mesh
from jax.sharding import PartitionSpec as P

EXPERT = ("z", "y")
XS = 4
CHUNKS = 2
HIGHEST = lax.Precision.HIGHEST
NT = (((1,), (1,)), ((), ()))
TN = (((0,), (0,)), ((), ()))
F32 = jnp.float32
BF16 = jnp.bfloat16


def vmem_call(body, out_shape, n_smem, n_in, flops, nbytes, scratch=(), limit=40 << 20):
    smem = pl.BlockSpec(memory_space=pltpu.SMEM)
    vmem = pl.BlockSpec(memory_space=pltpu.VMEM)
    outs = jax.tree.map(lambda _: vmem, out_shape)
    return pl.pallas_call(
        body,
        out_shape=out_shape,
        in_specs=[smem] * n_smem + [vmem] * n_in,
        out_specs=outs,
        scratch_shapes=list(scratch),
        compiler_params=pltpu.CompilerParams(vmem_limit_bytes=limit),
        cost_estimate=pl.CostEstimate(flops=flops, bytes_accessed=nbytes, transcendentals=0),
    )


def dequant_rows(values, scales):
    lead = values.shape[:-1]
    blocks = scales.shape[-1]
    width = values.shape[-1]
    grid = values.astype(F32).reshape(lead + (blocks, width // blocks))
    return (grid * scales[..., None]).reshape(lead + (width,)).astype(BF16)


def dequant_matrix(values, scales):
    rows_in, cols_in = values.shape
    row_blocks, col_blocks = scales.shape
    grid = values.astype(F32).reshape(
        row_blocks, rows_in // row_blocks, col_blocks, cols_in // col_blocks
    )
    return (grid * scales[:, None, :, None]).reshape(rows_in, cols_in).astype(BF16)


def select_body(experts, slots, core_ref, route_ref, weight_ref, pick_ref, gate_ref):
    top, tokens = route_ref.shape
    rows = experts * slots
    label = lax.broadcasted_iota(jnp.int32, (experts, tokens), 0)
    named = jnp.zeros((experts, tokens), F32)
    weight = jnp.zeros((experts, tokens), F32)
    for k in range(top):
        hit = route_ref[k : k + 1, :] == label
        named = named + jnp.where(hit, 1.0, 0.0)
        weight = weight + jnp.where(hit, weight_ref[k : k + 1, :], 0.0)
    before = lax.broadcasted_iota(jnp.int32, (tokens, tokens), 0) < lax.broadcasted_iota(
        jnp.int32, (tokens, tokens), 1
    )
    earlier = jnp.dot(
        named.astype(BF16), jnp.where(before, 1.0, 0.0).astype(BF16), preferred_element_type=F32
    )
    slot = jnp.where(named > 0.0, earlier, -1.0)
    row = lax.broadcasted_iota(jnp.int32, (rows, experts), 0)
    first = lax.broadcasted_iota(jnp.int32, (rows, experts), 1) * slots
    spread = jnp.where((row >= first) & (row < first + slots), 1.0, 0.0)
    slot_row = jnp.dot(spread.astype(BF16), slot.astype(BF16), preferred_element_type=F32)
    weight_row = jnp.dot(spread, weight, precision=HIGHEST, preferred_element_type=F32)
    place = lax.broadcasted_iota(jnp.int32, (rows, tokens), 0).astype(F32)
    place = place - slots * jnp.floor((place + 0.5) * (1.0 / slots))
    base = (core_ref[0] * (slots * CHUNKS)).astype(F32)
    for ch in range(CHUNKS):
        hit = slot_row == place + (base + float(ch * slots))
        pick_ref[ch] = jnp.where(hit, 1.0, 0.0).astype(BF16)
        gate = jnp.sum(jnp.where(hit, weight_row, 0.0), axis=1, keepdims=True)
        gate_ref[ch] = jnp.broadcast_to(gate, (rows, tokens))


def dispatch_body(pick_ref, gate_ref, mine_ref, other_ref, *out_refs):
    half = mine_ref.shape[1]
    for ch in range(CHUNKS):
        pick = pick_ref[ch]
        gate = gate_ref[ch][:, :1]
        out = out_refs[ch]
        out[:, :half] = (jnp.dot(pick, mine_ref[...], preferred_element_type=F32) * gate).astype(BF16)
        out[:, half:] = (jnp.dot(pick, other_ref[...], preferred_element_type=F32) * gate).astype(BF16)


def hidden_body(x_ref, rows_ref, mine_ref, other_ref, own_ref, *send_refs):
    half = mine_ref.shape[1]
    size = own_ref.shape[0]
    for k in range(XS):
        at = pl.multiple_of(lax.rem(x_ref[0] + k, XS) * size, 16)
        rows = rows_ref[pl.ds(at, size), :]
        part = lax.dot_general(rows[:, :half], mine_ref[...], NT, preferred_element_type=F32)
        part = part + lax.dot_general(rows[:, half:], other_ref[...], NT, preferred_element_type=F32)
        if k == 0:
            own_ref[...] = part
        else:
            send_refs[k - 1][...] = part.astype(BF16)


def back_body(x_ref, h0, h1, h2, h3, fac_ref, gm_ref, go_ref, um_ref, uo_ref, out_ref, gate_s, up_s):
    size = h0.shape[0]
    half = gm_ref.shape[0]
    for k, h in enumerate((h0, h1, h2, h3)):
        block = lax.rem(x_ref[0] + (XS - k), XS)
        at = pl.multiple_of(block * size, 16)
        grad = h[...].astype(F32)
        up_s[pl.ds(at, size), :] = (grad * fac_ref[block, 0].astype(F32)).astype(BF16)
        gate_s[pl.ds(at, size), :] = (grad * fac_ref[block, 1].astype(F32)).astype(BF16)
    for lo, g, u in ((0, gm_ref, um_ref), (half, go_ref, uo_ref)):
        total = lax.dot_general(gate_s[...], g[...], NT, preferred_element_type=F32)
        total = total + lax.dot_general(up_s[...], u[...], NT, preferred_element_type=F32)
        out_ref[:, lo : lo + half] = total.astype(BF16)


def swap(value):
    return lax.ppermute(value, "core", [(0, 1), (1, 0)])


def shift(value, k):
    return lax.ppermute(value, "x", [(i, (i + k) % XS) for i in range(XS)])


def shards(
    dy_values, dy_scales, route_expert, gate_weight, saved_pre, w_gate, w_up, w_down, w_scale
):
    core = lax.axis_index("core").astype(jnp.int32)
    xpos = lax.axis_index("x").astype(jnp.int32)[None]
    experts = lax.axis_size(EXPERT)
    tokens, cols = dy_values.shape[1:]
    rows_dev, _, hid = saved_pre.shape[1:]
    width = 2 * cols
    cap = rows_dev * XS * 2 // experts
    slots = cap // 2 // CHUNKS
    rows = experts * slots
    size = rows // XS

    mine = dequant_rows(dy_values[0], dy_scales[0])
    other = swap(mine)
    pick, gate = vmem_call(
        functools.partial(select_body, experts, slots),
        (
            jax.ShapeDtypeStruct((CHUNKS, rows, tokens), BF16),
            jax.ShapeDtypeStruct((CHUNKS, rows, tokens), F32),
        ),
        1, 2, 4 * rows * experts * tokens, 4 << 20,
    )(core[None], route_expert[0].T, gate_weight[0].T)
    outgoing = vmem_call(
        dispatch_body,
        tuple(jax.ShapeDtypeStruct((rows, width), BF16) for _ in range(CHUNKS)),
        0, 4, 2 * CHUNKS * rows * tokens * width, 4 << 20,
    )(pick, gate, mine, other)
    block = (experts, slots * width // 128, 128)
    incoming = []
    for ch in range(CHUNKS):
        got = lax.all_to_all(outgoing[ch].reshape(block), EXPERT, 0, 0, tiled=True)
        incoming.append(got.reshape(rows, width))

    pre = saved_pre[0]
    gate_pre = pre[:, 0, :].astype(F32)
    up_pre = pre[:, 1, :].astype(F32)
    sig = jax.nn.sigmoid(gate_pre)
    silu = gate_pre * sig
    factors = jnp.stack(
        [
            silu.astype(BF16),
            (up_pre * sig * (1.0 + gate_pre * (1.0 - sig))).astype(BF16),
            (silu * up_pre).astype(BF16),
        ]
    )
    groups = rows_dev // cap
    factors = factors.reshape(3, groups, 2, CHUNKS, slots, hid).transpose(2, 0, 3, 1, 4, 5)
    factors = factors.reshape(2, 3, CHUNKS, groups * slots, hid)
    kept = lax.dynamic_index_in_dim(factors, core, 0, keepdims=False)
    came = swap(lax.dynamic_index_in_dim(factors, 1 - core, 0, keepdims=False))
    low = jnp.where(core == 0, kept, came)
    high = jnp.where(core == 0, came, kept)
    factors = jnp.concatenate([low, high], axis=2)
    factors = lax.all_gather(factors, "x", axis=0, tiled=False)

    scales = w_scale[:, 0]
    gate_m = dequant_matrix(w_gate[0], scales[0])
    up_m = dequant_matrix(w_up[0], scales[1])
    down_m = dequant_matrix(w_down[0], scales[2].T)
    down_o = swap(down_m)
    gate_o = swap(gate_m)
    up_o = swap(up_m)

    sent = []
    for ch in range(CHUNKS):
        parts = vmem_call(
            hidden_body,
            (jax.ShapeDtypeStruct((size, hid), F32),)
            + tuple(jax.ShapeDtypeStruct((size, hid), BF16) for _ in range(XS - 1)),
            1, 3, 2 * rows * width * hid, 6 << 20,
        )(xpos, incoming[ch], down_m, down_o)
        total = parts[0]
        for k in (1, 3, 2):
            total = total + shift(parts[k], k).astype(F32)
        grad = total.astype(BF16)
        grads = [grad] + [shift(grad, k) for k in (1, 2, 3)]
        value = vmem_call(
            back_body,
            jax.ShapeDtypeStruct((rows, width), BF16),
            1, 9, 4 * rows * width * hid, 8 << 20,
            scratch=(pltpu.VMEM((rows, hid), BF16), pltpu.VMEM((rows, hid), BF16)),
        )(xpos, *grads, factors[:, :, ch], gate_m, gate_o, up_m, up_o)
        sent.append(lax.all_to_all(value.reshape(block), EXPERT, 0, 0, tiled=True))

    down_total = 0.0
    for ch in range(CHUNKS):
        act = factors[:, 2, ch].reshape(rows, hid)
        down_total = down_total + lax.dot_general(
            act, incoming[ch], TN, preferred_element_type=F32
        )
    down_grad = down_total[:, :cols] + swap(down_total[:, cols:].astype(BF16)).astype(F32)

    combined = 0.0
    for ch in range(CHUNKS):
        combined = combined + lax.dot_general(
            pick[ch], sent[ch].reshape(rows, width), TN, preferred_element_type=F32
        )
    input_grad = combined[:, :cols] + swap(combined[:, cols:])
    return (input_grad.astype(BF16)[None], down_grad.astype(BF16)[None])


def solution(mesh):
    devices = mesh.devices.reshape(XS, 2, 8, 8)
    fine = Mesh(devices, ("x", "core", "z", "y"))
    seq = ("x", "core")
    in_specs = (
        P(EXPERT, None, seq),
        P(EXPERT, None, seq),
        P(EXPERT, None, None),
        P(EXPERT, None, None),
        P(EXPERT, seq, None, None),
        P(EXPERT, seq, None),
        P(EXPERT, seq, None),
        P(EXPERT, None, seq),
        P(None, EXPERT, seq, None),
    )
    out_specs = (P(EXPERT, None, seq), P(EXPERT, None, seq))
    return jax.shard_map(shards, mesh=fine, in_specs=in_specs, out_specs=out_specs, check_vma=False)
```

time: 246 us -> 223 us (0.907)
  waiting for transfers between devices: 155 us -> 36.4 us
  starting transfers between devices: 30.8 us -> 112 us
  local copies, waits for them, and re-layouts: 10.9 us -> 30.5 us
  Pallas kernels: 0 us -> 15.4 us
  matrix products: 16.3 us -> 3.24 us
  other arithmetic: 16.7 us -> 9.47 us
    ppermute x0 -> x19, starting transfers between devices: none -> 67.9 us  [the longest x12 34 us: shift(): return lax.ppermute(value, 'x', [(i, (i + k) % XS) for i in range(XS)])]
    all_to_all x2 -> x4, waiting for transfers between devices: 70.5 us -> 15.3 us  [the longest x2 12.2 us: shards(): got = lax.all_to_all(outgoing[ch].reshape(block), EXPERT, 0, 0, tiled=True)]
    all_gather x1, waiting for transfers between devices: 49.4 us -> 0.02 us  [shards(): factors = lax.all_gather(factors, 'x', axis=0, tiled=False)]
    reduce_scatter x1 -> x0, waiting for transfers between devices: 35.1 us -> none  [shards(): lax.psum_scatter(lax.optimization_barrier(value.astype(jnp.bfloat16)).ast...]
    ppermute x0 -> x19, waiting for transfers between devices: none -> 21 us  [the longest x12 19.2 us: shift(): return lax.ppermute(value, 'x', [(i, (i + k) % XS) for i in range(XS)])]
    pallas_call x0 -> x6, Pallas kernels: none -> 15.4 us  [the longest x2 7.84 us: shards(): vmem_call(hidden_body, (jax.ShapeDtypeStruct((size, hid), F32),) + tuple(...]
    all_to_all x2 -> x4, starting transfers between devices: 30.5 us -> 43.8 us  [the longest x2 25.2 us: shards(): sent.append(lax.all_to_all(value.reshape(block), EXPERT, 0, 0, tiled=True))]
    dot_general x6 -> x4, matrix products: 16.3 us -> 3.24 us  [the longest x2 2.59 us: shards(): lax.dot_general(act, incoming[ch], TN, preferred_element_type=F32)]
  transfers between devices with their start and end apart: 4 -> 24, of which waited for: 4 -> 11; matrix products, arithmetic and copies ran while one was open for 5% -> 13% of each run, Pallas kernels for 0% -> 7%
where the time goes in v1:
time: 223 us; the launch traced here: 221 us
  starting transfers between devices  112 us (50%)
  waiting for transfers between devices  36.4 us (16%)
  local copies, waits for them, and re-layouts  30.5 us (14%)
  Pallas kernels  15.4 us (7%)
  between operations  14.7 us (7%)
  other arithmetic  9.47 us (4%)
  matrix products  3.24 us (1%)
    ppermute x12, starting transfers between devices, shift(): return lax.ppermute(value, 'x', [(i, (i + k) % XS) for i in range(XS)])  34 us
    ppermute x7, starting transfers between devices, swap(): return lax.ppermute(value, 'core', [(0, 1), (1, 0)])  33.8 us
    all_to_all x2, starting transfers between devices, shards(): sent.append(lax.all_to_all(value.reshape(block), EXPERT, 0, 0, tiled=True))  25.2 us
    ppermute x12, waiting for transfers between devices, shift(): return lax.ppermute(value, 'x', [(i, (i + k) % XS) for i in range(XS)])  19.2 us
    all_to_all x2, starting transfers between devices, shards(): got = lax.all_to_all(outgoing[ch].reshape(block), EXPERT, 0, 0, tiled=True)  18.6 us
    all_to_all x2, waiting for transfers between devices, shards(): got = lax.all_to_all(outgoing[ch].reshape(block), EXPERT, 0, 0, tiled=True)  12.2 us
    pallas_call x2, Pallas kernels, shards(): vmem_call(hidden_body, (jax.ShapeDtypeStruct((size, hid), F32),) + tuple(...  7.84 us
    pallas_call x2, Pallas kernels, shards(): vmem_call(back_body, jax.ShapeDtypeStruct((rows, width), BF16), 1, 9, 4 *...  6.55 us
  transfers between devices with their start and end apart: 24, of which 11 were waited for; matrix products, arithmetic and copies ran while one was open for 13% of the time, Pallas kernels for 7%

profile of v1, /device:TPU:1, one launch (start us, length us, event | category | flops | bytes accessed | tf_op | source)
XLA Modules:
  0.0 221.3 jit_solution(1365490787930262171)
XLA Ops:
  7.2 2.4 %fusion.16 = (bf16[160,1,1024]{2,1,0:T(2,128)(2,1)S(1)}, bf16[160,1,1024]{2,1,0:T(2,128)(2,1)S(1)}) fusion(bf16[160,2,1024]{2,1,0:T(2,128)(2,1)} %bitcast.101), kind=kLoop, calls=%fused_computation.42 | loop fusion | bytes 1310720 | tf_op jit(solution)/shard_map/slice | solution.py:168
  9.7 0.7 convert.10
  10.3 0.7 convert.11
  11.0 0.9 multiply_convert_fusion.1
  12.0 1.0 copy.53
  13.0 0.7 constant_dynamic-slice_fusion.1
  13.9 8.8 %collective-permute-start.8 = (bf16[3,2,40,1024]{3,2,1,0:T(8,128)(2,1)S(1)}, bf16[3,2,40,1024]{3,2,1,0:T(8,128)(2,1)S(1)}, u32[]{:S(2)}, u32[]{:S(2)}) collective-permute-start(bf16[3,2,40,1024]{3,2,1,0:T(8,128)(2,1)S(1)} %bitcast.103), channel_id=1, source_target_pairs={{0,64},{64,0},{1,65},{65,1},{2,66},{66,2},{3,67},{67,3},{4,68},{68... | collective-permute-start | bytes 1474568 | tf_op jit(solution)/shard_map/ppermute | solution.py:125
  22.7 1.5 collective-permute-done.8
  24.3 1.0 pad_maximum_fusion
  25.7 2.3 %collective-permute-start = (bf16[128,512]{1,0:T(8,128)(2,1)S(1)}, bf16[128,512]{1,0:T(8,128)(2,1)S(1)}, u32[]{:S(2)}, u32[]{:S(2)}) collective-permute-start(bf16[128,512]{1,0:T(8,128)(2,1)S(1)} %fusion.6.mine_ref), channel_id=1, source_target_pairs={{0,64},{64,0},{1,65},{65,1},{2,66},{66,2},{3,67},{67,3},{4,68},{68... | collective-permute-start | bytes 393224 | tf_op jit(solution)/shard_map/ppermute | solution.py:125
  29.4 1.2 reshape.161
  30.6 11.2 %all-to-all-start.2 = ((bf16[64,40,128]{2,1,0:T(8,128)(2,1)}), bf16[64,40,128]{2,1,0:T(8,128)(2,1)}, u32[]{:S(2)}, u32[]{:S(2)}) async-start(bf16[64,40,128]{2,1,0:T(8,128)(2,1)} %reshape.161), calls=%async_computation.2 | async-start | bytes 1310720 | tf_op jit(solution)/shard_map/all_to_all | solution.py:164
  42.7 2.7 %collective-permute-start.1 = (bf16[1024,512]{1,0:T(8,128)(2,1)S(1)}, bf16[1024,512]{1,0:T(8,128)(2,1)}, u32[]{:S(2)}, u32[]{:S(2)}) collective-permute-start(bf16[1024,512]{1,0:T(8,128)(2,1)S(1)} %fusion.2.mine_ref), channel_id=1, source_target_pairs={{0,64},{64,0},{1,65},{65,1},{2,66},{66,2},{3,67},{67,3},{4,68},{68... | collective-permute-start | bytes 3145736 | tf_op jit(solution)/shard_map/ppermute | solution.py:125
  45.6 0.7 fusion.um_ref
  46.3 1.9 collective-permute-start.10
  48.3 1.1 reshape.156
  49.4 12.2 %all-to-all-done.2 = bf16[64,40,128]{2,1,0:T(8,128)(2,1)} async-done(((bf16[64,40,128]{2,1,0:T(8,128)(2,1)}), bf16[64,40,128]{2,1,0:T(8,128)(2,1)}, u32[]{:S(2)}, u32[]{:S(2)}) %all-to-all-start.2) | async-done | bytes 655392 | tf_op jit(solution)/shard_map/all_to_all | solution.py:164
  61.5 7.5 %all-to-all-start = ((bf16[64,40,128]{2,1,0:T(8,128)(2,1)}), bf16[64,40,128]{2,1,0:T(8,128)(2,1)}, u32[]{:S(2)}, u32[]{:S(2)}) async-start(bf16[64,40,128]{2,1,0:T(8,128)(2,1)} %reshape.156), calls=%async_computation | async-start | bytes 1310720 | tf_op jit(solution)/shard_map/all_to_all | solution.py:164
  69.2 1.0 copy-done.12
  70.2 0.7 fusion.1.gm_ref
  71.0 3.5 %collective-permute-start.9 = (bf16[512,1024]{1,0:T(8,128)(2,1)S(1)}, bf16[512,1024]{1,0:T(8,128)(2,1)}, u32[]{:S(2)}, u32[]{:S(2)}) collective-permute-start(bf16[512,1024]{1,0:T(8,128)(2,1)S(1)} %fusion.1.gm_ref), channel_id=1, source_target_pairs={{0,64},{64,0},{1,65},{65,1},{2,66},{66,2},{3,67},{67,3},{4,68},{68... | collective-permute-start | bytes 3145736 | tf_op jit(solution)/shard_map/ppermute | solution.py:125
  74.5 2.1 reshape.162.rows_ref
  76.6 1.1 copy-done.1
  77.7 3.8 %shard_map.108 = (f32[80,1024]{1,0:T(8,128)S(1)}, bf16[80,1024]{1,0:T(8,128)(2,1)S(1)}, bf16[80,1024]{1,0:T(8,128)(2,1)S(1)}, bf16[80,1024]{1,0:T(8,128)(2,1)S(1)}) custom-call(s32[1]{0:T(128)} %bitcast.6.x_ref, bf16[320,1024]{1,0:T(8,128)(2,1)S(1)} %copy-done.1, bf16[1024,512]{1,0:T(8,128)(2,1)S(1)} %fusion.2.mine_ref, ...), custom_call_target="tpu_custom_call" | custom-call | flops 671088640 | bytes 6291456 | tf_op jit(solution)/shard_map/pallas_call | solution.py:199
  81.6 3.1 %collective-permute-start.11 = (bf16[80,1024]{1,0:T(8,128)(2,1)S(1)}, bf16[80,1024]{1,0:T(8,128)(2,1)S(1)}, u32[]{:S(2)}, u32[]{:S(2)}) collective-permute-start(bf16[80,1024]{1,0:T(8,128)(2,1)S(1)} %get-tuple-element.23), channel_id=1, source_target_pairs={{0,128},{128,256},{256,384},{384,0},{1,129},{129,257},{257,385},{3... | collective-permute-start | bytes 491528 | tf_op jit(solution)/shard_map/ppermute | solution.py:129
  84.7 3.4 %collective-permute-start.12 = (bf16[80,1024]{1,0:T(8,128)(2,1)S(1)}, bf16[80,1024]{1,0:T(8,128)(2,1)S(1)}, u32[]{:S(2)}, u32[]{:S(2)}) collective-permute-start(bf16[80,1024]{1,0:T(8,128)(2,1)S(1)} %get-tuple-element.24), channel_id=1, source_target_pairs={{0,384},{128,0},{256,128},{384,256},{1,385},{129,1},{257,129},{385... | collective-permute-start | bytes 491528 | tf_op jit(solution)/shard_map/ppermute | solution.py:129
  88.1 3.4 %collective-permute-start.13 = (bf16[80,1024]{1,0:T(8,128)(2,1)S(1)}, bf16[80,1024]{1,0:T(8,128)(2,1)S(1)}, u32[]{:S(2)}, u32[]{:S(2)}) collective-permute-start(bf16[80,1024]{1,0:T(8,128)(2,1)S(1)} %get-tuple-element.25), channel_id=1, source_target_pairs={{0,256},{128,384},{256,0},{384,128},{1,257},{129,385},{257,1},{385... | collective-permute-start | bytes 491528 | tf_op jit(solution)/shard_map/ppermute | solution.py:129
  92.1 4.6 %collective-permute-done.13 = bf16[80,1024]{1,0:T(8,128)(2,1)S(1)} collective-permute-done((bf16[80,1024]{1,0:T(8,128)(2,1)S(1)}, bf16[80,1024]{1,0:T(8,128)(2,1)S(1)}, u32[]{:S(2)}, u32[]{:S(2)}) %collective-permute-start.13) | collective-permute-done | bytes 163872 | tf_op jit(solution)/shard_map/ppermute | solution.py:129
  96.7 3.2 %collective-permute-start.16 = (bf16[80,1024]{1,0:T(8,128)(2,1)S(1)}, bf16[80,1024]{1,0:T(8,128)(2,1)}, u32[]{:S(2)}, u32[]{:S(2)}) collective-permute-start(bf16[80,1024]{1,0:T(8,128)(2,1)S(1)} %add_convert_fusion.h0), channel_id=1, source_target_pairs={{0,384},{128,0},{256,128},{384,256},{1,385},{129,1},{257,129},{385... | collective-permute-start | bytes 491528 | tf_op jit(solution)/shard_map/ppermute | solution.py:129
  99.9 3.4 %collective-permute-start.15 = (bf16[80,1024]{1,0:T(8,128)(2,1)S(1)}, bf16[80,1024]{1,0:T(8,128)(2,1)}, u32[]{:S(2)}, u32[]{:S(2)}) collective-permute-start(bf16[80,1024]{1,0:T(8,128)(2,1)S(1)} %add_convert_fusion.h0), channel_id=1, source_target_pairs={{0,256},{128,384},{256,0},{384,128},{1,257},{129,385},{257,1},{385... | collective-permute-start | bytes 491528 | tf_op jit(solution)/shard_map/ppermute | solution.py:129
  103.3 1.9 collective-permute-start.14
  105.3 2.5 %copy.56 = bf16[12,2,80,1024]{3,2,0,1:T(8,128)(2,1)S(1)} copy(bf16[12,2,80,1024]{3,2,1,0:T(8,128)(2,1)} %all-gather.3.cloned.1.call-done) | data formatting | bytes 7864320 | tf_op jit(solution)/shard_map/all_gather | solution.py:187
  107.8 2.0 slice_bitcast_fusion.1
  110.3 2.5 %collective-permute-done.14.h1 = bf16[80,1024]{1,0:T(8,128)(2,1)} collective-permute-done((bf16[80,1024]{1,0:T(8,128)(2,1)S(1)}, bf16[80,1024]{1,0:T(8,128)(2,1)}, u32[]{:S(2)}, u32[]{:S(2)}) %collective-permute-start.14) | collective-permute-done | bytes 163872 | tf_op jit(solution)/shard_map/ppermute | solution.py:129
  112.8 3.4 %shard_map.109 = bf16[320,1024]{1,0:T(8,128)(2,1)S(1)} custom-call(s32[1]{0:T(128)} %bitcast.6.x_ref, bf16[80,1024]{1,0:T(8,128)(2,1)S(1)} %add_convert_fusion.h0, bf16[80,1024]{1,0:T(8,128)(2,1)} %collective-permute-done.14.h1, bf16[80,1024]{1,0:T(8,128)(2,1)} %collective-permute-done.15.h2, bf16[80,1024]{1,0:T(8,128)(2,1)} %collective-permute-done.16.h3, ...), custom_call_target="tpu_custom_call" | custom-call | flops 1342177280 | bytes 8388608 | tf_op jit(solution)/shard_map/pallas_call | solution.py:210
  116.2 0.8 copy-done.5
  117.0 2.1 reshape.163
  119.1 12.4 %all-to-all-start.3 = ((bf16[64,40,128]{2,1,0:T(8,128)(2,1)}), bf16[64,40,128]{2,1,0:T(8,128)(2,1)}, u32[]{:S(2)}, u32[]{:S(2)}) async-start(bf16[64,40,128]{2,1,0:T(8,128)(2,1)} %reshape.163), calls=%async_computation.3 | async-start | bytes 1310720 | tf_op jit(solution)/shard_map/all_to_all | solution.py:216
  131.6 2.1 reshape.157.rows_ref
  133.7 1.1 copy-done.3
  134.7 4.0 %shard_map.106 = (f32[80,1024]{1,0:T(8,128)S(1)}, bf16[80,1024]{1,0:T(8,128)(2,1)S(1)}, bf16[80,1024]{1,0:T(8,128)(2,1)S(1)}, bf16[80,1024]{1,0:T(8,128)(2,1)S(1)}) custom-call(s32[1]{0:T(128)} %bitcast.6.x_ref, bf16[320,1024]{1,0:T(8,128)(2,1)S(1)} %copy-done.3, bf16[1024,512]{1,0:T(8,128)(2,1)S(1)} %fusion.2.mine_ref, ...), custom_call_target="tpu_custom_call" | custom-call | flops 671088640 | bytes 6291456 | tf_op jit(solution)/shard_map/pallas_call | solution.py:199
  138.7 1.9 collective-permute-start.2
  140.7 4.6 %collective-permute-start.3 = (bf16[80,1024]{1,0:T(8,128)(2,1)S(1)}, bf16[80,1024]{1,0:T(8,128)(2,1)S(1)}, u32[]{:S(2)}, u32[]{:S(2)}) collective-permute-start(bf16[80,1024]{1,0:T(8,128)(2,1)S(1)} %get-tuple-element.19), channel_id=1, source_target_pairs={{0,384},{128,0},{256,128},{384,256},{1,385},{129,1},{257,129},{385... | collective-permute-start | bytes 491528 | tf_op jit(solution)/shard_map/ppermute | solution.py:129
  145.2 1.9 collective-permute-start.4
  147.5 5.7 %collective-permute-done.4 = bf16[80,1024]{1,0:T(8,128)(2,1)S(1)} collective-permute-done((bf16[80,1024]{1,0:T(8,128)(2,1)S(1)}, bf16[80,1024]{1,0:T(8,128)(2,1)S(1)}, u32[]{:S(2)}, u32[]{:S(2)}) %collective-permute-start.4) | collective-permute-done | bytes 163872 | tf_op jit(solution)/shard_map/ppermute | solution.py:129
  153.3 2.2 collective-permute-start.7
  155.5 3.0 %collective-permute-start.6 = (bf16[80,1024]{1,0:T(8,128)(2,1)S(1)}, bf16[80,1024]{1,0:T(8,128)(2,1)S(1)}, u32[]{:S(2)}, u32[]{:S(2)}) collective-permute-start(bf16[80,1024]{1,0:T(8,128)(2,1)S(1)} %add_convert_fusion.1.h0), channel_id=1, source_target_pairs={{0,256},{128,384},{256,0},{384,128},{1,257},{129,385},{257,1},{385... | collective-permute-start | bytes 491528 | tf_op jit(solution)/shard_map/ppermute | solution.py:129
  158.5 2.0 collective-permute-start.5
  160.5 2.5 %collective-permute-done.6.h2 = bf16[80,1024]{1,0:T(8,128)(2,1)S(1)} collective-permute-done((bf16[80,1024]{1,0:T(8,128)(2,1)S(1)}, bf16[80,1024]{1,0:T(8,128)(2,1)S(1)}, u32[]{:S(2)}, u32[]{:S(2)}) %collective-permute-start.6) | collective-permute-done | bytes 163872 | tf_op jit(solution)/shard_map/ppermute | solution.py:129
  163.1 3.0 %collective-permute-done.5.h1 = bf16[80,1024]{1,0:T(8,128)(2,1)S(1)} collective-permute-done((bf16[80,1024]{1,0:T(8,128)(2,1)S(1)}, bf16[80,1024]{1,0:T(8,128)(2,1)S(1)}, u32[]{:S(2)}, u32[]{:S(2)}) %collective-permute-start.5) | collective-permute-done | bytes 163872 | tf_op jit(solution)/shard_map/ppermute | solution.py:129
  166.1 3.2 %shard_map.107 = bf16[320,1024]{1,0:T(8,128)(2,1)S(1)} custom-call(s32[1]{0:T(128)} %bitcast.6.x_ref, bf16[80,1024]{1,0:T(8,128)(2,1)S(1)} %add_convert_fusion.1.h0, bf16[80,1024]{1,0:T(8,128)(2,1)S(1)} %collective-permute-done.5.h1, bf16[80,1024]{1,0:T(8,128)(2,1)S(1)} %collective-permute-done.6.h2, bf16[80,1024]{1,0:T(8,128)(2,1)S(1)} %collective-permute-done.7.h3, ...), custom_call_target="tpu_custom_call" | custom-call | flops 1342177280 | bytes 8388608 | tf_op jit(solution)/shard_map/pallas_call | solution.py:210
  169.3 1.1 reshape.159
  170.4 1.5 fusion.15
  171.9 12.7 %all-to-all-start.1 = ((bf16[64,40,128]{2,1,0:T(8,128)(2,1)}), bf16[64,40,128]{2,1,0:T(8,128)(2,1)S(1)}, u32[]{:S(2)}, u32[]{:S(2)}) async-start(bf16[64,40,128]{2,1,0:T(8,128)(2,1)} %reshape.159), calls=%async_computation.1 | async-start | bytes 1310720 | tf_op jit(solution)/shard_map/all_to_all | solution.py:216
  184.7 1.3 fusion.17
  186.0 1.3 convolution_add_fusion
  187.3 2.0 copy-done.9
  189.3 1.1 slice.98
  190.4 6.2 %collective-permute-start.18 = (bf16[1024,512]{1,0:T(8,128)(2,1)}, bf16[1024,512]{1,0:T(8,128)(2,1)}, u32[]{:S(2)}, u32[]{:S(2)}) collective-permute-start(bf16[1024,512]{1,0:T(8,128)(2,1)} %slice.98), channel_id=1, source_target_pairs={{0,64},{64,0},{1,65},{65,1},{2,66},{66,2},{3,67},{67,3},{4,68},{68... | collective-permute-start | bytes 3145736 | tf_op jit(solution)/shard_map/ppermute | solution.py:125
  196.6 1.4 reshape.164
  198.0 3.1 %all-to-all-done.1 = bf16[64,40,128]{2,1,0:T(8,128)(2,1)S(1)} async-done(((bf16[64,40,128]{2,1,0:T(8,128)(2,1)}), bf16[64,40,128]{2,1,0:T(8,128)(2,1)S(1)}, u32[]{:S(2)}, u32[]{:S(2)}) %all-to-all-start.1) | async-done | bytes 655392 | tf_op jit(solution)/shard_map/all_to_all | solution.py:216
  202.1 8.4 %collective-permute-start.17 = (f32[128,512]{1,0:T(8,128)S(1)}, f32[128,512]{1,0:T(8,128)S(1)}, u32[]{:S(2)}, u32[]{:S(2)}) collective-permute-start(f32[128,512]{1,0:T(8,128)S(1)} %slice.69), channel_id=1, source_target_pairs={{0,64},{64,0},{1,65},{65,1},{2,66},{66,2},{3,67},{67,3},{4,68},{68... | collective-permute-start | bytes 786440 | tf_op jit(solution)/shard_map/ppermute | solution.py:125
  210.5 3.2 %fusion.4 = bf16[1,1024,512]{2,1,0:T(8,128)(2,1)} fusion(bf16[1024,512]{1,0:T(8,128)(2,1)} %collective-permute-done.18, f32[1024,1024]{1,0:T(8,128)} %copy-done.9), kind=kLoop, calls=%fused_computation.13 | loop fusion | flops 1572864 | bytes 4194304 | tf_op jit(solution)/shard_map/broadcast_in_dim | solution.py:232
  213.8 0.7 fusion.8
  (65 shorter events, 5.9 us)
Async XLA Ops:
  7.2 98.1 %all-gather.3.cloned.1.call-start = ((), (), s32[]{:S(2)}) async-start(), calls=%async_computation.4 | async-start | bytes 4915200 | tf_op jit(solution)/shard_map/all_gather | solution.py:187
  13.9 10.3 %collective-permute-start.8 = (bf16[3,2,40,1024]{3,2,1,0:T(8,128)(2,1)S(1)}, bf16[3,2,40,1024]{3,2,1,0:T(8,128)(2,1)S(1)}, u32[]{:S(2)}, u32[]{:S(2)}) collective-permute-start(bf16[3,2,40,1024]{3,2,1,0:T(8,128)(2,1)S(1)} %bitcast.103), channel_id=1, source_target_pairs={{0,64},{64,0},{1,65},{65,1},{2,66},{66,2},{3,67},{67,3},{4,68},{68... | collective-permute-start | bytes 1474568 | tf_op jit(solution)/shard_map/ppermute | solution.py:125
  24.1 1.2 copy-start.15
  24.2 1.4 copy-start.13
  24.2 3.7 %copy-start.6 = (s32[1,128,8]{1,2,0:T(8,128)S(1)}, s32[1,128,8]{1,2,0:T(8,128)}, u32[]{:S(2)}) copy-start(s32[1,128,8]{1,2,0:T(8,128)} %param.11) | copy-start | bytes 12292
  24.3 3.7 %copy-start.7 = (f32[1,128,8]{1,2,0:T(8,128)S(1)}, f32[1,128,8]{1,2,0:T(8,128)}, u32[]{:S(2)}) copy-start(f32[1,128,8]{1,2,0:T(8,128)} %param.12) | copy-start | bytes 12292
  25.4 16.3 %copy-start.14 = (f32[3,1,4,8]{3,2,1,0:T(4,128)S(1)}, f32[3,1,4,8]{3,2,1,0:T(4,128)}, u32[]{:S(2)}) copy-start(f32[3,1,4,8]{3,2,1,0:T(4,128)} %param.17) | copy-start | bytes 1156
  25.7 3.3 %collective-permute-start = (bf16[128,512]{1,0:T(8,128)(2,1)S(1)}, bf16[128,512]{1,0:T(8,128)(2,1)S(1)}, u32[]{:S(2)}, u32[]{:S(2)}) collective-permute-start(bf16[128,512]{1,0:T(8,128)(2,1)S(1)} %fusion.6.mine_ref), channel_id=1, source_target_pairs={{0,64},{64,0},{1,65},{65,1},{2,66},{66,2},{3,67},{67,3},{4,68},{68... | collective-permute-start | bytes 393224 | tf_op jit(solution)/shard_map/ppermute | solution.py:125
  29.4 12.8 %copy-start.10 = (bf16[1,1024,512]{2,1,0:T(8,128)(2,1)S(1)}, bf16[1,1024,512]{2,1,0:T(8,128)(2,1)}, u32[]{:S(2)}) copy-start(bf16[1,1024,512]{2,1,0:T(8,128)(2,1)} %param.16) | copy-start | bytes 3145732
  30.6 30.9 %all-to-all-start.2 = ((bf16[64,40,128]{2,1,0:T(8,128)(2,1)}), bf16[64,40,128]{2,1,0:T(8,128)(2,1)}, u32[]{:S(2)}, u32[]{:S(2)}) async-start(bf16[64,40,128]{2,1,0:T(8,128)(2,1)} %reshape.161), calls=%async_computation.2 | async-start | bytes 1310720 | tf_op jit(solution)/shard_map/all_to_all | solution.py:164
  42.7 2.9 %copy-start.11 = (bf16[1,512,1024]{2,1,0:T(8,128)(2,1)S(1)}, bf16[1,512,1024]{2,1,0:T(8,128)(2,1)}, u32[]{:S(2)}) copy-start(bf16[1,512,1024]{2,1,0:T(8,128)(2,1)} %param.15) | copy-start | bytes 3145732
  42.7 34.0 %collective-permute-start.1 = (bf16[1024,512]{1,0:T(8,128)(2,1)S(1)}, bf16[1024,512]{1,0:T(8,128)(2,1)}, u32[]{:S(2)}, u32[]{:S(2)}) collective-permute-start(bf16[1024,512]{1,0:T(8,128)(2,1)S(1)} %fusion.2.mine_ref), channel_id=1, source_target_pairs={{0,64},{64,0},{1,65},{65,1},{2,66},{66,2},{3,67},{67,3},{4,68},{68... | collective-permute-start | bytes 3145736 | tf_op jit(solution)/shard_map/ppermute | solution.py:125
  46.3 64.0 %collective-permute-start.10 = (bf16[512,1024]{1,0:T(8,128)(2,1)S(1)}, bf16[512,1024]{1,0:T(8,128)(2,1)}, u32[]{:S(2)}, u32[]{:S(2)}) collective-permute-start(bf16[512,1024]{1,0:T(8,128)(2,1)S(1)} %fusion.um_ref), channel_id=1, source_target_pairs={{0,64},{64,0},{1,65},{65,1},{2,66},{66,2},{3,67},{67,3},{4,68},{68... | collective-permute-start | bytes 3145736 | tf_op jit(solution)/shard_map/ppermute | solution.py:125
  61.5 57.6 %all-to-all-start = ((bf16[64,40,128]{2,1,0:T(8,128)(2,1)}), bf16[64,40,128]{2,1,0:T(8,128)(2,1)}, u32[]{:S(2)}, u32[]{:S(2)}) async-start(bf16[64,40,128]{2,1,0:T(8,128)(2,1)} %reshape.156), calls=%async_computation | async-start | bytes 1310720 | tf_op jit(solution)/shard_map/all_to_all | solution.py:164
  69.0 1.2 copy-start.12
  71.0 39.3 %collective-permute-start.9 = (bf16[512,1024]{1,0:T(8,128)(2,1)S(1)}, bf16[512,1024]{1,0:T(8,128)(2,1)}, u32[]{:S(2)}, u32[]{:S(2)}) collective-permute-start(bf16[512,1024]{1,0:T(8,128)(2,1)S(1)} %fusion.1.gm_ref), channel_id=1, source_target_pairs={{0,64},{64,0},{1,65},{65,1},{2,66},{66,2},{3,67},{67,3},{4,68},{68... | collective-permute-start | bytes 3145736 | tf_op jit(solution)/shard_map/ppermute | solution.py:125
  76.6 1.1 copy-start.1
  81.6 10.0 %collective-permute-start.11 = (bf16[80,1024]{1,0:T(8,128)(2,1)S(1)}, bf16[80,1024]{1,0:T(8,128)(2,1)S(1)}, u32[]{:S(2)}, u32[]{:S(2)}) collective-permute-start(bf16[80,1024]{1,0:T(8,128)(2,1)S(1)} %get-tuple-element.23), channel_id=1, source_target_pairs={{0,128},{128,256},{256,384},{384,0},{1,129},{129,257},{257,385},{3... | collective-permute-start | bytes 491528 | tf_op jit(solution)/shard_map/ppermute | solution.py:129
  84.7 7.4 %collective-permute-start.12 = (bf16[80,1024]{1,0:T(8,128)(2,1)S(1)}, bf16[80,1024]{1,0:T(8,128)(2,1)S(1)}, u32[]{:S(2)}, u32[]{:S(2)}) collective-permute-start(bf16[80,1024]{1,0:T(8,128)(2,1)S(1)} %get-tuple-element.24), channel_id=1, source_target_pairs={{0,384},{128,0},{256,128},{384,256},{1,385},{129,1},{257,129},{385... | collective-permute-start | bytes 491528 | tf_op jit(solution)/shard_map/ppermute | solution.py:129
  88.1 8.6 %collective-permute-start.13 = (bf16[80,1024]{1,0:T(8,128)(2,1)S(1)}, bf16[80,1024]{1,0:T(8,128)(2,1)S(1)}, u32[]{:S(2)}, u32[]{:S(2)}) collective-permute-start(bf16[80,1024]{1,0:T(8,128)(2,1)S(1)} %get-tuple-element.25), channel_id=1, source_target_pairs={{0,256},{128,384},{256,0},{384,128},{1,257},{129,385},{257,1},{385... | collective-permute-start | bytes 491528 | tf_op jit(solution)/shard_map/ppermute | solution.py:129
  96.7 13.6 %collective-permute-start.16 = (bf16[80,1024]{1,0:T(8,128)(2,1)S(1)}, bf16[80,1024]{1,0:T(8,128)(2,1)}, u32[]{:S(2)}, u32[]{:S(2)}) collective-permute-start(bf16[80,1024]{1,0:T(8,128)(2,1)S(1)} %add_convert_fusion.h0), channel_id=1, source_target_pairs={{0,384},{128,0},{256,128},{384,256},{1,385},{129,1},{257,129},{385... | collective-permute-start | bytes 491528 | tf_op jit(solution)/shard_map/ppermute | solution.py:129
  99.9 10.4 %collective-permute-start.15 = (bf16[80,1024]{1,0:T(8,128)(2,1)S(1)}, bf16[80,1024]{1,0:T(8,128)(2,1)}, u32[]{:S(2)}, u32[]{:S(2)}) collective-permute-start(bf16[80,1024]{1,0:T(8,128)(2,1)S(1)} %add_convert_fusion.h0), channel_id=1, source_target_pairs={{0,256},{128,384},{256,0},{384,128},{1,257},{129,385},{257,1},{385... | collective-permute-start | bytes 491528 | tf_op jit(solution)/shard_map/ppermute | solution.py:129
  103.3 9.5 %collective-permute-start.14 = (bf16[80,1024]{1,0:T(8,128)(2,1)S(1)}, bf16[80,1024]{1,0:T(8,128)(2,1)}, u32[]{:S(2)}, u32[]{:S(2)}) collective-permute-start(bf16[80,1024]{1,0:T(8,128)(2,1)S(1)} %add_convert_fusion.h0), channel_id=1, source_target_pairs={{0,128},{128,256},{256,384},{384,0},{1,129},{129,257},{257,385},{3... | collective-permute-start | bytes 491528 | tf_op jit(solution)/shard_map/ppermute | solution.py:129
  107.8 2.5 %copy-start.8 = (bf16[12,2,80,1024]{3,2,0,1:T(8,128)(2,1)}, bf16[12,2,80,1024]{3,2,0,1:T(8,128)(2,1)S(1)}, u32[]{:S(2)}) copy-start(bf16[12,2,80,1024]{3,2,0,1:T(8,128)(2,1)S(1)} %copy.56) | copy-start | bytes 11796484
  116.2 0.8 copy-start.5
  119.1 52.8 %all-to-all-start.3 = ((bf16[64,40,128]{2,1,0:T(8,128)(2,1)}), bf16[64,40,128]{2,1,0:T(8,128)(2,1)}, u32[]{:S(2)}, u32[]{:S(2)}) async-start(bf16[64,40,128]{2,1,0:T(8,128)(2,1)} %reshape.163), calls=%async_computation.3 | async-start | bytes 1310720 | tf_op jit(solution)/shard_map/all_to_all | solution.py:216
  133.7 1.1 copy-start.3
  134.7 31.4 %copy-start = (bf16[4,3,80,1024]{3,2,1,0:T(8,128)(2,1)S(1)}, bf16[4,3,80,1024]{3,2,1,0:T(8,128)(2,1)}, u32[]{:S(2)}) copy-start(bf16[4,3,80,1024]{3,2,1,0:T(8,128)(2,1)} %get-tuple-element.28.fac_ref) | copy-start | bytes 5898244
  138.7 8.4 %collective-permute-start.2 = (bf16[80,1024]{1,0:T(8,128)(2,1)S(1)}, bf16[80,1024]{1,0:T(8,128)(2,1)S(1)}, u32[]{:S(2)}, u32[]{:S(2)}) collective-permute-start(bf16[80,1024]{1,0:T(8,128)(2,1)S(1)} %get-tuple-element.18), channel_id=1, source_target_pairs={{0,128},{128,256},{256,384},{384,0},{1,129},{129,257},{257,385},{3... | collective-permute-start | bytes 491528 | tf_op jit(solution)/shard_map/ppermute | solution.py:129
  140.7 6.8 %collective-permute-start.3 = (bf16[80,1024]{1,0:T(8,128)(2,1)S(1)}, bf16[80,1024]{1,0:T(8,128)(2,1)S(1)}, u32[]{:S(2)}, u32[]{:S(2)}) collective-permute-start(bf16[80,1024]{1,0:T(8,128)(2,1)S(1)} %get-tuple-element.19), channel_id=1, source_target_pairs={{0,384},{128,0},{256,128},{384,256},{1,385},{129,1},{257,129},{385... | collective-permute-start | bytes 491528 | tf_op jit(solution)/shard_map/ppermute | solution.py:129
  145.2 8.0 %collective-permute-start.4 = (bf16[80,1024]{1,0:T(8,128)(2,1)S(1)}, bf16[80,1024]{1,0:T(8,128)(2,1)S(1)}, u32[]{:S(2)}, u32[]{:S(2)}) collective-permute-start(bf16[80,1024]{1,0:T(8,128)(2,1)S(1)} %get-tuple-element.20), channel_id=1, source_target_pairs={{0,256},{128,384},{256,0},{384,128},{1,257},{129,385},{257,1},{385... | collective-permute-start | bytes 491528 | tf_op jit(solution)/shard_map/ppermute | solution.py:129
  153.3 7.2 %collective-permute-start.7 = (bf16[80,1024]{1,0:T(8,128)(2,1)S(1)}, bf16[80,1024]{1,0:T(8,128)(2,1)S(1)}, u32[]{:S(2)}, u32[]{:S(2)}) collective-permute-start(bf16[80,1024]{1,0:T(8,128)(2,1)S(1)} %add_convert_fusion.1.h0), channel_id=1, source_target_pairs={{0,384},{128,0},{256,128},{384,256},{1,385},{129,1},{257,129},{385... | collective-permute-start | bytes 491528 | tf_op jit(solution)/shard_map/ppermute | solution.py:129
  155.5 7.6 %collective-permute-start.6 = (bf16[80,1024]{1,0:T(8,128)(2,1)S(1)}, bf16[80,1024]{1,0:T(8,128)(2,1)S(1)}, u32[]{:S(2)}, u32[]{:S(2)}) collective-permute-start(bf16[80,1024]{1,0:T(8,128)(2,1)S(1)} %add_convert_fusion.1.h0), channel_id=1, source_target_pairs={{0,256},{128,384},{256,0},{384,128},{1,257},{129,385},{257,1},{385... | collective-permute-start | bytes 491528 | tf_op jit(solution)/shard_map/ppermute | solution.py:129
  158.5 7.6 %collective-permute-start.5 = (bf16[80,1024]{1,0:T(8,128)(2,1)S(1)}, bf16[80,1024]{1,0:T(8,128)(2,1)S(1)}, u32[]{:S(2)}, u32[]{:S(2)}) collective-permute-start(bf16[80,1024]{1,0:T(8,128)(2,1)S(1)} %add_convert_fusion.1.h0), channel_id=1, source_target_pairs={{0,128},{128,256},{256,384},{384,0},{1,129},{129,257},{257,385},{3... | collective-permute-start | bytes 491528 | tf_op jit(solution)/shard_map/ppermute | solution.py:129
  170.4 14.3 %copy-start.4 = (bf16[320,1024]{1,0:T(8,128)(2,1)S(1)}, bf16[320,1024]{1,0:T(8,128)(2,1)}, u32[]{:S(2)}) copy-start(bf16[320,1024]{1,0:T(8,128)(2,1)} %reshape.157.rows_ref) | copy-start | bytes 1966084
  171.9 29.2 %all-to-all-start.1 = ((bf16[64,40,128]{2,1,0:T(8,128)(2,1)}), bf16[64,40,128]{2,1,0:T(8,128)(2,1)S(1)}, u32[]{:S(2)}, u32[]{:S(2)}) async-start(bf16[64,40,128]{2,1,0:T(8,128)(2,1)} %reshape.159), calls=%async_computation.1 | async-start | bytes 1310720 | tf_op jit(solution)/shard_map/all_to_all | solution.py:216
  184.7 1.3 copy-start.2
  187.3 2.0 copy-start.9
  190.4 20.1 %collective-permute-start.18 = (bf16[1024,512]{1,0:T(8,128)(2,1)}, bf16[1024,512]{1,0:T(8,128)(2,1)}, u32[]{:S(2)}, u32[]{:S(2)}) collective-permute-start(bf16[1024,512]{1,0:T(8,128)(2,1)} %slice.98), channel_id=1, source_target_pairs={{0,64},{64,0},{1,65},{65,1},{2,66},{66,2},{3,67},{67,3},{4,68},{68... | collective-permute-start | bytes 3145736 | tf_op jit(solution)/shard_map/ppermute | solution.py:125
  202.1 11.7 %collective-permute-start.17 = (f32[128,512]{1,0:T(8,128)S(1)}, f32[128,512]{1,0:T(8,128)S(1)}, u32[]{:S(2)}, u32[]{:S(2)}) collective-permute-start(f32[128,512]{1,0:T(8,128)S(1)} %slice.69), channel_id=1, source_target_pairs={{0,64},{64,0},{1,65},{65,1},{2,66},{66,2},{3,67},{67,3},{4,68},{68... | collective-permute-start | bytes 786440 | tf_op jit(solution)/shard_map/ppermute | solution.py:125
Sparse Core Ops, SparseCore 0:
  25.4 50.3 all-gather.2

commit v2 on v1

v2 whole, which is shorter than its diff:
```python
import functools

import jax
import jax.numpy as jnp
from jax import lax
from jax.experimental import pallas as pl
from jax.experimental.pallas import tpu as pltpu
from jax.sharding import Mesh
from jax.sharding import PartitionSpec as P

EXPERT = ("z", "y")
SEQ = ("x", "core")
XS = 4
CHUNKS = 1
LANES = 128
HIGHEST = lax.Precision.HIGHEST
NT = (((1,), (1,)), ((), ()))
TN = (((0,), (0,)), ((), ()))
F32 = jnp.float32
BF16 = jnp.bfloat16


def vmem_call(body, out_shape, n_smem, n_in, flops, nbytes, scratch=(), limit=40 << 20):
    smem = pl.BlockSpec(memory_space=pltpu.SMEM)
    vmem = pl.BlockSpec(memory_space=pltpu.VMEM)
    outs = jax.tree.map(lambda _: vmem, out_shape)
    return pl.pallas_call(
        body,
        out_shape=out_shape,
        in_specs=[smem] * n_smem + [vmem] * n_in,
        out_specs=outs,
        scratch_shapes=list(scratch),
        compiler_params=pltpu.CompilerParams(vmem_limit_bytes=limit),
        cost_estimate=pl.CostEstimate(flops=flops, bytes_accessed=nbytes, transcendentals=0),
    )


def shape(dims, dtype=BF16):
    return jax.ShapeDtypeStruct(dims, dtype)


def dequant_matrix(values, scales):
    rows_in, cols_in = values.shape
    row_blocks, col_blocks = scales.shape
    grid = values.astype(F32).reshape(
        row_blocks, rows_in // row_blocks, col_blocks, cols_in // col_blocks
    )
    return (grid * scales[:, None, :, None]).reshape(rows_in, cols_in).astype(BF16)


def iota(dims, axis):
    return lax.broadcasted_iota(jnp.int32, dims, axis)


def onehot(condition, dtype=BF16):
    return jnp.where(condition, 1.0, 0.0).astype(dtype)


def dy_body(value_ref, scale_ref, out_ref):
    blocks, cols = scale_ref.shape[0], value_ref.shape[1]
    first = iota((blocks, cols), 0) * (cols // blocks)
    lane = iota((blocks, cols), 1)
    spread = onehot((lane >= first) & (lane < first + cols // blocks), F32)
    scale = lax.dot_general(
        scale_ref[...], spread, TN, precision=HIGHEST, preferred_element_type=F32
    )
    out_ref[...] = (value_ref[...].astype(F32) * scale).astype(BF16)


def select_body(experts, slots, core_ref, route_ref, weight_ref, pick_ref, gate_ref):
    top, tokens = route_ref.shape
    rows = experts * slots
    label = iota((experts, tokens), 0)
    named = jnp.zeros((experts, tokens), F32)
    weight = jnp.zeros((experts, tokens), F32)
    for k in range(top):
        hit = route_ref[k : k + 1, :] == label
        named = named + jnp.where(hit, 1.0, 0.0)
        weight = weight + jnp.where(hit, weight_ref[k : k + 1, :], 0.0)
    before = onehot(iota((tokens, tokens), 0) < iota((tokens, tokens), 1))
    earlier = jnp.dot(named.astype(BF16), before, preferred_element_type=F32)
    slot = jnp.where(named > 0.0, earlier, -1.0)
    row = iota((rows, experts), 0)
    first = iota((rows, experts), 1) * slots
    spread = (row >= first) & (row < first + slots)
    slot_row = jnp.dot(onehot(spread), slot.astype(BF16), preferred_element_type=F32)
    weight_row = jnp.dot(
        onehot(spread, F32), weight, precision=HIGHEST, preferred_element_type=F32
    )
    place = iota((rows, tokens), 0).astype(F32)
    place = place - slots * jnp.floor((place + 0.5) * (1.0 / slots))
    base = (core_ref[0] * (slots * CHUNKS)).astype(F32)
    for ch in range(CHUNKS):
        hit = slot_row == place + (base + float(ch * slots))
        pick_ref[ch] = onehot(hit)
        gate = jnp.sum(jnp.where(hit, weight_row, 0.0), axis=1, keepdims=True)
        gate_ref[ch] = jnp.broadcast_to(gate, (rows, tokens))


def tile_rows(value, tile_s, at):
    rows = value.shape[0]
    per = tile_s.shape[0] // rows
    for j in range(value.shape[1] // LANES):
        tile_s[pl.ds(at + j, rows, stride=per), :] = value[:, j * LANES : (j + 1) * LANES]


def untile_rows(tile_ref, tile_s, rows_ref):
    rows, per = tile_ref.shape[:2]
    tile_s[...] = tile_ref[...].astype(F32).reshape(rows * per, LANES)
    for j in range(per):
        rows_ref[:, j * LANES : (j + 1) * LANES] = tile_s[pl.ds(j, rows, stride=per), :].astype(
            BF16
        )


def dispatch_body(pick_ref, gate_ref, mine_ref, other_ref, *refs):
    out_refs, tile_s = refs[:-1], refs[-1]
    for ch in range(CHUNKS):
        pick = pick_ref[ch]
        gate = gate_ref[ch][:, :1]
        for i, half in enumerate((mine_ref, other_ref)):
            rows = jnp.dot(pick, half[...], preferred_element_type=F32) * gate
            tile_rows(rows, tile_s, i * half.shape[1] // LANES)
        out_refs[ch][...] = tile_s[...].reshape(out_refs[ch].shape).astype(BF16)


def factor_body(slots, ch, core_ref, pre_ref, silu_ref, slope_ref, act_ref):
    rows, whole = silu_ref.shape[0], pre_ref.shape[1]
    cap = whole // (rows // slots)
    row = iota((rows, whole), 0).astype(F32)
    group = jnp.floor((row + 0.5) * (1.0 / slots))
    base = (core_ref[0] * (slots * CHUNKS) + ch * slots).astype(F32)
    pick = onehot(iota((rows, whole), 1).astype(F32) == row + group * (cap - slots) + base)
    gate_pre = jnp.dot(pick, pre_ref[0], preferred_element_type=F32)
    up_pre = jnp.dot(pick, pre_ref[1], preferred_element_type=F32)
    sig = jax.nn.sigmoid(gate_pre)
    silu = gate_pre * sig
    silu_ref[...] = silu.astype(BF16)
    slope_ref[...] = (up_pre * sig * (1.0 + gate_pre * (1.0 - sig))).astype(BF16)
    act_ref[...] = (silu * up_pre).astype(BF16)


def hidden_body(tile_ref, mine_ref, other_ref, rows_ref, low_ref, high_ref, tile_s):
    half = mine_ref.shape[1]
    size = low_ref.shape[0]
    untile_rows(tile_ref, tile_s, rows_ref)
    for i, out in enumerate((low_ref, high_ref)):
        rows = rows_ref[i * size : (i + 1) * size, :]
        part = lax.dot_general(rows[:, :half], mine_ref[...], NT, preferred_element_type=F32)
        part = part + lax.dot_general(
            rows[:, half:], other_ref[...], NT, preferred_element_type=F32
        )
        out[...] = part.astype(BF16)


def back_body(
    low, low_in, high, high_in, silu_ref, slope_ref, gm_ref, go_ref, um_ref, uo_ref,
    out_ref, gate_s, up_s, tile_s,
):
    size = low.shape[0]
    half = gm_ref.shape[0]
    for i, (here, came) in enumerate(((low, low_in), (high, high_in))):
        at = slice(i * size, (i + 1) * size)
        grad = here[...].astype(F32) + came[...].astype(F32)
        up_s[at, :] = (grad * silu_ref[at, :].astype(F32)).astype(BF16)
        gate_s[at, :] = (grad * slope_ref[at, :].astype(F32)).astype(BF16)
    for i, (g, u) in enumerate(((gm_ref, um_ref), (go_ref, uo_ref))):
        total = lax.dot_general(gate_s[...], g[...], NT, preferred_element_type=F32)
        total = total + lax.dot_general(up_s[...], u[...], NT, preferred_element_type=F32)
        tile_rows(total, tile_s, i * half // LANES)
    out_ref[...] = tile_s[...].reshape(out_ref.shape).astype(BF16)


def combine_body(pick_ref, tile_ref, out_ref, rows_s, tile_s):
    untile_rows(tile_ref, tile_s, rows_s)
    out_ref[...] = lax.dot_general(pick_ref[...], rows_s[...], TN, preferred_element_type=F32)


def swap(value):
    return lax.ppermute(value, "core", [(0, 1), (1, 0)])


def pair(value, mask):
    return lax.ppermute(value, "x", [(i, i ^ mask) for i in range(XS)])


def added(a, b):
    return (a.astype(F32) + b.astype(F32)).astype(BF16)


def shards(
    dy_values, dy_scales, route_expert, gate_weight, saved_pre, w_gate, w_up, w_down, w_scale
):
    core = lax.axis_index("core").astype(jnp.int32)[None]
    experts = lax.axis_size(EXPERT)
    tokens, cols = dy_values.shape[1:]
    rows_dev, _, hid = saved_pre.shape[1:]
    width = 2 * cols
    per = width // LANES
    cap = rows_dev * XS * 2 // experts
    slots = cap // 2 // CHUNKS
    rows = experts * slots
    tiles = (rows, per, LANES)
    block = (experts, slots * per, LANES)

    mine = vmem_call(dy_body, shape((tokens, cols)), 0, 2, 1 << 20, 1 << 18)(
        dy_values[0], dy_scales[0].T
    )
    other = swap(mine)
    pick, gate = vmem_call(
        functools.partial(select_body, experts, slots),
        (shape((CHUNKS, rows, tokens)), shape((CHUNKS, rows, tokens), F32)),
        1, 2, 4 * rows * experts * tokens, 1 << 20,
    )(core, route_expert[0].T, gate_weight[0].T)
    outgoing = vmem_call(
        dispatch_body,
        tuple(shape(tiles) for _ in range(CHUNKS)),
        0, 4, 2 * CHUNKS * rows * tokens * width, 2 << 20,
        scratch=(pltpu.VMEM((rows * per, LANES), F32),),
    )(pick, gate, mine, other)
    incoming = [
        lax.all_to_all(sent.reshape(block), EXPERT, 0, 0, tiled=True).reshape(tiles)
        for sent in outgoing
    ]

    saved_pre, w_gate, w_up, w_down, w_scale, _ = lax.optimization_barrier(
        (saved_pre, w_gate, w_up, w_down, w_scale, outgoing[0])
    )
    pre = lax.all_gather(saved_pre[0].transpose(1, 0, 2), SEQ, axis=1, tiled=True)
    scales = w_scale[:, 0]
    down_m = dequant_matrix(w_down[0], scales[2].T)
    gate_m = dequant_matrix(w_gate[0], scales[0])
    up_m = dequant_matrix(w_up[0], scales[1])
    down_o = swap(down_m)
    gate_o = swap(gate_m)
    up_o = swap(up_m)

    taken, returned, acts = [], [], []
    for ch in range(CHUNKS):
        silu, slope, act = vmem_call(
            functools.partial(factor_body, slots, ch),
            tuple(shape((rows, hid)) for _ in range(3)),
            1, 1, 4 * rows * rows_dev * XS * 2 * hid, 8 << 20,
        )(core, pre)
        acts.append(act)
        arrived, low, high = vmem_call(
            hidden_body,
            (shape((rows, width)), shape((rows // 2, hid)), shape((rows // 2, hid))),
            0, 3, 2 * rows * width * hid, 4 << 20,
            scratch=(pltpu.VMEM((rows * per, LANES), F32),),
        )(incoming[ch], down_m, down_o)
        taken.append(arrived)
        low = added(low, pair(low, 1))
        high = added(high, pair(high, 3))
        low_in = pair(low, 3)
        high_in = pair(high, 1)
        value = vmem_call(
            back_body,
            shape(tiles),
            0, 10, 4 * rows * width * hid, 6 << 20,
            scratch=(
                pltpu.VMEM((rows, hid), BF16),
                pltpu.VMEM((rows, hid), BF16),
                pltpu.VMEM((rows * per, LANES), F32),
            ),
        )(low, low_in, high, high_in, silu, slope, gate_m, gate_o, up_m, up_o)
        returned.append(
            lax.all_to_all(value.reshape(block), EXPERT, 0, 0, tiled=True).reshape(tiles)
        )

    down_total = 0.0
    for act, arrived in zip(acts, taken):
        down_total = down_total + lax.dot_general(act, arrived, TN, preferred_element_type=F32)
    down_grad = down_total[:, :cols] + swap(down_total[:, cols:].astype(BF16)).astype(F32)
    down_grad = down_grad.astype(BF16)[None]
    down_grad, *returned = lax.optimization_barrier((down_grad, *returned))

    combined = 0.0
    for ch in range(CHUNKS):
        combined = combined + vmem_call(
            combine_body,
            shape((tokens, width), F32),
            0, 2, 2 * rows * tokens * width, 2 << 20,
            scratch=(pltpu.VMEM((rows, width), BF16), pltpu.VMEM((rows * per, LANES), F32)),
        )(pick[ch], returned[ch])
    input_grad = combined[:, :cols] + swap(combined[:, cols:])
    return (input_grad.astype(BF16)[None], down_grad)


def solution(mesh):
    fine = Mesh(mesh.devices.reshape(XS, 2, 8, 8), SEQ + EXPERT)
    in_specs = (
        P(EXPERT, None, SEQ),
        P(EXPERT, None, SEQ),
        P(EXPERT, None, None),
        P(EXPERT, None, None),
        P(EXPERT, SEQ, None, None),
        P(EXPERT, SEQ, None),
        P(EXPERT, SEQ, None),
        P(EXPERT, None, SEQ),
        P(None, EXPERT, SEQ, None),
    )
    out_specs = (P(EXPERT, None, SEQ), P(EXPERT, None, SEQ))
    return jax.shard_map(shards, mesh=fine, in_specs=in_specs, out_specs=out_specs, check_vma=False)
```

time: 223 us -> 172 us (0.77)
  starting transfers between devices: 112 us -> 67.4 us
  local copies, waits for them, and re-layouts: 30.5 us -> 8.14 us
  waiting for transfers between devices: 36.4 us -> 58 us
  other arithmetic: 9.47 us -> 4.34 us
    all_to_all x4 -> x2, waiting for transfers between devices: 15.3 us -> 46.2 us  [the longest x1 28.5 us: shards(): lax.all_to_all(sent.reshape(block), EXPERT, 0, 0, tiled=True).reshape(tiles)]
    all_to_all x4 -> x2, starting transfers between devices: 43.8 us -> 22.4 us  [the longest x1 11.3 us: shards(): lax.all_to_all(value.reshape(block), EXPERT, 0, 0, tiled=True)]
    ppermute x12 -> x4, starting transfers between devices: 34 us -> 13.6 us  [pair(): return lax.ppermute(value, 'x', [(i, i ^ mask) for i in range(XS)])]
    ppermute x12 -> x4, waiting for transfers between devices: 19.2 us -> 6.01 us  [pair(): return lax.ppermute(value, 'x', [(i, i ^ mask) for i in range(XS)])]
    reshape x8 -> x0, local copies, waits for them, and re-layouts: 11.4 us -> none  [the longest x2 4.21 us: shards(): incoming.append(got.reshape(rows, width))]
    slice x2 -> x0, local copies, waits for them, and re-layouts: 3.94 us -> none  [the longest x1 2.44 us: shards(): gate_pre = pre[:, 0, :].astype(F32)]
    ppermute x7 -> x6, waiting for transfers between devices: 1.87 us -> 5.76 us  [swap(): return lax.ppermute(value, 'core', [(0, 1), (1, 0)])]
    all_gather x1 -> x0, local copies, waits for them, and re-layouts: 2.52 us -> none  [shards(): factors = lax.all_gather(factors, 'x', axis=0, tiled=False)]
  transfers between devices with their start and end apart: 24 -> 13, of which waited for: 11 -> 8; matrix products, arithmetic and copies ran while one was open for 13% -> 5% of each run, Pallas kernels for 7% -> 4%
where the time goes in v2:
time: 172 us; the launch traced here: 171 us
  starting transfers between devices  67.4 us (39%)
  waiting for transfers between devices  58 us (34%)
  Pallas kernels  15.6 us (9%)
  between operations  14.4 us (8%)
  local copies, waits for them, and re-layouts  8.14 us (5%)
  other arithmetic  4.34 us (3%)
  matrix products  3.15 us (2%)
    ppermute x6, starting transfers between devices, swap(): return lax.ppermute(value, 'core', [(0, 1), (1, 0)])  31.4 us
    all_to_all x1, waiting for transfers between devices, shards(): lax.all_to_all(sent.reshape(block), EXPERT, 0, 0, tiled=True).reshape(tiles)  28.5 us
    all_to_all x1, waiting for transfers between devices, shards(): lax.all_to_all(value.reshape(block), EXPERT, 0, 0, tiled=True)  17.6 us
    ppermute x4, starting transfers between devices, pair(): return lax.ppermute(value, 'x', [(i, i ^ mask) for i in range(XS)])  13.6 us
    all_to_all x1, starting transfers between devices, shards(): lax.all_to_all(value.reshape(block), EXPERT, 0, 0, tiled=True)  11.3 us
    all_to_all x1, starting transfers between devices, shards(): lax.all_to_all(sent.reshape(block), EXPERT, 0, 0, tiled=True).reshape(tiles)  11.1 us
    pallas_call x1, Pallas kernels, shards(): vmem_call(back_body, shape(tiles), 0, 10, 4 * rows * width * hid, 6 << 20...  6.15 us
    unnamed x30, local copies, waits for them, and re-layouts  6.14 us
  transfers between devices with their start and end apart: 13, of which 8 were waited for; matrix products, arithmetic and copies ran while one was open for 5% of the time, Pallas kernels for 4%

profile of v2, /device:TPU:1, one launch (start us, length us, event | category | flops | bytes accessed | tf_op | source)
XLA Modules:
  0.0 171.0 jit_solution(7173136600402349303)
XLA Ops:
  7.2 0.0 all-gather.2.cloned.1.call-start
  7.2 0.0 copy-start.2
  7.2 0.9 copy-done.2
  8.1 0.7 copy-done.3
  8.8 0.4 shard_map.105.mine_ref
  9.2 8.8 %collective-permute-start = (bf16[128,512]{1,0:T(8,128)(2,1)S(1)}, bf16[128,512]{1,0:T(8,128)(2,1)S(1)}, u32[]{:S(2)}, u32[]{:S(2)}) collective-permute-start(bf16[128,512]{1,0:T(8,128)(2,1)S(1)} %shard_map.105.mine_ref), channel_id=1, source_target_pairs={{0,64},{64,0},{1,65},{65,1},{2,66},{66,2},{3,67},{67,3},{4,68},{68... | collective-permute-start | bytes 393224 | tf_op jit(solution)/shard_map/ppermute | solution.py:180
  18.0 0.0 copy-start.5
  18.0 0.7 copy-done.5
  18.7 0.7 copy-done.6
  19.4 0.7 shard_map.104
  20.1 0.0 collective-permute-done.other_ref
  20.1 1.8 %shard_map.106 = bf16[640,8,128]{2,1,0:T(8,128)(2,1)} custom-call(bf16[1,640,128]{2,1,0:T(8,128)(2,1)S(1)} %get-tuple-element.17.pick_ref, f32[1,640,128]{2,1,0:T(8,128)S(1)} %get-tuple-element.18.gate_ref, bf16[128,512]{1,0:T(8,128)(2,1)S(1)} %shard_map.105.mine_ref, bf16[128,512]{1,0:T(8,128)(2,1)S(1)} %collective-permute-done.other_ref), custom_call_target="tpu_custom_call" | custom-call | flops 167772160 | bytes 2097152 | tf_op jit(solution)/shard_map/pallas_call | solution.py:215
  21.9 0.7 copy-done
  22.6 0.0 copy-done.13
  22.6 1.0 copy.20
  23.6 0.0 all-gather.2.cloned.1.call-update
  23.6 0.0 copy-start.10
  23.6 11.1 %all-to-all-start = ((bf16[64,80,128]{2,1,0:T(8,128)(2,1)}), bf16[64,80,128]{2,1,0:T(8,128)(2,1)S(1)}, u32[]{:S(2)}, u32[]{:S(2)}) async-start(bf16[64,80,128]{2,1,0:T(8,128)(2,1)} %bitcast.11), calls=%async_computation | async-start | bytes 2621440 | tf_op jit(solution)/shard_map/all_to_all | solution.py:222
  34.7 0.0 copy-done.14
  34.7 0.1 copy.12
  34.8 0.3 mul.37
  35.1 0.0 copy-done.10
  35.1 0.4 fusion.2.mine_ref
  35.6 2.2 %collective-permute-start.1 = (bf16[1024,512]{1,0:T(8,128)(2,1)S(1)}, bf16[1024,512]{1,0:T(8,128)(2,1)S(1)}, u32[]{:S(2)}, u32[]{:S(2)}) collective-permute-start(bf16[1024,512]{1,0:T(8,128)(2,1)S(1)} %fusion.2.mine_ref), channel_id=1, source_target_pairs={{0,64},{64,0},{1,65},{65,1},{2,66},{66,2},{3,67},{67,3},{4,68},{68... | collective-permute-start | bytes 3145736 | tf_op jit(solution)/shard_map/ppermute | solution.py:180
  37.8 2.3 %collective-permute-done.1.other_ref = bf16[1024,512]{1,0:T(8,128)(2,1)S(1)} collective-permute-done((bf16[1024,512]{1,0:T(8,128)(2,1)S(1)}, bf16[1024,512]{1,0:T(8,128)(2,1)S(1)}, u32[]{:S(2)}, u32[]{:S(2)}) %collective-permute-start.1) | collective-permute-done | bytes 1048608 | tf_op jit(solution)/shard_map/ppermute | solution.py:180
  40.1 28.5 %all-to-all-done = bf16[64,80,128]{2,1,0:T(8,128)(2,1)S(1)} async-done(((bf16[64,80,128]{2,1,0:T(8,128)(2,1)}), bf16[64,80,128]{2,1,0:T(8,128)(2,1)S(1)}, u32[]{:S(2)}, u32[]{:S(2)}) %all-to-all-start) | async-done | bytes 1310752 | tf_op jit(solution)/shard_map/all_to_all | solution.py:222
  68.7 1.7 shard_map.108
  70.3 0.0 copy-start.7
  70.3 0.0 copy-start.11
  70.4 3.4 %collective-permute-start.3 = (bf16[320,1024]{1,0:T(8,128)(2,1)S(1)}, bf16[320,1024]{1,0:T(8,128)(2,1)S(1)}, u32[]{:S(2)}, u32[]{:S(2)}) collective-permute-start(bf16[320,1024]{1,0:T(8,128)(2,1)S(1)} %get-tuple-element.24), channel_id=1, source_target_pairs={{0,128},{128,0},{256,384},{384,256},{1,129},{129,1},{257,385},{385... | collective-permute-start | bytes 1966088 | tf_op jit(solution)/shard_map/ppermute | solution.py:184
  73.7 3.7 %collective-permute-start.5 = (bf16[320,1024]{1,0:T(8,128)(2,1)S(1)}, bf16[320,1024]{1,0:T(8,128)(2,1)S(1)}, u32[]{:S(2)}, u32[]{:S(2)}) collective-permute-start(bf16[320,1024]{1,0:T(8,128)(2,1)S(1)} %get-tuple-element.25), channel_id=1, source_target_pairs={{0,384},{128,256},{256,128},{384,0},{1,385},{129,257},{257,129},{3... | collective-permute-start | bytes 1966088 | tf_op jit(solution)/shard_map/ppermute | solution.py:184
  77.5 0.2 mul.41
  77.7 0.7 fusion.1.gm_ref
  78.4 0.0 copy-start.12
  78.4 4.9 %collective-permute-start.7 = (bf16[512,1024]{1,0:T(8,128)(2,1)S(1)}, bf16[512,1024]{1,0:T(8,128)(2,1)}, u32[]{:S(2)}, u32[]{:S(2)}) collective-permute-start(bf16[512,1024]{1,0:T(8,128)(2,1)S(1)} %fusion.1.gm_ref), channel_id=1, source_target_pairs={{0,64},{64,0},{1,65},{65,1},{2,66},{66,2},{3,67},{67,3},{4,68},{68... | collective-permute-start | bytes 3145736 | tf_op jit(solution)/shard_map/ppermute | solution.py:180
  83.3 0.2 mul.45
  83.5 0.7 fusion.um_ref
  84.3 1.9 %collective-permute-start.8 = (bf16[512,1024]{1,0:T(8,128)(2,1)S(1)}, bf16[512,1024]{1,0:T(8,128)(2,1)}, u32[]{:S(2)}, u32[]{:S(2)}) collective-permute-start(bf16[512,1024]{1,0:T(8,128)(2,1)S(1)} %fusion.um_ref), channel_id=1, source_target_pairs={{0,64},{64,0},{1,65},{65,1},{2,66},{66,2},{3,67},{67,3},{4,68},{68... | collective-permute-start | bytes 3145736 | tf_op jit(solution)/shard_map/ppermute | solution.py:180
  86.2 0.2 collective-permute-done.3
  86.4 0.2 add_convert_fusion.1.low
  86.7 4.4 %collective-permute-start.4 = (bf16[320,1024]{1,0:T(8,128)(2,1)S(1)}, bf16[320,1024]{1,0:T(8,128)(2,1)}, u32[]{:S(2)}, u32[]{:S(2)}) collective-permute-start(bf16[320,1024]{1,0:T(8,128)(2,1)S(1)} %add_convert_fusion.1.low), channel_id=1, source_target_pairs={{0,384},{128,256},{256,128},{384,0},{1,385},{129,257},{257,129},{3... | collective-permute-start | bytes 1966088 | tf_op jit(solution)/shard_map/ppermute | solution.py:184
  91.1 0.0 collective-permute-done.5
  91.1 0.2 add_convert_fusion.high
  91.4 2.1 %collective-permute-start.6 = (bf16[320,1024]{1,0:T(8,128)(2,1)S(1)}, bf16[320,1024]{1,0:T(8,128)(2,1)}, u32[]{:S(2)}, u32[]{:S(2)}) collective-permute-start(bf16[320,1024]{1,0:T(8,128)(2,1)S(1)} %add_convert_fusion.high), channel_id=1, source_target_pairs={{0,128},{128,0},{256,384},{384,256},{1,129},{129,1},{257,385},{385... | collective-permute-start | bytes 1966088 | tf_op jit(solution)/shard_map/ppermute | solution.py:184
  93.5 0.0 all-gather.2.cloned.1.call-done.pre_ref
  93.5 0.0 copy-start.4
  93.5 2.5 %copy-done.4 = bf16[2,1280,1024]{2,1,0:T(8,128)(2,1)S(1)} copy-done((bf16[2,1280,1024]{2,1,0:T(8,128)(2,1)S(1)}, bf16[2,1280,1024]{2,1,0:T(8,128)(2,1)}, u32[]{:S(2)}) %copy-start.4) | copy-done | bytes 5242904
  96.0 3.9 %shard_map.107 = (bf16[640,1024]{1,0:T(8,128)(2,1)S(1)}, bf16[640,1024]{1,0:T(8,128)(2,1)S(1)}, bf16[640,1024]{1,0:T(8,128)(2,1)S(1)}) custom-call(s32[1]{0:T(128)} %bitcast.core_ref, bf16[2,1280,1024]{2,1,0:T(8,128)(2,1)S(1)} %copy-done.4), custom_call_target="tpu_custom_call" | custom-call | flops 3355443200 | bytes 8388608 | tf_op jit(solution)/shard_map/pallas_call | solution.py:240
  99.9 0.0 collective-permute-done.7.go_ref
  99.9 0.0 collective-permute-done.8.uo_ref
  99.9 5.2 %collective-permute-done.4.low_in = bf16[320,1024]{1,0:T(8,128)(2,1)} collective-permute-done((bf16[320,1024]{1,0:T(8,128)(2,1)S(1)}, bf16[320,1024]{1,0:T(8,128)(2,1)}, u32[]{:S(2)}, u32[]{:S(2)}) %collective-permute-start.4) | collective-permute-done | bytes 655392 | tf_op jit(solution)/shard_map/ppermute | solution.py:184
  105.1 0.6 collective-permute-done.6.high_in
  105.7 6.2 %shard_map.109 = bf16[640,8,128]{2,1,0:T(8,128)(2,1)} custom-call(bf16[320,1024]{1,0:T(8,128)(2,1)S(1)} %add_convert_fusion.1.low, bf16[320,1024]{1,0:T(8,128)(2,1)} %collective-permute-done.4.low_in, bf16[320,1024]{1,0:T(8,128)(2,1)S(1)} %add_convert_fusion.high, bf16[320,1024]{1,0:T(8,128)(2,1)} %collective-permute-done.6.high_in, ...), custom_call_target="tpu_custom_call" | custom-call | flops 2684354560 | bytes 6291456 | tf_op jit(solution)/shard_map/pallas_call | solution.py:257
  111.8 11.3 %all-to-all-start.1 = ((bf16[64,80,128]{2,1,0:T(8,128)(2,1)}), bf16[64,80,128]{2,1,0:T(8,128)(2,1)S(1)}, u32[]{:S(2)}, u32[]{:S(2)}) async-start(bf16[64,80,128]{2,1,0:T(8,128)(2,1)} %bitcast.21), calls=%async_computation.1 | async-start | bytes 2621440 | tf_op jit(solution)/shard_map/all_to_all | solution.py:268
  123.2 3.2 %fusion.7 = f32[1024,1024]{1,0:T(8,128)S(1)} fusion(bf16[640,1024]{1,0:T(8,128)(2,1)} %copy-done.9, bf16[640,1024]{1,0:T(8,128)(2,1)S(1)} %copy-done.8), kind=kOutput, calls=%fused_computation.19 | convolution fusion | flops 1342177280 | bytes 6815744 | tf_op jit(solution)/shard_map/dot_general | solution.py:273
  126.3 0.2 slice.50
  126.5 5.5 %collective-permute-start.2 = (bf16[1024,512]{1,0:T(8,128)(2,1)S(1)}, bf16[1024,512]{1,0:T(8,128)(2,1)S(1)}, u32[]{:S(2)}, u32[]{:S(2)}) collective-permute-start(bf16[1024,512]{1,0:T(8,128)(2,1)S(1)} %slice.50), channel_id=1, source_target_pairs={{0,64},{64,0},{1,65},{65,1},{2,66},{66,2},{3,67},{67,3},{4,68},{68... | collective-permute-start | bytes 3145736 | tf_op jit(solution)/shard_map/ppermute | solution.py:180
  132.0 2.3 %collective-permute-done.2 = bf16[1024,512]{1,0:T(8,128)(2,1)S(1)} collective-permute-done((bf16[1024,512]{1,0:T(8,128)(2,1)S(1)}, bf16[1024,512]{1,0:T(8,128)(2,1)S(1)}, u32[]{:S(2)}, u32[]{:S(2)}) %collective-permute-start.2) | collective-permute-done | bytes 1048608 | tf_op jit(solution)/shard_map/ppermute | solution.py:180
  134.2 1.3 fusion.4
  135.6 17.6 %all-to-all-done.1 = bf16[64,80,128]{2,1,0:T(8,128)(2,1)S(1)} async-done(((bf16[64,80,128]{2,1,0:T(8,128)(2,1)}), bf16[64,80,128]{2,1,0:T(8,128)(2,1)S(1)}, u32[]{:S(2)}, u32[]{:S(2)}) %all-to-all-start.1) | async-done | bytes 1310752 | tf_op jit(solution)/shard_map/all_to_all | solution.py:268
  153.2 1.0 shard_map.110
  154.2 8.1 %collective-permute-start.9 = (f32[128,512]{1,0:T(8,128)S(1)}, f32[128,512]{1,0:T(8,128)S(1)}, u32[]{:S(2)}, u32[]{:S(2)}) collective-permute-start(f32[128,512]{1,0:T(8,128)S(1)} %slice.35), channel_id=1, source_target_pairs={{0,64},{64,0},{1,65},{65,1},{2,66},{66,2},{3,67},{67,3},{4,68},{68... | collective-permute-start | bytes 786440 | tf_op jit(solution)/shard_map/ppermute | solution.py:180
  162.3 1.1 collective-permute-done.9
  163.5 0.7 fusion.6
  (16 shorter events, 0.0 us)
Async XLA Ops:
  7.2 86.3 %all-gather.2.cloned.1.call-start = ((), (), s32[]{:S(2)}) async-start(), calls=%async_computation.2 | async-start | bytes 5898240 | tf_op jit(solution)/shard_map/all_gather | solution.py:229
  7.2 0.9 copy-start.2
  8.1 0.7 copy-start.3
  9.2 10.9 %collective-permute-start = (bf16[128,512]{1,0:T(8,128)(2,1)S(1)}, bf16[128,512]{1,0:T(8,128)(2,1)S(1)}, u32[]{:S(2)}, u32[]{:S(2)}) collective-permute-start(bf16[128,512]{1,0:T(8,128)(2,1)S(1)} %shard_map.105.mine_ref), channel_id=1, source_target_pairs={{0,64},{64,0},{1,65},{65,1},{2,66},{66,2},{3,67},{67,3},{4,68},{68... | collective-permute-start | bytes 393224 | tf_op jit(solution)/shard_map/ppermute | solution.py:180
  18.0 0.7 copy-start.5
  18.7 0.7 copy-start.6
  19.4 3.2 %copy-start.13 = (bf16[1,160,2,1024]{3,2,1,0:T(2,128)(2,1)S(1)}, bf16[1,160,2,1024]{3,2,1,0:T(2,128)(2,1)}, u32[]{:S(2)}) copy-start(bf16[1,160,2,1024]{3,2,1,0:T(2,128)(2,1)} %param.13) | copy-start | bytes 1966084
  21.9 0.7 copy-start
  22.6 12.1 %copy-start.14 = (f32[3,1,4,8]{3,2,1,0:T(4,128)S(1)}, f32[3,1,4,8]{3,2,1,0:T(4,128)}, u32[]{:S(2)}) copy-start(f32[3,1,4,8]{3,2,1,0:T(4,128)} %param.17) | copy-start | bytes 1156
  23.6 11.5 %copy-start.10 = (bf16[1,1024,512]{2,1,0:T(8,128)(2,1)S(1)}, bf16[1,1024,512]{2,1,0:T(8,128)(2,1)}, u32[]{:S(2)}) copy-start(bf16[1,1024,512]{2,1,0:T(8,128)(2,1)} %param.16) | copy-start | bytes 3145732
  23.6 45.1 %all-to-all-start = ((bf16[64,80,128]{2,1,0:T(8,128)(2,1)}), bf16[64,80,128]{2,1,0:T(8,128)(2,1)S(1)}, u32[]{:S(2)}, u32[]{:S(2)}) async-start(bf16[64,80,128]{2,1,0:T(8,128)(2,1)} %bitcast.11), calls=%async_computation | async-start | bytes 2621440 | tf_op jit(solution)/shard_map/all_to_all | solution.py:222
  35.6 4.6 %collective-permute-start.1 = (bf16[1024,512]{1,0:T(8,128)(2,1)S(1)}, bf16[1024,512]{1,0:T(8,128)(2,1)S(1)}, u32[]{:S(2)}, u32[]{:S(2)}) collective-permute-start(bf16[1024,512]{1,0:T(8,128)(2,1)S(1)} %fusion.2.mine_ref), channel_id=1, source_target_pairs={{0,64},{64,0},{1,65},{65,1},{2,66},{66,2},{3,67},{67,3},{4,68},{68... | collective-permute-start | bytes 3145736 | tf_op jit(solution)/shard_map/ppermute | solution.py:180
  70.3 8.1 %copy-start.7 = (bf16[640,1024]{1,0:T(8,128)(2,1)}, bf16[640,1024]{1,0:T(8,128)(2,1)S(1)}, u32[]{:S(2)}) copy-start(bf16[640,1024]{1,0:T(8,128)(2,1)S(1)} %get-tuple-element.23) | copy-start | bytes 3932164
  70.3 7.4 %copy-start.11 = (bf16[1,512,1024]{2,1,0:T(8,128)(2,1)S(1)}, bf16[1,512,1024]{2,1,0:T(8,128)(2,1)}, u32[]{:S(2)}) copy-start(bf16[1,512,1024]{2,1,0:T(8,128)(2,1)} %param.14) | copy-start | bytes 3145732
  70.4 16.1 %collective-permute-start.3 = (bf16[320,1024]{1,0:T(8,128)(2,1)S(1)}, bf16[320,1024]{1,0:T(8,128)(2,1)S(1)}, u32[]{:S(2)}, u32[]{:S(2)}) collective-permute-start(bf16[320,1024]{1,0:T(8,128)(2,1)S(1)} %get-tuple-element.24), channel_id=1, source_target_pairs={{0,128},{128,0},{256,384},{384,256},{1,129},{129,1},{257,385},{385... | collective-permute-start | bytes 1966088 | tf_op jit(solution)/shard_map/ppermute | solution.py:184
  73.7 17.4 %collective-permute-start.5 = (bf16[320,1024]{1,0:T(8,128)(2,1)S(1)}, bf16[320,1024]{1,0:T(8,128)(2,1)S(1)}, u32[]{:S(2)}, u32[]{:S(2)}) collective-permute-start(bf16[320,1024]{1,0:T(8,128)(2,1)S(1)} %get-tuple-element.25), channel_id=1, source_target_pairs={{0,384},{128,256},{256,128},{384,0},{1,385},{129,257},{257,129},{3... | collective-permute-start | bytes 1966088 | tf_op jit(solution)/shard_map/ppermute | solution.py:184
  78.4 5.1 %copy-start.12 = (bf16[1,512,1024]{2,1,0:T(8,128)(2,1)S(1)}, bf16[1,512,1024]{2,1,0:T(8,128)(2,1)}, u32[]{:S(2)}) copy-start(bf16[1,512,1024]{2,1,0:T(8,128)(2,1)} %param.15) | copy-start | bytes 3145732
  78.4 21.4 %collective-permute-start.7 = (bf16[512,1024]{1,0:T(8,128)(2,1)S(1)}, bf16[512,1024]{1,0:T(8,128)(2,1)}, u32[]{:S(2)}, u32[]{:S(2)}) collective-permute-start(bf16[512,1024]{1,0:T(8,128)(2,1)S(1)} %fusion.1.gm_ref), channel_id=1, source_target_pairs={{0,64},{64,0},{1,65},{65,1},{2,66},{66,2},{3,67},{67,3},{4,68},{68... | collective-permute-start | bytes 3145736 | tf_op jit(solution)/shard_map/ppermute | solution.py:180
  84.3 15.6 %collective-permute-start.8 = (bf16[512,1024]{1,0:T(8,128)(2,1)S(1)}, bf16[512,1024]{1,0:T(8,128)(2,1)}, u32[]{:S(2)}, u32[]{:S(2)}) collective-permute-start(bf16[512,1024]{1,0:T(8,128)(2,1)S(1)} %fusion.um_ref), channel_id=1, source_target_pairs={{0,64},{64,0},{1,65},{65,1},{2,66},{66,2},{3,67},{67,3},{4,68},{68... | collective-permute-start | bytes 3145736 | tf_op jit(solution)/shard_map/ppermute | solution.py:180
  86.7 18.4 %collective-permute-start.4 = (bf16[320,1024]{1,0:T(8,128)(2,1)S(1)}, bf16[320,1024]{1,0:T(8,128)(2,1)}, u32[]{:S(2)}, u32[]{:S(2)}) collective-permute-start(bf16[320,1024]{1,0:T(8,128)(2,1)S(1)} %add_convert_fusion.1.low), channel_id=1, source_target_pairs={{0,384},{128,256},{256,128},{384,0},{1,385},{129,257},{257,129},{3... | collective-permute-start | bytes 1966088 | tf_op jit(solution)/shard_map/ppermute | solution.py:184
  91.4 14.3 %collective-permute-start.6 = (bf16[320,1024]{1,0:T(8,128)(2,1)S(1)}, bf16[320,1024]{1,0:T(8,128)(2,1)}, u32[]{:S(2)}, u32[]{:S(2)}) collective-permute-start(bf16[320,1024]{1,0:T(8,128)(2,1)S(1)} %add_convert_fusion.high), channel_id=1, source_target_pairs={{0,128},{128,0},{256,384},{384,256},{1,129},{129,1},{257,385},{385... | collective-permute-start | bytes 1966088 | tf_op jit(solution)/shard_map/ppermute | solution.py:184
  93.5 2.5 %copy-start.4 = (bf16[2,1280,1024]{2,1,0:T(8,128)(2,1)S(1)}, bf16[2,1280,1024]{2,1,0:T(8,128)(2,1)}, u32[]{:S(2)}) copy-start(bf16[2,1280,1024]{2,1,0:T(8,128)(2,1)} %all-gather.2.cloned.1.call-done.pre_ref) | copy-start | bytes 15728644
  99.9 12.0 %copy-start.9 = (bf16[640,1024]{1,0:T(8,128)(2,1)}, bf16[640,1024]{1,0:T(8,128)(2,1)S(1)}, u32[]{:S(2)}) copy-start(bf16[640,1024]{1,0:T(8,128)(2,1)S(1)} %get-tuple-element.20) | copy-start | bytes 3932164
  111.8 11.3 %copy-start.8 = (bf16[640,1024]{1,0:T(8,128)(2,1)S(1)}, bf16[640,1024]{1,0:T(8,128)(2,1)}, u32[]{:S(2)}) copy-start(bf16[640,1024]{1,0:T(8,128)(2,1)} %copy-done.7) | copy-start | bytes 3932164
  111.8 41.4 %all-to-all-start.1 = ((bf16[64,80,128]{2,1,0:T(8,128)(2,1)}), bf16[64,80,128]{2,1,0:T(8,128)(2,1)S(1)}, u32[]{:S(2)}, u32[]{:S(2)}) async-start(bf16[64,80,128]{2,1,0:T(8,128)(2,1)} %bitcast.21), calls=%async_computation.1 | async-start | bytes 2621440 | tf_op jit(solution)/shard_map/all_to_all | solution.py:268
  126.5 26.7 %copy-start.1 = (bf16[1,640,128]{2,1,0:T(8,128)(2,1)S(1)}, bf16[1,640,128]{2,1,0:T(8,128)(2,1)}, u32[]{:S(2)}) copy-start(bf16[1,640,128]{2,1,0:T(8,128)(2,1)} %copy-done) | copy-start | bytes 491524
  126.5 7.7 %collective-permute-start.2 = (bf16[1024,512]{1,0:T(8,128)(2,1)S(1)}, bf16[1024,512]{1,0:T(8,128)(2,1)S(1)}, u32[]{:S(2)}, u32[]{:S(2)}) collective-permute-start(bf16[1024,512]{1,0:T(8,128)(2,1)S(1)} %slice.50), channel_id=1, source_target_pairs={{0,64},{64,0},{1,65},{65,1},{2,66},{66,2},{3,67},{67,3},{4,68},{68... | collective-permute-start | bytes 3145736 | tf_op jit(solution)/shard_map/ppermute | solution.py:180
  154.2 9.2 %collective-permute-start.9 = (f32[128,512]{1,0:T(8,128)S(1)}, f32[128,512]{1,0:T(8,128)S(1)}, u32[]{:S(2)}, u32[]{:S(2)}) collective-permute-start(f32[128,512]{1,0:T(8,128)S(1)} %slice.35), channel_id=1, source_target_pairs={{0,64},{64,0},{1,65},{65,1},{2,66},{66,2},{3,67},{67,3},{4,68},{68... | collective-permute-start | bytes 786440 | tf_op jit(solution)/shard_map/ppermute | solution.py:180
Sparse Core Ops, SparseCore 0:
  23.7 41.0 all-gather.1

commit v3 on v2

--- a/solution.py
+++ b/solution.py
@@ -4,6 +4,7 @@
 import jax.numpy as jnp
 from jax import lax
 from jax.experimental import pallas as pl
+from jax.experimental.layout import Layout, with_layout_constraint
 from jax.experimental.pallas import tpu as pltpu
 from jax.sharding import Mesh
 from jax.sharding import PartitionSpec as P
@@ -11,7 +12,6 @@
 EXPERT = ("z", "y")
 SEQ = ("x", "core")
 XS = 4
-CHUNKS = 1
 LANES = 128
 HIGHEST = lax.Precision.HIGHEST
 NT = (((1,), (1,)), ((), ()))
@@ -20,7 +20,7 @@
 BF16 = jnp.bfloat16
 
 
-def vmem_call(body, out_shape, n_smem, n_in, flops, nbytes, scratch=(), limit=40 << 20):
+def vmem_call(body, out_shape, n_smem, n_in, flops, nbytes, scratch=(), limit=16 << 20):
     smem = pl.BlockSpec(memory_space=pltpu.SMEM)
     vmem = pl.BlockSpec(memory_space=pltpu.VMEM)
     outs = jax.tree.map(lambda _: vmem, out_shape)
@@ -89,12 +89,10 @@
     )
     place = iota((rows, tokens), 0).astype(F32)
     place = place - slots * jnp.floor((place + 0.5) * (1.0 / slots))
-    base = (core_ref[0] * (slots * CHUNKS)).astype(F32)
-    for ch in range(CHUNKS):
-        hit = slot_row == place + (base + float(ch * slots))
-        pick_ref[ch] = onehot(hit)
-        gate = jnp.sum(jnp.where(hit, weight_row, 0.0), axis=1, keepdims=True)
-        gate_ref[ch] = jnp.broadcast_to(gate, (rows, tokens))
+    hit = slot_row == place + (core_ref[0] * slots).astype(F32)
+    pick_ref[...] = onehot(hit)
+    gate = jnp.sum(jnp.where(hit, weight_row, 0.0), axis=1, keepdims=True)
+    gate_ref[...] = jnp.broadcast_to(gate, (rows, tokens))
 
 
 def tile_rows(value, tile_s, at):
@@ -113,31 +111,76 @@
         )
 
 
-def dispatch_body(pick_ref, gate_ref, mine_ref, other_ref, *refs):
-    out_refs, tile_s = refs[:-1], refs[-1]
-    for ch in range(CHUNKS):
-        pick = pick_ref[ch]
-        gate = gate_ref[ch][:, :1]
-        for i, half in enumerate((mine_ref, other_ref)):
-            rows = jnp.dot(pick, half[...], preferred_element_type=F32) * gate
-            tile_rows(rows, tile_s, i * half.shape[1] // LANES)
-        out_refs[ch][...] = tile_s[...].reshape(out_refs[ch].shape).astype(BF16)
-
-
-def factor_body(slots, ch, core_ref, pre_ref, silu_ref, slope_ref, act_ref):
-    rows, whole = silu_ref.shape[0], pre_ref.shape[1]
-    cap = whole // (rows // slots)
-    row = iota((rows, whole), 0).astype(F32)
-    group = jnp.floor((row + 0.5) * (1.0 / slots))
-    base = (core_ref[0] * (slots * CHUNKS) + ch * slots).astype(F32)
-    pick = onehot(iota((rows, whole), 1).astype(F32) == row + group * (cap - slots) + base)
-    gate_pre = jnp.dot(pick, pre_ref[0], preferred_element_type=F32)
-    up_pre = jnp.dot(pick, pre_ref[1], preferred_element_type=F32)
-    sig = jax.nn.sigmoid(gate_pre)
-    silu = gate_pre * sig
-    silu_ref[...] = silu.astype(BF16)
-    slope_ref[...] = (up_pre * sig * (1.0 + gate_pre * (1.0 - sig))).astype(BF16)
-    act_ref[...] = (silu * up_pre).astype(BF16)
+def dispatch_body(pick_ref, gate_ref, mine_ref, other_ref, out_ref, tile_s):
+    pick = pick_ref[...]
+    gate = gate_ref[:, :1]
+    for i, half in enumerate((mine_ref, other_ref)):
+        rows = jnp.dot(pick, half[...], preferred_element_type=F32) * gate
+        tile_rows(rows, tile_s, i * half.shape[1] // LANES)
+    out_ref[...] = tile_s[...].reshape(out_ref.shape).astype(BF16)
+
+
+def side_body(turn, core_ref, pre_ref, rows_ref, *refs):
+    outs, (silu_v, slope_v, act_v, mine_v, other_v, sems) = refs[-10:-6], refs[-6:]
+    rows = rows_ref.shape[0]
+    cols = mine_v.shape[1]
+    size = rows // 4
+
+    @pl.when(core_ref[0] == turn)
+    def _():
+        for at in range(0, rows, size):
+            cut = slice(at, at + size)
+            gate_pre = pre_ref[0, cut, :].astype(F32)
+            up_pre = pre_ref[1, cut, :].astype(F32)
+            sig = jax.nn.sigmoid(gate_pre)
+            silu = gate_pre * sig
+            silu_v[cut, :] = silu.astype(BF16)
+            slope_v[cut, :] = (up_pre * sig * (1.0 + gate_pre * (1.0 - sig))).astype(BF16)
+            act_v[cut, :] = (silu * up_pre).astype(BF16)
+        held = (silu_v, slope_v, mine_v, other_v)
+        stores = [
+            pltpu.make_async_copy(src, dst, sems.at[i])
+            for i, (src, dst) in enumerate(zip(held, outs))
+        ]
+        stores[0].start()
+        stores[1].start()
+        mine_v[...] = lax.dot_general(
+            act_v[...], rows_ref[:, :cols], TN, preferred_element_type=F32
+        )
+        stores[2].start()
+        other_v[...] = lax.dot_general(
+            act_v[...], rows_ref[:, cols:], TN, preferred_element_type=F32
+        ).astype(BF16)
+        stores[3].start()
+        for store in stores:
+            store.wait()
+
+
+def side_call(turn, core, pre, arrived, before):
+    rows, width = arrived.shape
+    hid = pre.shape[2]
+    held = pl.BlockSpec(memory_space=pl.ANY)
+    vmem = pl.BlockSpec(memory_space=pltpu.VMEM)
+    wide, tall = (rows, hid), (hid, width // 2)
+    return pl.pallas_call(
+        functools.partial(side_body, turn),
+        out_shape=(shape(wide), shape(wide), shape(tall, F32), shape(tall)),
+        in_specs=[pl.BlockSpec(memory_space=pltpu.SMEM), vmem, vmem] + [held] * len(before),
+        out_specs=(held,) * 4,
+        scratch_shapes=[
+            pltpu.VMEM(wide, BF16),
+            pltpu.VMEM(wide, BF16),
+            pltpu.VMEM(wide, BF16),
+            pltpu.VMEM(tall, F32),
+            pltpu.VMEM(tall, BF16),
+            pltpu.SemaphoreType.DMA((4,)),
+        ],
+        input_output_aliases={3 + i: i for i in range(len(before))},
+        compiler_params=pltpu.CompilerParams(vmem_limit_bytes=22 << 20),
+        cost_estimate=pl.CostEstimate(
+            flops=2 * rows * width * hid, bytes_accessed=11 << 20, transcendentals=0
+        ),
+    )(core, pre, arrived, *before)
 
 
 def hidden_body(tile_ref, mine_ref, other_ref, rows_ref, low_ref, high_ref, tile_s):
@@ -198,7 +241,7 @@
     width = 2 * cols
     per = width // LANES
     cap = rows_dev * XS * 2 // experts
-    slots = cap // 2 // CHUNKS
+    slots = cap // 2
     rows = experts * slots
     tiles = (rows, per, LANES)
     block = (experts, slots * per, LANES)
@@ -207,82 +250,76 @@
         dy_values[0], dy_scales[0].T
     )
     other = swap(mine)
+    saved_pre, mine = lax.optimization_barrier((saved_pre, mine))
+    pre = lax.all_gather(saved_pre[0], SEQ, axis=0, tiled=True)
+    pre = with_layout_constraint(pre, Layout((0, 1, 2)))
     pick, gate = vmem_call(
         functools.partial(select_body, experts, slots),
-        (shape((CHUNKS, rows, tokens)), shape((CHUNKS, rows, tokens), F32)),
+        (shape((rows, tokens)), shape((rows, tokens), F32)),
         1, 2, 4 * rows * experts * tokens, 1 << 20,
     )(core, route_expert[0].T, gate_weight[0].T)
     outgoing = vmem_call(
         dispatch_body,
-        tuple(shape(tiles) for _ in range(CHUNKS)),
-        0, 4, 2 * CHUNKS * rows * tokens * width, 2 << 20,
+        shape(tiles),
+        0, 4, 2 * rows * tokens * width, 2 << 20,
         scratch=(pltpu.VMEM((rows * per, LANES), F32),),
     )(pick, gate, mine, other)
-    incoming = [
-        lax.all_to_all(sent.reshape(block), EXPERT, 0, 0, tiled=True).reshape(tiles)
-        for sent in outgoing
-    ]
-
-    saved_pre, w_gate, w_up, w_down, w_scale, _ = lax.optimization_barrier(
-        (saved_pre, w_gate, w_up, w_down, w_scale, outgoing[0])
-    )
-    pre = lax.all_gather(saved_pre[0].transpose(1, 0, 2), SEQ, axis=1, tiled=True)
+    outgoing, w_gate, w_up, w_down, w_scale = lax.optimization_barrier(
+        (outgoing, w_gate, w_up, w_down, w_scale)
+    )
+    incoming = lax.all_to_all(outgoing.reshape(block), EXPERT, 0, 0, tiled=True).reshape(tiles)
     scales = w_scale[:, 0]
     down_m = dequant_matrix(w_down[0], scales[2].T)
+    down_o = swap(down_m)
     gate_m = dequant_matrix(w_gate[0], scales[0])
     up_m = dequant_matrix(w_up[0], scales[1])
-    down_o = swap(down_m)
     gate_o = swap(gate_m)
     up_o = swap(up_m)
-
-    taken, returned, acts = [], [], []
-    for ch in range(CHUNKS):
-        silu, slope, act = vmem_call(
-            functools.partial(factor_body, slots, ch),
-            tuple(shape((rows, hid)) for _ in range(3)),
-            1, 1, 4 * rows * rows_dev * XS * 2 * hid, 8 << 20,
-        )(core, pre)
-        acts.append(act)
-        arrived, low, high = vmem_call(
-            hidden_body,
-            (shape((rows, width)), shape((rows // 2, hid)), shape((rows // 2, hid))),
-            0, 3, 2 * rows * width * hid, 4 << 20,
-            scratch=(pltpu.VMEM((rows * per, LANES), F32),),
-        )(incoming[ch], down_m, down_o)
-        taken.append(arrived)
-        low = added(low, pair(low, 1))
-        high = added(high, pair(high, 3))
-        low_in = pair(low, 3)
-        high_in = pair(high, 1)
-        value = vmem_call(
-            back_body,
-            shape(tiles),
-            0, 10, 4 * rows * width * hid, 6 << 20,
-            scratch=(
-                pltpu.VMEM((rows, hid), BF16),
-                pltpu.VMEM((rows, hid), BF16),
-                pltpu.VMEM((rows * per, LANES), F32),
-            ),
-        )(low, low_in, high, high_in, silu, slope, gate_m, gate_o, up_m, up_o)
-        returned.append(
-            lax.all_to_all(value.reshape(block), EXPERT, 0, 0, tiled=True).reshape(tiles)
-        )
-
-    down_total = 0.0
-    for act, arrived in zip(acts, taken):
-        down_total = down_total + lax.dot_general(act, arrived, TN, preferred_element_type=F32)
-    down_grad = down_total[:, :cols] + swap(down_total[:, cols:].astype(BF16)).astype(F32)
+    pre = lax.dynamic_slice_in_dim(
+        pre.reshape(experts, cap, 2, hid), core[0] * slots, slots, axis=1
+    )
+    pre = pre.reshape(rows, 2, hid).transpose(1, 0, 2)
+    incoming, pre, gate_o, up_o = lax.optimization_barrier((incoming, pre, gate_o, up_o))
+
+    half = rows // 2
+    arrived, low, high = vmem_call(
+        hidden_body,
+        (shape((rows, width)), shape((half, hid)), shape((half, hid))),
+        0, 3, 2 * rows * width * hid, 4 << 20,
+        scratch=(pltpu.VMEM((rows * per, LANES), F32),),
+    )(incoming, down_m, down_o)
+
+    side = side_call(0, core, pre, arrived, ())
+    low, high, *side = lax.optimization_barrier((low, high, *side))
+    low = added(low, pair(low, 1))
+    high = added(high, pair(high, 3))
+    high, *side = lax.optimization_barrier((high, *side))
+    silu, slope, down_mine, down_other = side_call(1, core, pre, arrived, side)
+    sent = vmem_call(
+        back_body,
+        shape(tiles),
+        0, 10, 4 * rows * width * hid, 6 << 20,
+        scratch=(
+            pltpu.VMEM((rows, hid), BF16),
+            pltpu.VMEM((rows, hid), BF16),
+            pltpu.VMEM((rows * per, LANES), F32),
+        ),
+        limit=20 << 20,
+    )(
+        low, pair(low, 3), high, pair(high, 1), silu, slope, gate_m, gate_o, up_m, up_o
+    )
+    returned = lax.all_to_all(sent.reshape(block), EXPERT, 0, 0, tiled=True).reshape(tiles)
+
+    down_grad = down_mine + swap(down_other).astype(F32)
     down_grad = down_grad.astype(BF16)[None]
-    down_grad, *returned = lax.optimization_barrier((down_grad, *returned))
-
-    combined = 0.0
-    for ch in range(CHUNKS):
-        combined = combined + vmem_call(
-            combine_body,
-            shape((tokens, width), F32),
-            0, 2, 2 * rows * tokens * width, 2 << 20,
-            scratch=(pltpu.VMEM((rows, width), BF16), pltpu.VMEM((rows * per, LANES), F32)),
-        )(pick[ch], returned[ch])
+    down_grad, returned = lax.optimization_barrier((down_grad, returned))
+
+    combined = vmem_call(
+        combine_body,
+        shape((tokens, width), F32),
+        0, 2, 2 * rows * tokens * width, 2 << 20,
+        scratch=(pltpu.VMEM((rows, width), BF16), pltpu.VMEM((rows * per, LANES), F32)),
+    )(pick, returned)
     input_grad = combined[:, :cols] + swap(combined[:, cols:])
     return (input_grad.astype(BF16)[None], down_grad)
 

time: 172 us -> 169 us (0.983)
  waiting for transfers between devices: 58 us -> 45.6 us
  local copies, waits for them, and re-layouts: 8.14 us -> 13.1 us
  starting transfers between devices: 67.4 us -> 71.2 us
  matrix products: 3.15 us -> 0 us
  other arithmetic: 4.34 us -> 7.06 us
    all_to_all x1, waiting for transfers between devices: 28.5 us -> 11.4 us  [shards(): lax.all_to_all(sent.reshape(block), EXPERT, 0, 0, tiled=True).reshape(tiles)]
    all_to_all x1, waiting for transfers between devices: 17.6 us -> 5.49 us  [shards(): lax.all_to_all(outgoing.reshape(block), EXPERT, 0, 0, tiled=True)]
    all_gather x1, waiting for transfers between devices: 0.02 us -> 11.8 us  [shards(): pre = lax.all_gather(saved_pre[0], SEQ, axis=0, tiled=True)]
    ppermute x4, waiting for transfers between devices: 6.01 us -> 13.3 us  [pair(): return lax.ppermute(value, 'x', [(i, i ^ mask) for i in range(XS)])]
    ppermute x6, starting transfers between devices: 31.4 us -> 38.4 us  [swap(): return lax.ppermute(value, 'core', [(0, 1), (1, 0)])]
    dynamic_slice x0 -> x1, local copies, waits for them, and re-layouts: none -> 3.55 us  [shards(): lax.dynamic_slice_in_dim(pre.reshape(experts, cap, 2, hid), core[0] * slo...]
    dot_general x1 -> x0, matrix products: 3.15 us -> none  [shards(): lax.dot_general(act, arrived, TN, preferred_element_type=F32)]
    convert_element_type x3, other arithmetic: 1.84 us -> 4.57 us  [dequant_matrix(): (grid * scales[:, None, :, None]).reshape(rows_in, cols_in).astype(BF16)]
  transfers between devices with their start and end apart: 13 -> 13, of which waited for: 8 -> 8; matrix products, arithmetic and copies ran while one was open for 5% -> 7% of each run, Pallas kernels for 4% -> 4%
where the time goes in v3:
time: 169 us; the launch traced here: 168 us
  starting transfers between devices  71.2 us (42%)
  waiting for transfers between devices  45.6 us (27%)
  Pallas kernels  17 us (10%)
  between operations  14.4 us (9%)
  local copies, waits for them, and re-layouts  13.1 us (8%)
  other arithmetic  7.06 us (4%)
    ppermute x6, starting transfers between devices, swap(): return lax.ppermute(value, 'core', [(0, 1), (1, 0)])  38.4 us
    ppermute x4, waiting for transfers between devices, pair(): return lax.ppermute(value, 'x', [(i, i ^ mask) for i in range(XS)])  13.3 us
    ppermute x4, starting transfers between devices, pair(): return lax.ppermute(value, 'x', [(i, i ^ mask) for i in range(XS)])  11.9 us
    all_gather x1, waiting for transfers between devices, shards(): pre = lax.all_gather(saved_pre[0], SEQ, axis=0, tiled=True)  11.8 us
    all_to_all x1, waiting for transfers between devices, shards(): lax.all_to_all(sent.reshape(block), EXPERT, 0, 0, tiled=True).reshape(tiles)  11.4 us
    all_to_all x1, starting transfers between devices, shards(): lax.all_to_all(outgoing.reshape(block), EXPERT, 0, 0, tiled=True)  11.3 us
    all_to_all x1, starting transfers between devices, shards(): lax.all_to_all(sent.reshape(block), EXPERT, 0, 0, tiled=True).reshape(tiles)  9.63 us
    unnamed x28, local copies, waits for them, and re-layouts  7.9 us
  transfers between devices with their start and end apart: 13, of which 8 were waited for; matrix products, arithmetic and copies ran while one was open for 7% of the time, Pallas kernels for 4%

profile of v3, /device:TPU:1, one launch (start us, length us, event | category | flops | bytes accessed | tf_op | source)
XLA Modules:
  0.0 168.3 jit_solution(127657137828745531)
XLA Ops:
  7.2 0.0 all-gather.3.cloned.1.call-start
  7.2 0.0 copy-start.6
  7.2 0.9 copy-done.6
  8.1 0.7 copy-done.7
  8.8 0.4 shard_map.105.mine_ref
  9.2 0.0 all-gather.3.cloned.1.call-update
  9.2 8.8 %collective-permute-start = (bf16[128,512]{1,0:T(8,128)(2,1)S(1)}, bf16[128,512]{1,0:T(8,128)(2,1)S(1)}, u32[]{:S(2)}, u32[]{:S(2)}) collective-permute-start(bf16[128,512]{1,0:T(8,128)(2,1)S(1)} %shard_map.105.mine_ref), channel_id=1, source_target_pairs={{0,64},{64,0},{1,65},{65,1},{2,66},{66,2},{3,67},{67,3},{4,68},{68... | collective-permute-start | bytes 393224 | tf_op jit(solution)/shard_map/ppermute | solution.py:223
  18.0 0.0 copy-start.8
  18.1 0.7 copy-done.8
  18.7 0.7 copy-done.9
  19.4 0.7 shard_map.104
  20.1 0.0 collective-permute-done.other_ref
  20.1 0.0 copy-start.13
  20.1 1.8 %shard_map.106 = bf16[640,8,128]{2,1,0:T(8,128)(2,1)} custom-call(bf16[640,128]{1,0:T(8,128)(2,1)S(1)} %get-tuple-element.39.pick_ref, f32[640,128]{1,0:T(8,128)S(1)} %get-tuple-element.40.gate_ref, bf16[128,512]{1,0:T(8,128)(2,1)S(1)} %shard_map.105.mine_ref, bf16[128,512]{1,0:T(8,128)(2,1)S(1)} %collective-permute-done.other_ref), custom_call_target="tpu_custom_call" | custom-call | flops 167772160 | bytes 2097152 | tf_op jit(solution)/shard_map/pallas_call | solution.py:261
  21.9 0.7 copy-done.4
  22.6 11.3 %all-to-all-start = ((bf16[64,80,128]{2,1,0:T(8,128)(2,1)}), bf16[64,80,128]{2,1,0:T(8,128)(2,1)}, u32[]{:S(2)}, u32[]{:S(2)}) async-start(bf16[64,80,128]{2,1,0:T(8,128)(2,1)} %bitcast.8), calls=%async_computation | async-start | bytes 2621440 | tf_op jit(solution)/shard_map/all_to_all | solution.py:270
  33.9 0.0 copy-done.13
  33.9 0.1 copy.21
  34.0 0.2 mul.46
  34.2 0.0 copy-done.10
  34.2 1.6 fusion.1.um_ref
  35.8 2.3 %collective-permute-start.2 = (bf16[512,1024]{1,0:T(8,128)(2,1)}, bf16[512,1024]{1,0:T(8,128)(2,1)}, u32[]{:S(2)}, u32[]{:S(2)}) collective-permute-start(bf16[512,1024]{1,0:T(8,128)(2,1)} %fusion.1.um_ref), channel_id=1, source_target_pairs={{0,64},{64,0},{1,65},{65,1},{2,66},{66,2},{3,67},{67,3},{4,68},{68... | collective-permute-start | bytes 3145736 | tf_op jit(solution)/shard_map/ppermute | solution.py:223
  38.1 0.2 mul.42
  38.3 0.0 copy-done.11
  38.3 1.6 fusion.2.gm_ref
  39.9 2.2 %collective-permute-start.1 = (bf16[512,1024]{1,0:T(8,128)(2,1)}, bf16[512,1024]{1,0:T(8,128)(2,1)}, u32[]{:S(2)}, u32[]{:S(2)}) collective-permute-start(bf16[512,1024]{1,0:T(8,128)(2,1)} %fusion.2.gm_ref), channel_id=1, source_target_pairs={{0,64},{64,0},{1,65},{65,1},{2,66},{66,2},{3,67},{67,3},{4,68},{68... | collective-permute-start | bytes 3145736 | tf_op jit(solution)/shard_map/ppermute | solution.py:223
  42.2 0.3 mul.49
  42.5 1.4 fusion.mine_ref
  43.9 2.2 %collective-permute-start.3 = (bf16[1024,512]{1,0:T(8,128)(2,1)}, bf16[1024,512]{1,0:T(8,128)(2,1)}, u32[]{:S(2)}, u32[]{:S(2)}) collective-permute-start(bf16[1024,512]{1,0:T(8,128)(2,1)} %fusion.mine_ref), channel_id=1, source_target_pairs={{0,64},{64,0},{1,65},{65,1},{2,66},{66,2},{3,67},{67,3},{4,68},{68... | collective-permute-start | bytes 3145736 | tf_op jit(solution)/shard_map/ppermute | solution.py:223
  46.1 11.8 %all-gather.3.cloned.1.call-done = bf16[1,1280,2,1024]{3,2,0,1:T(2,128)(2,1)} async-done(((bf16[1,160,2,1024]{3,2,0,1:T(2,128)(2,1)}), bf16[1,1280,2,1024]{3,2,0,1:T(2,128)(2,1)}) %all-gather.3.cloned.1.call-update) | async-done | bytes 5242896 | tf_op jit(solution)/shard_map/all_gather | solution.py:254
  57.9 3.5 %constant_dynamic-slice_fusion = bf16[64,10,2,1024]{3,2,1,0:T(2,128)(2,1)S(1)} fusion(bf16[64,20,2,1024]{3,2,1,0:T(2,128)(2,1)} %bitcast.74, s32[]{:T(128)S(6)} %select_n.3), kind=kLoop, calls=%fused_computation.17 | loop fusion | bytes 5242884 | tf_op jit(solution)/shard_map/dynamic_slice | solution.py:278
  61.4 0.8 copy.29
  62.2 0.0 collective-permute-done.2.uo_ref
  62.2 0.0 collective-permute-done.1.go_ref
  62.3 5.5 %all-to-all-done = bf16[64,80,128]{2,1,0:T(8,128)(2,1)} async-done(((bf16[64,80,128]{2,1,0:T(8,128)(2,1)}), bf16[64,80,128]{2,1,0:T(8,128)(2,1)}, u32[]{:S(2)}, u32[]{:S(2)}) %all-to-all-start) | async-done | bytes 1310752 | tf_op jit(solution)/shard_map/all_to_all | solution.py:270
  67.7 0.0 collective-permute-done.3.other_ref
  67.7 3.6 %shard_map.107 = (bf16[640,1024]{1,0:T(8,128)(2,1)S(1)}, bf16[320,1024]{1,0:T(8,128)(2,1)S(1)}, bf16[320,1024]{1,0:T(8,128)(2,1)S(1)}) custom-call(bf16[640,8,128]{2,1,0:T(8,128)(2,1)} %bitcast.9.tile_ref, bf16[1024,512]{1,0:T(8,128)(2,1)} %fusion.mine_ref, bf16[1024,512]{1,0:T(8,128)(2,1)} %collective-permute-done.3.other_ref), custom_call_target="tpu_custom_call" | custom-call | flops 1342177280 | bytes 4194304 | tf_op jit(solution)/shard_map/pallas_call | solution.py:285
  71.4 0.2 shard_map.108
  71.6 4.4 %collective-permute-start.4 = (bf16[320,1024]{1,0:T(8,128)(2,1)S(1)}, bf16[320,1024]{1,0:T(8,128)(2,1)S(1)}, u32[]{:S(2)}, u32[]{:S(2)}) collective-permute-start(bf16[320,1024]{1,0:T(8,128)(2,1)S(1)} %get-tuple-element.57), channel_id=1, source_target_pairs={{0,384},{128,256},{256,128},{384,0},{1,385},{129,257},{257,129},{3... | collective-permute-start | bytes 1966088 | tf_op jit(solution)/shard_map/ppermute | solution.py:227
  76.0 1.9 %collective-permute-start.6 = (bf16[320,1024]{1,0:T(8,128)(2,1)S(1)}, bf16[320,1024]{1,0:T(8,128)(2,1)S(1)}, u32[]{:S(2)}, u32[]{:S(2)}) collective-permute-start(bf16[320,1024]{1,0:T(8,128)(2,1)S(1)} %get-tuple-element.68), channel_id=1, source_target_pairs={{0,128},{128,0},{256,384},{384,256},{1,129},{129,1},{257,385},{385... | collective-permute-start | bytes 1966088 | tf_op jit(solution)/shard_map/ppermute | solution.py:227
  77.9 6.8 %collective-permute-done.4 = bf16[320,1024]{1,0:T(8,128)(2,1)S(1)} collective-permute-done((bf16[320,1024]{1,0:T(8,128)(2,1)S(1)}, bf16[320,1024]{1,0:T(8,128)(2,1)S(1)}, u32[]{:S(2)}, u32[]{:S(2)}) %collective-permute-start.4) | collective-permute-done | bytes 655392 | tf_op jit(solution)/shard_map/ppermute | solution.py:227
  84.7 0.2 add_convert_fusion.2.high
  84.9 1.9 %collective-permute-start.8 = (bf16[320,1024]{1,0:T(8,128)(2,1)S(1)}, bf16[320,1024]{1,0:T(8,128)(2,1)S(1)}, u32[]{:S(2)}, u32[]{:S(2)}) collective-permute-start(bf16[320,1024]{1,0:T(8,128)(2,1)S(1)} %add_convert_fusion.2.high), channel_id=1, source_target_pairs={{0,128},{128,0},{256,384},{384,256},{1,129},{129,1},{257,385},{385... | collective-permute-start | bytes 1966088 | tf_op jit(solution)/shard_map/ppermute | solution.py:227
  86.9 0.7 collective-permute-done.6
  87.6 0.2 add_convert_fusion.1.low
  87.9 3.6 %collective-permute-start.7 = (bf16[320,1024]{1,0:T(8,128)(2,1)S(1)}, bf16[320,1024]{1,0:T(8,128)(2,1)S(1)}, u32[]{:S(2)}, u32[]{:S(2)}) collective-permute-start(bf16[320,1024]{1,0:T(8,128)(2,1)S(1)} %add_convert_fusion.1.low), channel_id=1, source_target_pairs={{0,384},{128,256},{256,128},{384,0},{1,385},{129,257},{257,129},{3... | collective-permute-start | bytes 1966088 | tf_op jit(solution)/shard_map/ppermute | solution.py:227
  91.5 4.0 %shard_map.109 = (bf16[640,1024]{1,0:T(8,128)(2,1)S(1)}, bf16[640,1024]{1,0:T(8,128)(2,1)S(1)}, f32[1024,512]{1,0:T(8,128)S(1)}, bf16[1024,512]{1,0:T(8,128)(2,1)S(1)}) custom-call(s32[1]{0:T(128)} %bitcast.core_ref, bf16[2,640,1024]{2,1,0:T(8,128)(2,1)S(1)} %bitcast.63, ...), custom_call_target="tpu_custom_call", output_to_operand_aliasing={{0}: (3, {}), {1}: (4, {}), {2}: (5, {}), {3}: (6, {})} | custom-call | flops 1342177280 | bytes 11534336 | tf_op jit(solution)/shard_map/pallas_call | solution.py:165
  95.5 1.3 copy-done
  96.9 1.0 copy-done.3
  97.8 5.8 %collective-permute-done.8.high_in = bf16[320,1024]{1,0:T(8,128)(2,1)S(1)} collective-permute-done((bf16[320,1024]{1,0:T(8,128)(2,1)S(1)}, bf16[320,1024]{1,0:T(8,128)(2,1)S(1)}, u32[]{:S(2)}, u32[]{:S(2)}) %collective-permute-start.8) | collective-permute-done | bytes 655392 | tf_op jit(solution)/shard_map/ppermute | solution.py:227
  103.6 0.0 collective-permute-done.7.low_in
  103.6 5.3 %shard_map.110 = bf16[640,8,128]{2,1,0:T(8,128)(2,1)S(1)} custom-call(bf16[320,1024]{1,0:T(8,128)(2,1)S(1)} %add_convert_fusion.1.low, bf16[320,1024]{1,0:T(8,128)(2,1)S(1)} %collective-permute-done.7.low_in, bf16[320,1024]{1,0:T(8,128)(2,1)S(1)} %add_convert_fusion.2.high, bf16[320,1024]{1,0:T(8,128)(2,1)S(1)} %collective-permute-done.8.high_in, ...), custom_call_target="tpu_custom_call" | custom-call | flops 2684354560 | bytes 6291456 | tf_op jit(solution)/shard_map/pallas_call | solution.py:298
  109.0 0.0 copy-start.2
  109.0 1.1 copy-done.2
  110.0 9.6 %all-to-all-start.1 = ((bf16[64,80,128]{2,1,0:T(8,128)(2,1)}), bf16[64,80,128]{2,1,0:T(8,128)(2,1)S(1)}, u32[]{:S(2)}, u32[]{:S(2)}) async-start(bf16[64,80,128]{2,1,0:T(8,128)(2,1)} %bitcast.65), calls=%async_computation.1 | async-start | bytes 2621440 | tf_op jit(solution)/shard_map/all_to_all | solution.py:311
  119.7 10.3 %collective-permute-start.5 = (bf16[1024,512]{1,0:T(8,128)(2,1)}, bf16[1024,512]{1,0:T(8,128)(2,1)S(1)}, u32[]{:S(2)}, u32[]{:S(2)}) collective-permute-start(bf16[1024,512]{1,0:T(8,128)(2,1)} %copy-done.3), channel_id=1, source_target_pairs={{0,64},{64,0},{1,65},{65,1},{2,66},{66,2},{3,67},{67,3},{4,68},{68... | collective-permute-start | bytes 3145736 | tf_op jit(solution)/shard_map/ppermute | solution.py:223
  130.0 2.5 %collective-permute-done.5 = bf16[1024,512]{1,0:T(8,128)(2,1)S(1)} collective-permute-done((bf16[1024,512]{1,0:T(8,128)(2,1)}, bf16[1024,512]{1,0:T(8,128)(2,1)S(1)}, u32[]{:S(2)}, u32[]{:S(2)}) %collective-permute-start.5) | collective-permute-done | bytes 1048608 | tf_op jit(solution)/shard_map/ppermute | solution.py:223
  132.5 1.3 fusion.3
  133.8 11.4 %all-to-all-done.1 = bf16[64,80,128]{2,1,0:T(8,128)(2,1)S(1)} async-done(((bf16[64,80,128]{2,1,0:T(8,128)(2,1)}), bf16[64,80,128]{2,1,0:T(8,128)(2,1)S(1)}, u32[]{:S(2)}, u32[]{:S(2)}) %all-to-all-start.1) | async-done | bytes 1310752 | tf_op jit(solution)/shard_map/all_to_all | solution.py:311
  145.2 0.9 copy-done.5
  146.1 1.0 shard_map.111
  147.1 12.5 %collective-permute-start.9 = (f32[128,512]{1,0:T(8,128)S(1)}, f32[128,512]{1,0:T(8,128)S(1)}, u32[]{:S(2)}, u32[]{:S(2)}) collective-permute-start(f32[128,512]{1,0:T(8,128)S(1)} %slice.24), channel_id=1, source_target_pairs={{0,64},{64,0},{1,65},{65,1},{2,66},{66,2},{3,67},{67,3},{4,68},{68... | collective-permute-start | bytes 786440 | tf_op jit(solution)/shard_map/ppermute | solution.py:223
  159.6 1.1 collective-permute-done.9
  160.7 0.7 fusion.5
  (14 shorter events, 0.0 us)
Async XLA Ops:
  7.2 50.7 %all-gather.3.cloned.1.call-start = ((), (), s32[]{:S(2)}) async-start(), calls=%async_computation.2 | async-start | bytes 5898240 | tf_op jit(solution)/shard_map/all_gather | solution.py:254
  7.2 0.9 copy-start.6
  8.1 0.7 copy-start.7
  9.2 10.9 %collective-permute-start = (bf16[128,512]{1,0:T(8,128)(2,1)S(1)}, bf16[128,512]{1,0:T(8,128)(2,1)S(1)}, u32[]{:S(2)}, u32[]{:S(2)}) collective-permute-start(bf16[128,512]{1,0:T(8,128)(2,1)S(1)} %shard_map.105.mine_ref), channel_id=1, source_target_pairs={{0,64},{64,0},{1,65},{65,1},{2,66},{66,2},{3,67},{67,3},{4,68},{68... | collective-permute-start | bytes 393224 | tf_op jit(solution)/shard_map/ppermute | solution.py:223
  18.0 0.7 copy-start.8
  18.7 0.7 copy-start.9
  20.1 13.8 %copy-start.13 = (f32[3,1,4,8]{3,2,1,0:T(4,128)S(1)}, f32[3,1,4,8]{3,2,1,0:T(4,128)}, u32[]{:S(2)}) copy-start(f32[3,1,4,8]{3,2,1,0:T(4,128)} %param.17) | copy-start | bytes 1156
  21.9 0.7 copy-start.4
  22.6 11.6 %copy-start.10 = (bf16[1,512,1024]{2,1,0:T(8,128)(2,1)S(1)}, bf16[1,512,1024]{2,1,0:T(8,128)(2,1)}, u32[]{:S(2)}) copy-start(bf16[1,512,1024]{2,1,0:T(8,128)(2,1)} %param.15) | copy-start | bytes 3145732
  22.6 45.1 %all-to-all-start = ((bf16[64,80,128]{2,1,0:T(8,128)(2,1)}), bf16[64,80,128]{2,1,0:T(8,128)(2,1)}, u32[]{:S(2)}, u32[]{:S(2)}) async-start(bf16[64,80,128]{2,1,0:T(8,128)(2,1)} %bitcast.8), calls=%async_computation | async-start | bytes 2621440 | tf_op jit(solution)/shard_map/all_to_all | solution.py:270
  35.8 2.5 %copy-start.11 = (bf16[1,512,1024]{2,1,0:T(8,128)(2,1)S(1)}, bf16[1,512,1024]{2,1,0:T(8,128)(2,1)}, u32[]{:S(2)}) copy-start(bf16[1,512,1024]{2,1,0:T(8,128)(2,1)} %param.14) | copy-start | bytes 3145732
  35.8 26.5 %collective-permute-start.2 = (bf16[512,1024]{1,0:T(8,128)(2,1)}, bf16[512,1024]{1,0:T(8,128)(2,1)}, u32[]{:S(2)}, u32[]{:S(2)}) collective-permute-start(bf16[512,1024]{1,0:T(8,128)(2,1)} %fusion.1.um_ref), channel_id=1, source_target_pairs={{0,64},{64,0},{1,65},{65,1},{2,66},{66,2},{3,67},{67,3},{4,68},{68... | collective-permute-start | bytes 3145736 | tf_op jit(solution)/shard_map/ppermute | solution.py:223
  39.9 2.6 %copy-start.12 = (bf16[1,1024,512]{2,1,0:T(8,128)(2,1)S(1)}, bf16[1,1024,512]{2,1,0:T(8,128)(2,1)}, u32[]{:S(2)}) copy-start(bf16[1,1024,512]{2,1,0:T(8,128)(2,1)} %param.16) | copy-start | bytes 3145732
  39.9 22.3 %collective-permute-start.1 = (bf16[512,1024]{1,0:T(8,128)(2,1)}, bf16[512,1024]{1,0:T(8,128)(2,1)}, u32[]{:S(2)}, u32[]{:S(2)}) collective-permute-start(bf16[512,1024]{1,0:T(8,128)(2,1)} %fusion.2.gm_ref), channel_id=1, source_target_pairs={{0,64},{64,0},{1,65},{65,1},{2,66},{66,2},{3,67},{67,3},{4,68},{68... | collective-permute-start | bytes 3145736 | tf_op jit(solution)/shard_map/ppermute | solution.py:223
  43.9 23.8 %collective-permute-start.3 = (bf16[1024,512]{1,0:T(8,128)(2,1)}, bf16[1024,512]{1,0:T(8,128)(2,1)}, u32[]{:S(2)}, u32[]{:S(2)}) collective-permute-start(bf16[1024,512]{1,0:T(8,128)(2,1)} %fusion.mine_ref), channel_id=1, source_target_pairs={{0,64},{64,0},{1,65},{65,1},{2,66},{66,2},{3,67},{67,3},{4,68},{68... | collective-permute-start | bytes 3145736 | tf_op jit(solution)/shard_map/ppermute | solution.py:223
  71.6 13.1 %collective-permute-start.4 = (bf16[320,1024]{1,0:T(8,128)(2,1)S(1)}, bf16[320,1024]{1,0:T(8,128)(2,1)S(1)}, u32[]{:S(2)}, u32[]{:S(2)}) collective-permute-start(bf16[320,1024]{1,0:T(8,128)(2,1)S(1)} %get-tuple-element.57), channel_id=1, source_target_pairs={{0,384},{128,256},{256,128},{384,0},{1,385},{129,257},{257,129},{3... | collective-permute-start | bytes 1966088 | tf_op jit(solution)/shard_map/ppermute | solution.py:227
  76.0 11.6 %collective-permute-start.6 = (bf16[320,1024]{1,0:T(8,128)(2,1)S(1)}, bf16[320,1024]{1,0:T(8,128)(2,1)S(1)}, u32[]{:S(2)}, u32[]{:S(2)}) collective-permute-start(bf16[320,1024]{1,0:T(8,128)(2,1)S(1)} %get-tuple-element.68), channel_id=1, source_target_pairs={{0,128},{128,0},{256,384},{384,256},{1,129},{129,1},{257,385},{385... | collective-permute-start | bytes 1966088 | tf_op jit(solution)/shard_map/ppermute | solution.py:227
  84.9 18.7 %collective-permute-start.8 = (bf16[320,1024]{1,0:T(8,128)(2,1)S(1)}, bf16[320,1024]{1,0:T(8,128)(2,1)S(1)}, u32[]{:S(2)}, u32[]{:S(2)}) collective-permute-start(bf16[320,1024]{1,0:T(8,128)(2,1)S(1)} %add_convert_fusion.2.high), channel_id=1, source_target_pairs={{0,128},{128,0},{256,384},{384,256},{1,129},{129,1},{257,385},{385... | collective-permute-start | bytes 1966088 | tf_op jit(solution)/shard_map/ppermute | solution.py:227
  87.9 15.8 %collective-permute-start.7 = (bf16[320,1024]{1,0:T(8,128)(2,1)S(1)}, bf16[320,1024]{1,0:T(8,128)(2,1)S(1)}, u32[]{:S(2)}, u32[]{:S(2)}) collective-permute-start(bf16[320,1024]{1,0:T(8,128)(2,1)S(1)} %add_convert_fusion.1.low), channel_id=1, source_target_pairs={{0,384},{128,256},{256,128},{384,0},{1,385},{129,257},{257,129},{3... | collective-permute-start | bytes 1966088 | tf_op jit(solution)/shard_map/ppermute | solution.py:227
  95.5 1.3 copy-start
  96.9 1.0 copy-start.3
  109.0 1.1 copy-start.2
  110.0 22.4 %copy-start.1 = (f32[1024,512]{1,0:T(8,128)S(1)}, f32[1024,512]{1,0:T(8,128)}, u32[]{:S(2)}) copy-start(f32[1024,512]{1,0:T(8,128)} %copy-done) | copy-start | bytes 6291460
  110.0 35.1 %all-to-all-start.1 = ((bf16[64,80,128]{2,1,0:T(8,128)(2,1)}), bf16[64,80,128]{2,1,0:T(8,128)(2,1)S(1)}, u32[]{:S(2)}, u32[]{:S(2)}) async-start(bf16[64,80,128]{2,1,0:T(8,128)(2,1)} %bitcast.65), calls=%async_computation.1 | async-start | bytes 2621440 | tf_op jit(solution)/shard_map/all_to_all | solution.py:311
  119.7 12.8 %collective-permute-start.5 = (bf16[1024,512]{1,0:T(8,128)(2,1)}, bf16[1024,512]{1,0:T(8,128)(2,1)S(1)}, u32[]{:S(2)}, u32[]{:S(2)}) collective-permute-start(bf16[1024,512]{1,0:T(8,128)(2,1)} %copy-done.3), channel_id=1, source_target_pairs={{0,64},{64,0},{1,65},{65,1},{2,66},{66,2},{3,67},{67,3},{4,68},{68... | collective-permute-start | bytes 3145736 | tf_op jit(solution)/shard_map/ppermute | solution.py:223
  145.2 0.9 copy-start.5
  147.1 13.6 %collective-permute-start.9 = (f32[128,512]{1,0:T(8,128)S(1)}, f32[128,512]{1,0:T(8,128)S(1)}, u32[]{:S(2)}, u32[]{:S(2)}) collective-permute-start(f32[128,512]{1,0:T(8,128)S(1)} %slice.24), channel_id=1, source_target_pairs={{0,64},{64,0},{1,65},{65,1},{2,66},{66,2},{3,67},{67,3},{4,68},{68... | collective-permute-start | bytes 786440 | tf_op jit(solution)/shard_map/ppermute | solution.py:223
Sparse Core Ops, SparseCore 0:
  10.1 47.7 all-gather.2

commit v4 on v3

--- a/solution.py
+++ b/solution.py
@@ -269,12 +269,13 @@
     )
     incoming = lax.all_to_all(outgoing.reshape(block), EXPERT, 0, 0, tiled=True).reshape(tiles)
     scales = w_scale[:, 0]
-    down_m = dequant_matrix(w_down[0], scales[2].T)
-    down_o = swap(down_m)
     gate_m = dequant_matrix(w_gate[0], scales[0])
     up_m = dequant_matrix(w_up[0], scales[1])
     gate_o = swap(gate_m)
     up_o = swap(up_m)
+    gate_o, up_o, w_down = lax.optimization_barrier((gate_o, up_o, w_down))
+    down_m = dequant_matrix(w_down[0], scales[2].T)
+    down_o = swap(down_m)
     pre = lax.dynamic_slice_in_dim(
         pre.reshape(experts, cap, 2, hid), core[0] * slots, slots, axis=1
     )

time: 169 us -> 168 us (level)
  waiting for transfers between devices: 45.6 us -> 47.7 us
  other arithmetic: 7.06 us -> 5.31 us
    ppermute x6, waiting for transfers between devices: 3.63 us -> 6.16 us  [swap(): return lax.ppermute(value, 'core', [(0, 1), (1, 0)])]
    convert_element_type x3, other arithmetic: 4.57 us -> 2.82 us  [dequant_matrix(): (grid * scales[:, None, :, None]).reshape(rows_in, cols_in).astype(BF16)]
    unnamed x28 -> x40, local copies, waits for them, and re-layouts: 7.9 us -> 6.98 us
  transfers between devices with their start and end apart: 13 -> 13, of which waited for: 8 -> 9; matrix products, arithmetic and copies ran while one was open for 7% -> 6% of each run, Pallas kernels for 4% -> 4%
where the time goes in v4:
time: 168 us; the launch traced here: 167 us
  starting transfers between devices  71.7 us (43%)
  waiting for transfers between devices  47.7 us (28%)
  Pallas kernels  16.1 us (10%)
  between operations  14.4 us (9%)
  local copies, waits for them, and re-layouts  12.2 us (7%)
  other arithmetic  5.31 us (3%)
    ppermute x6, starting transfers between devices, swap(): return lax.ppermute(value, 'core', [(0, 1), (1, 0)])  38.7 us
    ppermute x4, waiting for transfers between devices, pair(): return lax.ppermute(value, 'x', [(i, i ^ mask) for i in range(XS)])  14 us
    ppermute x4, starting transfers between devices, pair(): return lax.ppermute(value, 'x', [(i, i ^ mask) for i in range(XS)])  12.1 us
    all_to_all x1, starting transfers between devices, shards(): lax.all_to_all(outgoing.reshape(block), EXPERT, 0, 0, tiled=True)  11.3 us
    all_to_all x1, waiting for transfers between devices, shards(): lax.all_to_all(sent.reshape(block), EXPERT, 0, 0, tiled=True).reshape(tiles)  11.1 us
    all_gather x1, waiting for transfers between devices, shards(): pre = lax.all_gather(saved_pre[0], SEQ, axis=0, tiled=True)  10.9 us
    all_to_all x1, starting transfers between devices, shards(): lax.all_to_all(sent.reshape(block), EXPERT, 0, 0, tiled=True).reshape(tiles)  9.63 us
    unnamed x40, local copies, waits for them, and re-layouts  6.98 us
  transfers between devices with their start and end apart: 13, of which 9 were waited for; matrix products, arithmetic and copies ran while one was open for 6% of the time, Pallas kernels for 4%

profile of v4, /device:TPU:1, one launch (start us, length us, event | category | flops | bytes accessed | tf_op | source)
XLA Modules:
  0.0 167.4 jit_solution(17741868228941805866)
XLA Ops:
  7.2 0.0 all-gather.3.cloned.1.call-start
  7.2 0.9 copy-done.12
  8.1 0.7 copy-done.13
  8.8 0.4 shard_map.105.mine_ref
  9.2 0.0 all-gather.3.cloned.1.call-update
  9.2 8.8 %collective-permute-start = (bf16[128,512]{1,0:T(8,128)(2,1)S(1)}, bf16[128,512]{1,0:T(8,128)(2,1)S(1)}, u32[]{:S(2)}, u32[]{:S(2)}) collective-permute-start(bf16[128,512]{1,0:T(8,128)(2,1)S(1)} %shard_map.105.mine_ref), channel_id=1, source_target_pairs={{0,64},{64,0},{1,65},{65,1},{2,66},{66,2},{3,67},{67,3},{4,68},{68... | collective-permute-start | bytes 393224 | tf_op jit(solution)/shard_map/ppermute | solution.py:223
  18.0 0.0 copy-start.14
  18.1 0.7 copy-done.14
  18.7 0.7 copy-done.15
  19.4 0.7 shard_map.104
  20.1 0.0 collective-permute-done.other_ref
  20.1 0.0 copy-start.19
  20.1 1.8 %shard_map.106 = bf16[640,8,128]{2,1,0:T(8,128)(2,1)} custom-call(bf16[640,128]{1,0:T(8,128)(2,1)S(1)} %get-tuple-element.42.pick_ref, f32[640,128]{1,0:T(8,128)S(1)} %get-tuple-element.43.gate_ref, bf16[128,512]{1,0:T(8,128)(2,1)S(1)} %shard_map.105.mine_ref, bf16[128,512]{1,0:T(8,128)(2,1)S(1)} %collective-permute-done.other_ref), custom_call_target="tpu_custom_call" | custom-call | flops 167772160 | bytes 2097152 | tf_op jit(solution)/shard_map/pallas_call | solution.py:261
  22.0 0.7 copy-done.10
  22.6 11.3 %all-to-all-start = ((bf16[64,80,128]{2,1,0:T(8,128)(2,1)}), bf16[64,80,128]{2,1,0:T(8,128)(2,1)}, u32[]{:S(2)}, u32[]{:S(2)}) async-start(bf16[64,80,128]{2,1,0:T(8,128)(2,1)} %bitcast.8), calls=%async_computation | async-start | bytes 2621440 | tf_op jit(solution)/shard_map/all_to_all | solution.py:270
  33.9 0.2 mul.46
  34.1 0.0 copy-done.16
  34.2 0.7 fusion.1.um_ref
  34.9 0.0 copy-start.3
  34.9 0.0 copy-start.17
  34.9 2.3 %collective-permute-start.2 = (bf16[512,1024]{1,0:T(8,128)(2,1)S(1)}, bf16[512,1024]{1,0:T(8,128)(2,1)S(1)}, u32[]{:S(2)}, u32[]{:S(2)}) collective-permute-start(bf16[512,1024]{1,0:T(8,128)(2,1)S(1)} %fusion.1.um_ref), channel_id=1, source_target_pairs={{0,64},{64,0},{1,65},{65,1},{2,66},{66,2},{3,67},{67,3},{4,68},{68... | collective-permute-start | bytes 3145736 | tf_op jit(solution)/shard_map/ppermute | solution.py:223
  37.2 0.2 mul.42
  37.4 0.7 fusion.2.gm_ref
  38.2 2.1 %collective-permute-start.1 = (bf16[512,1024]{1,0:T(8,128)(2,1)S(1)}, bf16[512,1024]{1,0:T(8,128)(2,1)}, u32[]{:S(2)}, u32[]{:S(2)}) collective-permute-start(bf16[512,1024]{1,0:T(8,128)(2,1)S(1)} %fusion.2.gm_ref), channel_id=1, source_target_pairs={{0,64},{64,0},{1,65},{65,1},{2,66},{66,2},{3,67},{67,3},{4,68},{68... | collective-permute-start | bytes 3145736 | tf_op jit(solution)/shard_map/ppermute | solution.py:223
  40.3 0.1 copy.21
  40.4 0.0 collective-permute-done.2.uo_ref
  40.4 2.5 %collective-permute-done.1.go_ref = bf16[512,1024]{1,0:T(8,128)(2,1)} collective-permute-done((bf16[512,1024]{1,0:T(8,128)(2,1)S(1)}, bf16[512,1024]{1,0:T(8,128)(2,1)}, u32[]{:S(2)}, u32[]{:S(2)}) %collective-permute-start.1) | collective-permute-done | bytes 1048608 | tf_op jit(solution)/shard_map/ppermute | solution.py:223
  43.0 0.3 mul.49
  43.3 1.4 fusion.mine_ref
  44.7 2.3 %collective-permute-start.3 = (bf16[1024,512]{1,0:T(8,128)(2,1)}, bf16[1024,512]{1,0:T(8,128)(2,1)}, u32[]{:S(2)}, u32[]{:S(2)}) collective-permute-start(bf16[1024,512]{1,0:T(8,128)(2,1)} %fusion.mine_ref), channel_id=1, source_target_pairs={{0,64},{64,0},{1,65},{65,1},{2,66},{66,2},{3,67},{67,3},{4,68},{68... | collective-permute-start | bytes 3145736 | tf_op jit(solution)/shard_map/ppermute | solution.py:223
  47.0 10.9 %all-gather.3.cloned.1.call-done = bf16[1,1280,2,1024]{3,2,0,1:T(2,128)(2,1)} async-done(((bf16[1,160,2,1024]{3,2,0,1:T(2,128)(2,1)}), bf16[1,1280,2,1024]{3,2,0,1:T(2,128)(2,1)}) %all-gather.3.cloned.1.call-update) | async-done | bytes 5242896 | tf_op jit(solution)/shard_map/all_gather | solution.py:254
  57.9 3.5 %constant_dynamic-slice_fusion = bf16[64,10,2,1024]{3,2,1,0:T(2,128)(2,1)S(1)} fusion(bf16[64,20,2,1024]{3,2,1,0:T(2,128)(2,1)} %bitcast.74, s32[]{:T(128)S(6)} %select_n.3), kind=kLoop, calls=%fused_computation.17 | loop fusion | bytes 5242884 | tf_op jit(solution)/shard_map/dynamic_slice | solution.py:279
  61.4 0.8 copy.29
  62.2 5.5 %all-to-all-done = bf16[64,80,128]{2,1,0:T(8,128)(2,1)} async-done(((bf16[64,80,128]{2,1,0:T(8,128)(2,1)}), bf16[64,80,128]{2,1,0:T(8,128)(2,1)}, u32[]{:S(2)}, u32[]{:S(2)}) %all-to-all-start) | async-done | bytes 1310752 | tf_op jit(solution)/shard_map/all_to_all | solution.py:270
  67.8 0.0 collective-permute-done.3.other_ref
  67.8 3.6 %shard_map.107 = (bf16[640,1024]{1,0:T(8,128)(2,1)S(1)}, bf16[320,1024]{1,0:T(8,128)(2,1)S(1)}, bf16[320,1024]{1,0:T(8,128)(2,1)S(1)}) custom-call(bf16[640,8,128]{2,1,0:T(8,128)(2,1)} %bitcast.9.tile_ref, bf16[1024,512]{1,0:T(8,128)(2,1)} %fusion.mine_ref, bf16[1024,512]{1,0:T(8,128)(2,1)} %collective-permute-done.3.other_ref), custom_call_target="tpu_custom_call" | custom-call | flops 1342177280 | bytes 4194304 | tf_op jit(solution)/shard_map/pallas_call | solution.py:286
  71.4 0.2 shard_map.108
  71.6 4.4 %collective-permute-start.4 = (bf16[320,1024]{1,0:T(8,128)(2,1)S(1)}, bf16[320,1024]{1,0:T(8,128)(2,1)S(1)}, u32[]{:S(2)}, u32[]{:S(2)}) collective-permute-start(bf16[320,1024]{1,0:T(8,128)(2,1)S(1)} %get-tuple-element.63), channel_id=1, source_target_pairs={{0,384},{128,256},{256,128},{384,0},{1,385},{129,257},{257,129},{3... | collective-permute-start | bytes 1966088 | tf_op jit(solution)/shard_map/ppermute | solution.py:227
  76.0 1.9 %collective-permute-start.6 = (bf16[320,1024]{1,0:T(8,128)(2,1)S(1)}, bf16[320,1024]{1,0:T(8,128)(2,1)S(1)}, u32[]{:S(2)}, u32[]{:S(2)}) collective-permute-start(bf16[320,1024]{1,0:T(8,128)(2,1)S(1)} %get-tuple-element.74), channel_id=1, source_target_pairs={{0,128},{128,0},{256,384},{384,256},{1,129},{129,1},{257,385},{385... | collective-permute-start | bytes 1966088 | tf_op jit(solution)/shard_map/ppermute | solution.py:227
  78.0 6.8 %collective-permute-done.4 = bf16[320,1024]{1,0:T(8,128)(2,1)S(1)} collective-permute-done((bf16[320,1024]{1,0:T(8,128)(2,1)S(1)}, bf16[320,1024]{1,0:T(8,128)(2,1)S(1)}, u32[]{:S(2)}, u32[]{:S(2)}) %collective-permute-start.4) | collective-permute-done | bytes 655392 | tf_op jit(solution)/shard_map/ppermute | solution.py:227
  84.7 0.2 add_convert_fusion.2.high
  85.0 1.9 %collective-permute-start.8 = (bf16[320,1024]{1,0:T(8,128)(2,1)S(1)}, bf16[320,1024]{1,0:T(8,128)(2,1)S(1)}, u32[]{:S(2)}, u32[]{:S(2)}) collective-permute-start(bf16[320,1024]{1,0:T(8,128)(2,1)S(1)} %add_convert_fusion.2.high), channel_id=1, source_target_pairs={{0,128},{128,0},{256,384},{384,256},{1,129},{129,1},{257,385},{385... | collective-permute-start | bytes 1966088 | tf_op jit(solution)/shard_map/ppermute | solution.py:227
  86.9 0.7 collective-permute-done.6
  87.7 0.2 add_convert_fusion.1.low
  87.9 0.0 copy-start.4
  87.9 0.0 copy-start.6
  87.9 0.0 copy-start.9
  87.9 3.9 %collective-permute-start.7 = (bf16[320,1024]{1,0:T(8,128)(2,1)S(1)}, bf16[320,1024]{1,0:T(8,128)(2,1)S(1)}, u32[]{:S(2)}, u32[]{:S(2)}) collective-permute-start(bf16[320,1024]{1,0:T(8,128)(2,1)S(1)} %add_convert_fusion.1.low), channel_id=1, source_target_pairs={{0,384},{128,256},{256,128},{384,0},{1,385},{129,257},{257,129},{3... | collective-permute-start | bytes 1966088 | tf_op jit(solution)/shard_map/ppermute | solution.py:227
  91.9 4.0 %shard_map.109 = (bf16[640,1024]{1,0:T(8,128)(2,1)S(1)}, bf16[640,1024]{1,0:T(8,128)(2,1)S(1)}, f32[1024,512]{1,0:T(8,128)S(1)}, bf16[1024,512]{1,0:T(8,128)(2,1)S(1)}) custom-call(s32[1]{0:T(128)} %bitcast.core_ref, bf16[2,640,1024]{2,1,0:T(8,128)(2,1)S(1)} %bitcast.63, ...), custom_call_target="tpu_custom_call", output_to_operand_aliasing={{0}: (3, {}), {1}: (4, {}), {2}: (5, {}), {3}: (6, {})} | custom-call | flops 1342177280 | bytes 11534336 | tf_op jit(solution)/shard_map/pallas_call | solution.py:165
  95.9 1.3 copy-done
  97.2 6.5 %collective-permute-done.8.high_in = bf16[320,1024]{1,0:T(8,128)(2,1)S(1)} collective-permute-done((bf16[320,1024]{1,0:T(8,128)(2,1)S(1)}, bf16[320,1024]{1,0:T(8,128)(2,1)S(1)}, u32[]{:S(2)}, u32[]{:S(2)}) %collective-permute-start.8) | collective-permute-done | bytes 655392 | tf_op jit(solution)/shard_map/ppermute | solution.py:227
  103.7 0.0 collective-permute-done.7.low_in
  103.7 4.4 %shard_map.110 = bf16[640,8,128]{2,1,0:T(8,128)(2,1)S(1)} custom-call(bf16[320,1024]{1,0:T(8,128)(2,1)S(1)} %add_convert_fusion.1.low, bf16[320,1024]{1,0:T(8,128)(2,1)S(1)} %collective-permute-done.7.low_in, bf16[320,1024]{1,0:T(8,128)(2,1)S(1)} %add_convert_fusion.2.high, bf16[320,1024]{1,0:T(8,128)(2,1)S(1)} %collective-permute-done.8.high_in, ...), custom_call_target="tpu_custom_call" | custom-call | flops 2684354560 | bytes 6291456 | tf_op jit(solution)/shard_map/pallas_call | solution.py:299
  108.1 1.1 copy-done.2
  109.2 9.6 %all-to-all-start.1 = ((bf16[64,80,128]{2,1,0:T(8,128)(2,1)}), bf16[64,80,128]{2,1,0:T(8,128)(2,1)S(1)}, u32[]{:S(2)}, u32[]{:S(2)}) async-start(bf16[64,80,128]{2,1,0:T(8,128)(2,1)} %bitcast.65), calls=%async_computation.1 | async-start | bytes 2621440 | tf_op jit(solution)/shard_map/all_to_all | solution.py:312
  118.8 10.6 %collective-permute-start.5 = (bf16[1024,512]{1,0:T(8,128)(2,1)}, bf16[1024,512]{1,0:T(8,128)(2,1)S(1)}, u32[]{:S(2)}, u32[]{:S(2)}) collective-permute-start(bf16[1024,512]{1,0:T(8,128)(2,1)} %copy-done.7), channel_id=1, source_target_pairs={{0,64},{64,0},{1,65},{65,1},{2,66},{66,2},{3,67},{67,3},{4,68},{68... | collective-permute-start | bytes 3145736 | tf_op jit(solution)/shard_map/ppermute | solution.py:223
  129.4 2.5 %collective-permute-done.5 = bf16[1024,512]{1,0:T(8,128)(2,1)S(1)} collective-permute-done((bf16[1024,512]{1,0:T(8,128)(2,1)}, bf16[1024,512]{1,0:T(8,128)(2,1)S(1)}, u32[]{:S(2)}, u32[]{:S(2)}) %collective-permute-start.5) | collective-permute-done | bytes 1048608 | tf_op jit(solution)/shard_map/ppermute | solution.py:223
  131.9 1.3 fusion.3
  133.2 11.1 %all-to-all-done.1 = bf16[64,80,128]{2,1,0:T(8,128)(2,1)S(1)} async-done(((bf16[64,80,128]{2,1,0:T(8,128)(2,1)}), bf16[64,80,128]{2,1,0:T(8,128)(2,1)S(1)}, u32[]{:S(2)}, u32[]{:S(2)}) %all-to-all-start.1) | async-done | bytes 1310752 | tf_op jit(solution)/shard_map/all_to_all | solution.py:312
  144.3 0.9 copy-done.11
  145.2 1.0 shard_map.111
  146.2 12.5 %collective-permute-start.9 = (f32[128,512]{1,0:T(8,128)S(1)}, f32[128,512]{1,0:T(8,128)S(1)}, u32[]{:S(2)}, u32[]{:S(2)}) collective-permute-start(f32[128,512]{1,0:T(8,128)S(1)} %slice.24), channel_id=1, source_target_pairs={{0,64},{64,0},{1,65},{65,1},{2,66},{66,2},{3,67},{67,3},{4,68},{68... | collective-permute-start | bytes 786440 | tf_op jit(solution)/shard_map/ppermute | solution.py:223
  158.8 1.1 collective-permute-done.9
  159.9 0.7 fusion.5
  (26 shorter events, 0.1 us)
Async XLA Ops:
  7.2 50.7 %all-gather.3.cloned.1.call-start = ((), (), s32[]{:S(2)}) async-start(), calls=%async_computation.2 | async-start | bytes 5898240 | tf_op jit(solution)/shard_map/all_gather | solution.py:254
  7.2 0.9 copy-start.12
  8.1 0.7 copy-start.13
  9.2 10.9 %collective-permute-start = (bf16[128,512]{1,0:T(8,128)(2,1)S(1)}, bf16[128,512]{1,0:T(8,128)(2,1)S(1)}, u32[]{:S(2)}, u32[]{:S(2)}) collective-permute-start(bf16[128,512]{1,0:T(8,128)(2,1)S(1)} %shard_map.105.mine_ref), channel_id=1, source_target_pairs={{0,64},{64,0},{1,65},{65,1},{2,66},{66,2},{3,67},{67,3},{4,68},{68... | collective-permute-start | bytes 393224 | tf_op jit(solution)/shard_map/ppermute | solution.py:223
  18.0 0.7 copy-start.14
  18.7 0.7 copy-start.15
  20.1 13.8 %copy-start.19 = (f32[3,1,4,8]{3,2,1,0:T(4,128)S(1)}, f32[3,1,4,8]{3,2,1,0:T(4,128)}, u32[]{:S(2)}) copy-start(f32[3,1,4,8]{3,2,1,0:T(4,128)} %param.17) | copy-start | bytes 1156
  22.0 0.7 copy-start.10
  22.6 11.5 %copy-start.16 = (bf16[1,512,1024]{2,1,0:T(8,128)(2,1)S(1)}, bf16[1,512,1024]{2,1,0:T(8,128)(2,1)}, u32[]{:S(2)}) copy-start(bf16[1,512,1024]{2,1,0:T(8,128)(2,1)} %param.15) | copy-start | bytes 3145732
  22.6 45.1 %all-to-all-start = ((bf16[64,80,128]{2,1,0:T(8,128)(2,1)}), bf16[64,80,128]{2,1,0:T(8,128)(2,1)}, u32[]{:S(2)}, u32[]{:S(2)}) async-start(bf16[64,80,128]{2,1,0:T(8,128)(2,1)} %bitcast.8), calls=%async_computation | async-start | bytes 2621440 | tf_op jit(solution)/shard_map/all_to_all | solution.py:270
  34.9 3.3 %copy-start.3 = (bf16[512,1024]{1,0:T(8,128)(2,1)}, bf16[512,1024]{1,0:T(8,128)(2,1)S(1)}, u32[]{:S(2)}) copy-start(bf16[512,1024]{1,0:T(8,128)(2,1)S(1)} %fusion.1.um_ref) | copy-start | bytes 3145732
  34.9 2.6 %copy-start.17 = (bf16[1,512,1024]{2,1,0:T(8,128)(2,1)S(1)}, bf16[1,512,1024]{2,1,0:T(8,128)(2,1)}, u32[]{:S(2)}) copy-start(bf16[1,512,1024]{2,1,0:T(8,128)(2,1)} %param.14) | copy-start | bytes 3145732
  34.9 5.5 %collective-permute-start.2 = (bf16[512,1024]{1,0:T(8,128)(2,1)S(1)}, bf16[512,1024]{1,0:T(8,128)(2,1)S(1)}, u32[]{:S(2)}, u32[]{:S(2)}) collective-permute-start(bf16[512,1024]{1,0:T(8,128)(2,1)S(1)} %fusion.1.um_ref), channel_id=1, source_target_pairs={{0,64},{64,0},{1,65},{65,1},{2,66},{66,2},{3,67},{67,3},{4,68},{68... | collective-permute-start | bytes 3145736 | tf_op jit(solution)/shard_map/ppermute | solution.py:223
  38.2 6.5 %copy-start.5 = (bf16[512,1024]{1,0:T(8,128)(2,1)}, bf16[512,1024]{1,0:T(8,128)(2,1)S(1)}, u32[]{:S(2)}) copy-start(bf16[512,1024]{1,0:T(8,128)(2,1)S(1)} %fusion.2.gm_ref) | copy-start | bytes 3145732
  38.2 4.8 %collective-permute-start.1 = (bf16[512,1024]{1,0:T(8,128)(2,1)S(1)}, bf16[512,1024]{1,0:T(8,128)(2,1)}, u32[]{:S(2)}, u32[]{:S(2)}) collective-permute-start(bf16[512,1024]{1,0:T(8,128)(2,1)S(1)} %fusion.2.gm_ref), channel_id=1, source_target_pairs={{0,64},{64,0},{1,65},{65,1},{2,66},{66,2},{3,67},{67,3},{4,68},{68... | collective-permute-start | bytes 3145736 | tf_op jit(solution)/shard_map/ppermute | solution.py:223
  40.4 2.9 %copy-start.18 = (bf16[1,1024,512]{2,1,0:T(8,128)(2,1)S(1)}, bf16[1,1024,512]{2,1,0:T(8,128)(2,1)}, u32[]{:S(2)}) copy-start(bf16[1,1024,512]{2,1,0:T(8,128)(2,1)} %param.16) | copy-start | bytes 3145732
  40.4 4.3 %copy-start.8 = (bf16[512,1024]{1,0:T(8,128)(2,1)}, bf16[512,1024]{1,0:T(8,128)(2,1)S(1)}, u32[]{:S(2)}) copy-start(bf16[512,1024]{1,0:T(8,128)(2,1)S(1)} %collective-permute-done.2.uo_ref) | copy-start | bytes 3145732
  44.7 23.1 %collective-permute-start.3 = (bf16[1024,512]{1,0:T(8,128)(2,1)}, bf16[1024,512]{1,0:T(8,128)(2,1)}, u32[]{:S(2)}, u32[]{:S(2)}) collective-permute-start(bf16[1024,512]{1,0:T(8,128)(2,1)} %fusion.mine_ref), channel_id=1, source_target_pairs={{0,64},{64,0},{1,65},{65,1},{2,66},{66,2},{3,67},{67,3},{4,68},{68... | collective-permute-start | bytes 3145736 | tf_op jit(solution)/shard_map/ppermute | solution.py:223
  71.6 13.1 %collective-permute-start.4 = (bf16[320,1024]{1,0:T(8,128)(2,1)S(1)}, bf16[320,1024]{1,0:T(8,128)(2,1)S(1)}, u32[]{:S(2)}, u32[]{:S(2)}) collective-permute-start(bf16[320,1024]{1,0:T(8,128)(2,1)S(1)} %get-tuple-element.63), channel_id=1, source_target_pairs={{0,384},{128,256},{256,128},{384,0},{1,385},{129,257},{257,129},{3... | collective-permute-start | bytes 1966088 | tf_op jit(solution)/shard_map/ppermute | solution.py:227
  76.0 11.6 %collective-permute-start.6 = (bf16[320,1024]{1,0:T(8,128)(2,1)S(1)}, bf16[320,1024]{1,0:T(8,128)(2,1)S(1)}, u32[]{:S(2)}, u32[]{:S(2)}) collective-permute-start(bf16[320,1024]{1,0:T(8,128)(2,1)S(1)} %get-tuple-element.74), channel_id=1, source_target_pairs={{0,128},{128,0},{256,384},{384,256},{1,129},{129,1},{257,385},{385... | collective-permute-start | bytes 1966088 | tf_op jit(solution)/shard_map/ppermute | solution.py:227
  85.0 18.7 %collective-permute-start.8 = (bf16[320,1024]{1,0:T(8,128)(2,1)S(1)}, bf16[320,1024]{1,0:T(8,128)(2,1)S(1)}, u32[]{:S(2)}, u32[]{:S(2)}) collective-permute-start(bf16[320,1024]{1,0:T(8,128)(2,1)S(1)} %add_convert_fusion.2.high), channel_id=1, source_target_pairs={{0,128},{128,0},{256,384},{384,256},{1,129},{129,1},{257,385},{385... | collective-permute-start | bytes 1966088 | tf_op jit(solution)/shard_map/ppermute | solution.py:227
  87.9 15.8 %copy-start.4 = (bf16[512,1024]{1,0:T(8,128)(2,1)S(1)}, bf16[512,1024]{1,0:T(8,128)(2,1)}, u32[]{:S(2)}) copy-start(bf16[512,1024]{1,0:T(8,128)(2,1)} %copy-done.3) | copy-start | bytes 3145732
  87.9 15.8 %copy-start.6 = (bf16[512,1024]{1,0:T(8,128)(2,1)S(1)}, bf16[512,1024]{1,0:T(8,128)(2,1)}, u32[]{:S(2)}) copy-start(bf16[512,1024]{1,0:T(8,128)(2,1)} %copy-done.5) | copy-start | bytes 3145732
  87.9 15.8 %copy-start.9 = (bf16[512,1024]{1,0:T(8,128)(2,1)S(1)}, bf16[512,1024]{1,0:T(8,128)(2,1)}, u32[]{:S(2)}) copy-start(bf16[512,1024]{1,0:T(8,128)(2,1)} %copy-done.8) | copy-start | bytes 3145732
  87.9 15.8 %collective-permute-start.7 = (bf16[320,1024]{1,0:T(8,128)(2,1)S(1)}, bf16[320,1024]{1,0:T(8,128)(2,1)S(1)}, u32[]{:S(2)}, u32[]{:S(2)}) collective-permute-start(bf16[320,1024]{1,0:T(8,128)(2,1)S(1)} %add_convert_fusion.1.low), channel_id=1, source_target_pairs={{0,384},{128,256},{256,128},{384,0},{1,385},{129,257},{257,129},{3... | collective-permute-start | bytes 1966088 | tf_op jit(solution)/shard_map/ppermute | solution.py:227
  95.9 1.4 copy-start
  97.2 10.9 %copy-start.7 = (bf16[1024,512]{1,0:T(8,128)(2,1)}, bf16[1024,512]{1,0:T(8,128)(2,1)S(1)}, u32[]{:S(2)}) copy-start(bf16[1024,512]{1,0:T(8,128)(2,1)S(1)} %get-tuple-element.73) | copy-start | bytes 3145732
  108.1 1.1 copy-start.2
  109.2 22.7 %copy-start.1 = (f32[1024,512]{1,0:T(8,128)S(1)}, f32[1024,512]{1,0:T(8,128)}, u32[]{:S(2)}) copy-start(f32[1024,512]{1,0:T(8,128)} %copy-done) | copy-start | bytes 6291460
  109.2 35.1 %all-to-all-start.1 = ((bf16[64,80,128]{2,1,0:T(8,128)(2,1)}), bf16[64,80,128]{2,1,0:T(8,128)(2,1)S(1)}, u32[]{:S(2)}, u32[]{:S(2)}) async-start(bf16[64,80,128]{2,1,0:T(8,128)(2,1)} %bitcast.65), calls=%async_computation.1 | async-start | bytes 2621440 | tf_op jit(solution)/shard_map/all_to_all | solution.py:312
  118.8 13.1 %collective-permute-start.5 = (bf16[1024,512]{1,0:T(8,128)(2,1)}, bf16[1024,512]{1,0:T(8,128)(2,1)S(1)}, u32[]{:S(2)}, u32[]{:S(2)}) collective-permute-start(bf16[1024,512]{1,0:T(8,128)(2,1)} %copy-done.7), channel_id=1, source_target_pairs={{0,64},{64,0},{1,65},{65,1},{2,66},{66,2},{3,67},{67,3},{4,68},{68... | collective-permute-start | bytes 3145736 | tf_op jit(solution)/shard_map/ppermute | solution.py:223
  144.3 0.9 copy-start.11
  146.2 13.7 %collective-permute-start.9 = (f32[128,512]{1,0:T(8,128)S(1)}, f32[128,512]{1,0:T(8,128)S(1)}, u32[]{:S(2)}, u32[]{:S(2)}) collective-permute-start(f32[128,512]{1,0:T(8,128)S(1)} %slice.24), channel_id=1, source_target_pairs={{0,64},{64,0},{1,65},{65,1},{2,66},{66,2},{3,67},{67,3},{4,68},{68... | collective-permute-start | bytes 786440 | tf_op jit(solution)/shard_map/ppermute | solution.py:223
Sparse Core Ops, SparseCore 0:
  10.1 47.7 all-gather.2

commit v5 on v4

--- a/solution.py
+++ b/solution.py
@@ -214,9 +214,12 @@
     out_ref[...] = tile_s[...].reshape(out_ref.shape).astype(BF16)
 
 
-def combine_body(pick_ref, tile_ref, out_ref, rows_s, tile_s):
+def combine_body(pick_ref, tile_ref, mine_ref, other_ref, rows_s, tile_s):
+    cols = mine_ref.shape[1]
     untile_rows(tile_ref, tile_s, rows_s)
-    out_ref[...] = lax.dot_general(pick_ref[...], rows_s[...], TN, preferred_element_type=F32)
+    total = lax.dot_general(pick_ref[...], rows_s[...], TN, preferred_element_type=F32)
+    mine_ref[...] = total[:, :cols]
+    other_ref[...] = total[:, cols:].astype(BF16)
 
 
 def swap(value):
@@ -315,13 +318,13 @@
     down_grad = down_grad.astype(BF16)[None]
     down_grad, returned = lax.optimization_barrier((down_grad, returned))
 
-    combined = vmem_call(
+    combined, leaving = vmem_call(
         combine_body,
-        shape((tokens, width), F32),
+        (shape((tokens, cols), F32), shape((tokens, cols))),
         0, 2, 2 * rows * tokens * width, 2 << 20,
         scratch=(pltpu.VMEM((rows, width), BF16), pltpu.VMEM((rows * per, LANES), F32)),
     )(pick, returned)
-    input_grad = combined[:, :cols] + swap(combined[:, cols:])
+    input_grad = combined + swap(leaving).astype(F32)
     return (input_grad.astype(BF16)[None], down_grad)
 
 

time: 168 us -> 168 us (level)
  no operation moved by 1% of the time
where the time goes in v5:
time: 168 us; the launch traced here: 167 us
  starting transfers between devices  71.7 us (43%)
  waiting for transfers between devices  47.5 us (28%)
  Pallas kernels  16.1 us (10%)
  between operations  14.4 us (9%)
  local copies, waits for them, and re-layouts  12.1 us (7%)
  other arithmetic  5.3 us (3%)
    ppermute x6, starting transfers between devices, swap(): return lax.ppermute(value, 'core', [(0, 1), (1, 0)])  38.7 us
    ppermute x4, waiting for transfers between devices, pair(): return lax.ppermute(value, 'x', [(i, i ^ mask) for i in range(XS)])  14 us
    ppermute x4, starting transfers between devices, pair(): return lax.ppermute(value, 'x', [(i, i ^ mask) for i in range(XS)])  12.1 us
    all_to_all x1, starting transfers between devices, shards(): lax.all_to_all(outgoing.reshape(block), EXPERT, 0, 0, tiled=True)  11.3 us
    all_to_all x1, waiting for transfers between devices, shards(): lax.all_to_all(sent.reshape(block), EXPERT, 0, 0, tiled=True).reshape(tiles)  11.1 us
    all_gather x1, waiting for transfers between devices, shards(): pre = lax.all_gather(saved_pre[0], SEQ, axis=0, tiled=True)  10.9 us
    all_to_all x1, starting transfers between devices, shards(): lax.all_to_all(sent.reshape(block), EXPERT, 0, 0, tiled=True).reshape(tiles)  9.62 us
    unnamed x40, local copies, waits for them, and re-layouts  6.99 us
  transfers between devices with their start and end apart: 13, of which 9 were waited for; matrix products, arithmetic and copies ran while one was open for 6% of the time, Pallas kernels for 4%

profile of v5, /device:TPU:1, one launch (start us, length us, event | category | flops | bytes accessed | tf_op | source)
XLA Modules:
  0.0 167.2 jit_solution(11359422158428902651)
XLA Ops:
  7.2 0.0 all-gather.3.cloned.1.call-start
  7.2 0.9 copy-done.12
  8.1 0.7 copy-done.13
  8.8 0.4 shard_map.105.mine_ref
  9.2 0.0 all-gather.3.cloned.1.call-update
  9.2 8.8 %collective-permute-start = (bf16[128,512]{1,0:T(8,128)(2,1)S(1)}, bf16[128,512]{1,0:T(8,128)(2,1)S(1)}, u32[]{:S(2)}, u32[]{:S(2)}) collective-permute-start(bf16[128,512]{1,0:T(8,128)(2,1)S(1)} %shard_map.105.mine_ref), channel_id=1, source_target_pairs={{0,64},{64,0},{1,65},{65,1},{2,66},{66,2},{3,67},{67,3},{4,68},{68... | collective-permute-start | bytes 393224 | tf_op jit(solution)/shard_map/ppermute | solution.py:226
  18.0 0.0 copy-start.14
  18.1 0.7 copy-done.14
  18.7 0.7 copy-done.15
  19.4 0.7 shard_map.104
  20.1 0.0 collective-permute-done.other_ref
  20.1 0.0 copy-start.19
  20.1 1.8 %shard_map.106 = bf16[640,8,128]{2,1,0:T(8,128)(2,1)} custom-call(bf16[640,128]{1,0:T(8,128)(2,1)S(1)} %get-tuple-element.44.pick_ref, f32[640,128]{1,0:T(8,128)S(1)} %get-tuple-element.45.gate_ref, bf16[128,512]{1,0:T(8,128)(2,1)S(1)} %shard_map.105.mine_ref, bf16[128,512]{1,0:T(8,128)(2,1)S(1)} %collective-permute-done.other_ref), custom_call_target="tpu_custom_call" | custom-call | flops 167772160 | bytes 2097152 | tf_op jit(solution)/shard_map/pallas_call | solution.py:264
  22.0 0.7 copy-done.10
  22.6 11.3 %all-to-all-start = ((bf16[64,80,128]{2,1,0:T(8,128)(2,1)}), bf16[64,80,128]{2,1,0:T(8,128)(2,1)}, u32[]{:S(2)}, u32[]{:S(2)}) async-start(bf16[64,80,128]{2,1,0:T(8,128)(2,1)} %bitcast.8), calls=%async_computation | async-start | bytes 2621440 | tf_op jit(solution)/shard_map/all_to_all | solution.py:273
  33.9 0.2 mul.46
  34.1 0.0 copy-done.16
  34.2 0.7 fusion.1.um_ref
  34.9 0.0 copy-start.17
  34.9 2.3 %collective-permute-start.2 = (bf16[512,1024]{1,0:T(8,128)(2,1)S(1)}, bf16[512,1024]{1,0:T(8,128)(2,1)S(1)}, u32[]{:S(2)}, u32[]{:S(2)}) collective-permute-start(bf16[512,1024]{1,0:T(8,128)(2,1)S(1)} %fusion.1.um_ref), channel_id=1, source_target_pairs={{0,64},{64,0},{1,65},{65,1},{2,66},{66,2},{3,67},{67,3},{4,68},{68... | collective-permute-start | bytes 3145736 | tf_op jit(solution)/shard_map/ppermute | solution.py:226
  37.2 0.2 mul.42
  37.4 0.7 fusion.2.gm_ref
  38.2 2.1 %collective-permute-start.1 = (bf16[512,1024]{1,0:T(8,128)(2,1)S(1)}, bf16[512,1024]{1,0:T(8,128)(2,1)}, u32[]{:S(2)}, u32[]{:S(2)}) collective-permute-start(bf16[512,1024]{1,0:T(8,128)(2,1)S(1)} %fusion.2.gm_ref), channel_id=1, source_target_pairs={{0,64},{64,0},{1,65},{65,1},{2,66},{66,2},{3,67},{67,3},{4,68},{68... | collective-permute-start | bytes 3145736 | tf_op jit(solution)/shard_map/ppermute | solution.py:226
  40.3 0.1 copy.21
  40.4 0.0 collective-permute-done.2.uo_ref
  40.4 2.5 %collective-permute-done.1.go_ref = bf16[512,1024]{1,0:T(8,128)(2,1)} collective-permute-done((bf16[512,1024]{1,0:T(8,128)(2,1)S(1)}, bf16[512,1024]{1,0:T(8,128)(2,1)}, u32[]{:S(2)}, u32[]{:S(2)}) %collective-permute-start.1) | collective-permute-done | bytes 1048608 | tf_op jit(solution)/shard_map/ppermute | solution.py:226
  43.0 0.3 mul.49
  43.3 1.4 fusion.mine_ref
  44.7 2.3 %collective-permute-start.3 = (bf16[1024,512]{1,0:T(8,128)(2,1)}, bf16[1024,512]{1,0:T(8,128)(2,1)}, u32[]{:S(2)}, u32[]{:S(2)}) collective-permute-start(bf16[1024,512]{1,0:T(8,128)(2,1)} %fusion.mine_ref), channel_id=1, source_target_pairs={{0,64},{64,0},{1,65},{65,1},{2,66},{66,2},{3,67},{67,3},{4,68},{68... | collective-permute-start | bytes 3145736 | tf_op jit(solution)/shard_map/ppermute | solution.py:226
  47.0 10.9 %all-gather.3.cloned.1.call-done = bf16[1,1280,2,1024]{3,2,0,1:T(2,128)(2,1)} async-done(((bf16[1,160,2,1024]{3,2,0,1:T(2,128)(2,1)}), bf16[1,1280,2,1024]{3,2,0,1:T(2,128)(2,1)}) %all-gather.3.cloned.1.call-update) | async-done | bytes 5242896 | tf_op jit(solution)/shard_map/all_gather | solution.py:257
  57.9 3.5 %constant_dynamic-slice_fusion = bf16[64,10,2,1024]{3,2,1,0:T(2,128)(2,1)S(1)} fusion(bf16[64,20,2,1024]{3,2,1,0:T(2,128)(2,1)} %bitcast.74, s32[]{:T(128)S(6)} %select_n.3), kind=kLoop, calls=%fused_computation.16 | loop fusion | bytes 5242884 | tf_op jit(solution)/shard_map/dynamic_slice | solution.py:282
  61.4 0.8 copy.29
  62.2 5.5 %all-to-all-done = bf16[64,80,128]{2,1,0:T(8,128)(2,1)} async-done(((bf16[64,80,128]{2,1,0:T(8,128)(2,1)}), bf16[64,80,128]{2,1,0:T(8,128)(2,1)}, u32[]{:S(2)}, u32[]{:S(2)}) %all-to-all-start) | async-done | bytes 1310752 | tf_op jit(solution)/shard_map/all_to_all | solution.py:273
  67.8 0.0 collective-permute-done.3.other_ref
  67.8 3.6 %shard_map.107 = (bf16[640,1024]{1,0:T(8,128)(2,1)S(1)}, bf16[320,1024]{1,0:T(8,128)(2,1)S(1)}, bf16[320,1024]{1,0:T(8,128)(2,1)S(1)}) custom-call(bf16[640,8,128]{2,1,0:T(8,128)(2,1)} %bitcast.9.tile_ref, bf16[1024,512]{1,0:T(8,128)(2,1)} %fusion.mine_ref, bf16[1024,512]{1,0:T(8,128)(2,1)} %collective-permute-done.3.other_ref), custom_call_target="tpu_custom_call" | custom-call | flops 1342177280 | bytes 4194304 | tf_op jit(solution)/shard_map/pallas_call | solution.py:289
  71.4 0.2 shard_map.108
  71.6 4.4 %collective-permute-start.4 = (bf16[320,1024]{1,0:T(8,128)(2,1)S(1)}, bf16[320,1024]{1,0:T(8,128)(2,1)S(1)}, u32[]{:S(2)}, u32[]{:S(2)}) collective-permute-start(bf16[320,1024]{1,0:T(8,128)(2,1)S(1)} %get-tuple-element.65), channel_id=1, source_target_pairs={{0,384},{128,256},{256,128},{384,0},{1,385},{129,257},{257,129},{3... | collective-permute-start | bytes 1966088 | tf_op jit(solution)/shard_map/ppermute | solution.py:230
  76.0 1.9 %collective-permute-start.6 = (bf16[320,1024]{1,0:T(8,128)(2,1)S(1)}, bf16[320,1024]{1,0:T(8,128)(2,1)S(1)}, u32[]{:S(2)}, u32[]{:S(2)}) collective-permute-start(bf16[320,1024]{1,0:T(8,128)(2,1)S(1)} %get-tuple-element.76), channel_id=1, source_target_pairs={{0,128},{128,0},{256,384},{384,256},{1,129},{129,1},{257,385},{385... | collective-permute-start | bytes 1966088 | tf_op jit(solution)/shard_map/ppermute | solution.py:230
  78.0 6.8 %collective-permute-done.4 = bf16[320,1024]{1,0:T(8,128)(2,1)S(1)} collective-permute-done((bf16[320,1024]{1,0:T(8,128)(2,1)S(1)}, bf16[320,1024]{1,0:T(8,128)(2,1)S(1)}, u32[]{:S(2)}, u32[]{:S(2)}) %collective-permute-start.4) | collective-permute-done | bytes 655392 | tf_op jit(solution)/shard_map/ppermute | solution.py:230
  84.7 0.2 add_convert_fusion.2.high
  85.0 1.9 %collective-permute-start.8 = (bf16[320,1024]{1,0:T(8,128)(2,1)S(1)}, bf16[320,1024]{1,0:T(8,128)(2,1)S(1)}, u32[]{:S(2)}, u32[]{:S(2)}) collective-permute-start(bf16[320,1024]{1,0:T(8,128)(2,1)S(1)} %add_convert_fusion.2.high), channel_id=1, source_target_pairs={{0,128},{128,0},{256,384},{384,256},{1,129},{129,1},{257,385},{385... | collective-permute-start | bytes 1966088 | tf_op jit(solution)/shard_map/ppermute | solution.py:230
  86.9 0.7 collective-permute-done.6
  87.6 0.2 add_convert_fusion.1.low
  87.9 3.9 %collective-permute-start.7 = (bf16[320,1024]{1,0:T(8,128)(2,1)S(1)}, bf16[320,1024]{1,0:T(8,128)(2,1)S(1)}, u32[]{:S(2)}, u32[]{:S(2)}) collective-permute-start(bf16[320,1024]{1,0:T(8,128)(2,1)S(1)} %add_convert_fusion.1.low), channel_id=1, source_target_pairs={{0,384},{128,256},{256,128},{384,0},{1,385},{129,257},{257,129},{3... | collective-permute-start | bytes 1966088 | tf_op jit(solution)/shard_map/ppermute | solution.py:230
  91.8 4.0 %shard_map.109 = (bf16[640,1024]{1,0:T(8,128)(2,1)S(1)}, bf16[640,1024]{1,0:T(8,128)(2,1)S(1)}, f32[1024,512]{1,0:T(8,128)S(1)}, bf16[1024,512]{1,0:T(8,128)(2,1)S(1)}) custom-call(s32[1]{0:T(128)} %bitcast.core_ref, bf16[2,640,1024]{2,1,0:T(8,128)(2,1)S(1)} %bitcast.63, ...), custom_call_target="tpu_custom_call", output_to_operand_aliasing={{0}: (3, {}), {1}: (4, {}), {2}: (5, {}), {3}: (6, {})} | custom-call | flops 1342177280 | bytes 11534336 | tf_op jit(solution)/shard_map/pallas_call | solution.py:165
  95.8 0.0 copy-start
  95.9 1.4 copy-done
  97.2 6.5 %collective-permute-done.8.high_in = bf16[320,1024]{1,0:T(8,128)(2,1)S(1)} collective-permute-done((bf16[320,1024]{1,0:T(8,128)(2,1)S(1)}, bf16[320,1024]{1,0:T(8,128)(2,1)S(1)}, u32[]{:S(2)}, u32[]{:S(2)}) %collective-permute-start.8) | collective-permute-done | bytes 655392 | tf_op jit(solution)/shard_map/ppermute | solution.py:230
  103.7 0.0 collective-permute-done.7.low_in
  103.7 0.0 copy-done.4
  103.7 4.4 %shard_map.110 = bf16[640,8,128]{2,1,0:T(8,128)(2,1)S(1)} custom-call(bf16[320,1024]{1,0:T(8,128)(2,1)S(1)} %add_convert_fusion.1.low, bf16[320,1024]{1,0:T(8,128)(2,1)S(1)} %collective-permute-done.7.low_in, bf16[320,1024]{1,0:T(8,128)(2,1)S(1)} %add_convert_fusion.2.high, bf16[320,1024]{1,0:T(8,128)(2,1)S(1)} %collective-permute-done.8.high_in, ...), custom_call_target="tpu_custom_call" | custom-call | flops 2684354560 | bytes 6291456 | tf_op jit(solution)/shard_map/pallas_call | solution.py:302
  108.1 0.0 copy-done.7
  108.1 0.0 copy-start.2
  108.1 1.0 copy-done.2
  109.2 9.6 %all-to-all-start.1 = ((bf16[64,80,128]{2,1,0:T(8,128)(2,1)}), bf16[64,80,128]{2,1,0:T(8,128)(2,1)S(1)}, u32[]{:S(2)}, u32[]{:S(2)}) async-start(bf16[64,80,128]{2,1,0:T(8,128)(2,1)} %bitcast.65), calls=%async_computation.1 | async-start | bytes 2621440 | tf_op jit(solution)/shard_map/all_to_all | solution.py:315
  118.8 10.6 %collective-permute-start.5 = (bf16[1024,512]{1,0:T(8,128)(2,1)}, bf16[1024,512]{1,0:T(8,128)(2,1)S(1)}, u32[]{:S(2)}, u32[]{:S(2)}) collective-permute-start(bf16[1024,512]{1,0:T(8,128)(2,1)} %copy-done.7), channel_id=1, source_target_pairs={{0,64},{64,0},{1,65},{65,1},{2,66},{66,2},{3,67},{67,3},{4,68},{68... | collective-permute-start | bytes 3145736 | tf_op jit(solution)/shard_map/ppermute | solution.py:226
  129.4 2.5 %collective-permute-done.5 = bf16[1024,512]{1,0:T(8,128)(2,1)S(1)} collective-permute-done((bf16[1024,512]{1,0:T(8,128)(2,1)}, bf16[1024,512]{1,0:T(8,128)(2,1)S(1)}, u32[]{:S(2)}, u32[]{:S(2)}) %collective-permute-start.5) | collective-permute-done | bytes 1048608 | tf_op jit(solution)/shard_map/ppermute | solution.py:226
  131.9 1.3 fusion.3
  133.2 11.1 %all-to-all-done.1 = bf16[64,80,128]{2,1,0:T(8,128)(2,1)S(1)} async-done(((bf16[64,80,128]{2,1,0:T(8,128)(2,1)}), bf16[64,80,128]{2,1,0:T(8,128)(2,1)S(1)}, u32[]{:S(2)}, u32[]{:S(2)}) %all-to-all-start.1) | async-done | bytes 1310752 | tf_op jit(solution)/shard_map/all_to_all | solution.py:315
  144.3 0.9 copy-done.11
  145.2 1.0 shard_map.111
  146.2 12.5 %collective-permute-start.9 = (bf16[128,512]{1,0:T(8,128)(2,1)S(1)}, bf16[128,512]{1,0:T(8,128)(2,1)S(1)}, u32[]{:S(2)}, u32[]{:S(2)}) collective-permute-start(bf16[128,512]{1,0:T(8,128)(2,1)S(1)} %get-tuple-element.84), channel_id=1, source_target_pairs={{0,64},{64,0},{1,65},{65,1},{2,66},{66,2},{3,67},{67,3},{4,68},{68... | collective-permute-start | bytes 393224 | tf_op jit(solution)/shard_map/ppermute | solution.py:226
  158.7 1.0 collective-permute-done.9
  159.7 0.7 fusion.4
  (25 shorter events, 0.0 us)
Async XLA Ops:
  7.2 50.7 %all-gather.3.cloned.1.call-start = ((), (), s32[]{:S(2)}) async-start(), calls=%async_computation.2 | async-start | bytes 5898240 | tf_op jit(solution)/shard_map/all_gather | solution.py:257
  7.2 0.9 copy-start.12
  8.1 0.7 copy-start.13
  9.2 10.9 %collective-permute-start = (bf16[128,512]{1,0:T(8,128)(2,1)S(1)}, bf16[128,512]{1,0:T(8,128)(2,1)S(1)}, u32[]{:S(2)}, u32[]{:S(2)}) collective-permute-start(bf16[128,512]{1,0:T(8,128)(2,1)S(1)} %shard_map.105.mine_ref), channel_id=1, source_target_pairs={{0,64},{64,0},{1,65},{65,1},{2,66},{66,2},{3,67},{67,3},{4,68},{68... | collective-permute-start | bytes 393224 | tf_op jit(solution)/shard_map/ppermute | solution.py:226
  18.0 0.7 copy-start.14
  18.7 0.7 copy-start.15
  20.1 13.8 %copy-start.19 = (f32[3,1,4,8]{3,2,1,0:T(4,128)S(1)}, f32[3,1,4,8]{3,2,1,0:T(4,128)}, u32[]{:S(2)}) copy-start(f32[3,1,4,8]{3,2,1,0:T(4,128)} %param.17) | copy-start | bytes 1156
  21.9 0.7 copy-start.10
  22.6 11.5 %copy-start.16 = (bf16[1,512,1024]{2,1,0:T(8,128)(2,1)S(1)}, bf16[1,512,1024]{2,1,0:T(8,128)(2,1)}, u32[]{:S(2)}) copy-start(bf16[1,512,1024]{2,1,0:T(8,128)(2,1)} %param.15) | copy-start | bytes 3145732
  22.6 45.1 %all-to-all-start = ((bf16[64,80,128]{2,1,0:T(8,128)(2,1)}), bf16[64,80,128]{2,1,0:T(8,128)(2,1)}, u32[]{:S(2)}, u32[]{:S(2)}) async-start(bf16[64,80,128]{2,1,0:T(8,128)(2,1)} %bitcast.8), calls=%async_computation | async-start | bytes 2621440 | tf_op jit(solution)/shard_map/all_to_all | solution.py:273
  34.9 3.3 %copy-start.3 = (bf16[512,1024]{1,0:T(8,128)(2,1)}, bf16[512,1024]{1,0:T(8,128)(2,1)S(1)}, u32[]{:S(2)}) copy-start(bf16[512,1024]{1,0:T(8,128)(2,1)S(1)} %fusion.1.um_ref) | copy-start | bytes 3145732
  34.9 2.6 %copy-start.17 = (bf16[1,512,1024]{2,1,0:T(8,128)(2,1)S(1)}, bf16[1,512,1024]{2,1,0:T(8,128)(2,1)}, u32[]{:S(2)}) copy-start(bf16[1,512,1024]{2,1,0:T(8,128)(2,1)} %param.14) | copy-start | bytes 3145732
  34.9 5.5 %collective-permute-start.2 = (bf16[512,1024]{1,0:T(8,128)(2,1)S(1)}, bf16[512,1024]{1,0:T(8,128)(2,1)S(1)}, u32[]{:S(2)}, u32[]{:S(2)}) collective-permute-start(bf16[512,1024]{1,0:T(8,128)(2,1)S(1)} %fusion.1.um_ref), channel_id=1, source_target_pairs={{0,64},{64,0},{1,65},{65,1},{2,66},{66,2},{3,67},{67,3},{4,68},{68... | collective-permute-start | bytes 3145736 | tf_op jit(solution)/shard_map/ppermute | solution.py:226
  38.2 6.5 %copy-start.5 = (bf16[512,1024]{1,0:T(8,128)(2,1)}, bf16[512,1024]{1,0:T(8,128)(2,1)S(1)}, u32[]{:S(2)}) copy-start(bf16[512,1024]{1,0:T(8,128)(2,1)S(1)} %fusion.2.gm_ref) | copy-start | bytes 3145732
  38.2 4.8 %collective-permute-start.1 = (bf16[512,1024]{1,0:T(8,128)(2,1)S(1)}, bf16[512,1024]{1,0:T(8,128)(2,1)}, u32[]{:S(2)}, u32[]{:S(2)}) collective-permute-start(bf16[512,1024]{1,0:T(8,128)(2,1)S(1)} %fusion.2.gm_ref), channel_id=1, source_target_pairs={{0,64},{64,0},{1,65},{65,1},{2,66},{66,2},{3,67},{67,3},{4,68},{68... | collective-permute-start | bytes 3145736 | tf_op jit(solution)/shard_map/ppermute | solution.py:226
  40.4 2.9 %copy-start.18 = (bf16[1,1024,512]{2,1,0:T(8,128)(2,1)S(1)}, bf16[1,1024,512]{2,1,0:T(8,128)(2,1)}, u32[]{:S(2)}) copy-start(bf16[1,1024,512]{2,1,0:T(8,128)(2,1)} %param.16) | copy-start | bytes 3145732
  40.4 4.3 %copy-start.8 = (bf16[512,1024]{1,0:T(8,128)(2,1)}, bf16[512,1024]{1,0:T(8,128)(2,1)S(1)}, u32[]{:S(2)}) copy-start(bf16[512,1024]{1,0:T(8,128)(2,1)S(1)} %collective-permute-done.2.uo_ref) | copy-start | bytes 3145732
  44.7 23.1 %collective-permute-start.3 = (bf16[1024,512]{1,0:T(8,128)(2,1)}, bf16[1024,512]{1,0:T(8,128)(2,1)}, u32[]{:S(2)}, u32[]{:S(2)}) collective-permute-start(bf16[1024,512]{1,0:T(8,128)(2,1)} %fusion.mine_ref), channel_id=1, source_target_pairs={{0,64},{64,0},{1,65},{65,1},{2,66},{66,2},{3,67},{67,3},{4,68},{68... | collective-permute-start | bytes 3145736 | tf_op jit(solution)/shard_map/ppermute | solution.py:226
  71.6 13.1 %collective-permute-start.4 = (bf16[320,1024]{1,0:T(8,128)(2,1)S(1)}, bf16[320,1024]{1,0:T(8,128)(2,1)S(1)}, u32[]{:S(2)}, u32[]{:S(2)}) collective-permute-start(bf16[320,1024]{1,0:T(8,128)(2,1)S(1)} %get-tuple-element.65), channel_id=1, source_target_pairs={{0,384},{128,256},{256,128},{384,0},{1,385},{129,257},{257,129},{3... | collective-permute-start | bytes 1966088 | tf_op jit(solution)/shard_map/ppermute | solution.py:230
  76.0 11.6 %collective-permute-start.6 = (bf16[320,1024]{1,0:T(8,128)(2,1)S(1)}, bf16[320,1024]{1,0:T(8,128)(2,1)S(1)}, u32[]{:S(2)}, u32[]{:S(2)}) collective-permute-start(bf16[320,1024]{1,0:T(8,128)(2,1)S(1)} %get-tuple-element.76), channel_id=1, source_target_pairs={{0,128},{128,0},{256,384},{384,256},{1,129},{129,1},{257,385},{385... | collective-permute-start | bytes 1966088 | tf_op jit(solution)/shard_map/ppermute | solution.py:230
  85.0 18.7 %collective-permute-start.8 = (bf16[320,1024]{1,0:T(8,128)(2,1)S(1)}, bf16[320,1024]{1,0:T(8,128)(2,1)S(1)}, u32[]{:S(2)}, u32[]{:S(2)}) collective-permute-start(bf16[320,1024]{1,0:T(8,128)(2,1)S(1)} %add_convert_fusion.2.high), channel_id=1, source_target_pairs={{0,128},{128,0},{256,384},{384,256},{1,129},{129,1},{257,385},{385... | collective-permute-start | bytes 1966088 | tf_op jit(solution)/shard_map/ppermute | solution.py:230
  87.9 15.8 %copy-start.4 = (bf16[512,1024]{1,0:T(8,128)(2,1)S(1)}, bf16[512,1024]{1,0:T(8,128)(2,1)}, u32[]{:S(2)}) copy-start(bf16[512,1024]{1,0:T(8,128)(2,1)} %copy-done.3) | copy-start | bytes 3145732
  87.9 15.8 %copy-start.6 = (bf16[512,1024]{1,0:T(8,128)(2,1)S(1)}, bf16[512,1024]{1,0:T(8,128)(2,1)}, u32[]{:S(2)}) copy-start(bf16[512,1024]{1,0:T(8,128)(2,1)} %copy-done.5) | copy-start | bytes 3145732
  87.9 15.8 %copy-start.9 = (bf16[512,1024]{1,0:T(8,128)(2,1)S(1)}, bf16[512,1024]{1,0:T(8,128)(2,1)}, u32[]{:S(2)}) copy-start(bf16[512,1024]{1,0:T(8,128)(2,1)} %copy-done.8) | copy-start | bytes 3145732
  87.9 15.8 %collective-permute-start.7 = (bf16[320,1024]{1,0:T(8,128)(2,1)S(1)}, bf16[320,1024]{1,0:T(8,128)(2,1)S(1)}, u32[]{:S(2)}, u32[]{:S(2)}) collective-permute-start(bf16[320,1024]{1,0:T(8,128)(2,1)S(1)} %add_convert_fusion.1.low), channel_id=1, source_target_pairs={{0,384},{128,256},{256,128},{384,0},{1,385},{129,257},{257,129},{3... | collective-permute-start | bytes 1966088 | tf_op jit(solution)/shard_map/ppermute | solution.py:230
  95.8 1.4 copy-start
  97.2 10.9 %copy-start.7 = (bf16[1024,512]{1,0:T(8,128)(2,1)}, bf16[1024,512]{1,0:T(8,128)(2,1)S(1)}, u32[]{:S(2)}) copy-start(bf16[1024,512]{1,0:T(8,128)(2,1)S(1)} %get-tuple-element.75) | copy-start | bytes 3145732
  108.1 1.1 copy-start.2
  109.2 22.7 %copy-start.1 = (f32[1024,512]{1,0:T(8,128)S(1)}, f32[1024,512]{1,0:T(8,128)}, u32[]{:S(2)}) copy-start(f32[1024,512]{1,0:T(8,128)} %copy-done) | copy-start | bytes 6291460
  109.2 35.1 %all-to-all-start.1 = ((bf16[64,80,128]{2,1,0:T(8,128)(2,1)}), bf16[64,80,128]{2,1,0:T(8,128)(2,1)S(1)}, u32[]{:S(2)}, u32[]{:S(2)}) async-start(bf16[64,80,128]{2,1,0:T(8,128)(2,1)} %bitcast.65), calls=%async_computation.1 | async-start | bytes 2621440 | tf_op jit(solution)/shard_map/all_to_all | solution.py:315
  118.8 13.1 %collective-permute-start.5 = (bf16[1024,512]{1,0:T(8,128)(2,1)}, bf16[1024,512]{1,0:T(8,128)(2,1)S(1)}, u32[]{:S(2)}, u32[]{:S(2)}) collective-permute-start(bf16[1024,512]{1,0:T(8,128)(2,1)} %copy-done.7), channel_id=1, source_target_pairs={{0,64},{64,0},{1,65},{65,1},{2,66},{66,2},{3,67},{67,3},{4,68},{68... | collective-permute-start | bytes 3145736 | tf_op jit(solution)/shard_map/ppermute | solution.py:226
  144.3 0.9 copy-start.11
  146.2 13.5 %collective-permute-start.9 = (bf16[128,512]{1,0:T(8,128)(2,1)S(1)}, bf16[128,512]{1,0:T(8,128)(2,1)S(1)}, u32[]{:S(2)}, u32[]{:S(2)}) collective-permute-start(bf16[128,512]{1,0:T(8,128)(2,1)S(1)} %get-tuple-element.84), channel_id=1, source_target_pairs={{0,64},{64,0},{1,65},{65,1},{2,66},{66,2},{3,67},{67,3},{4,68},{68... | collective-permute-start | bytes 393224 | tf_op jit(solution)/shard_map/ppermute | solution.py:226
Sparse Core Ops, SparseCore 0:
  10.1 47.7 all-gather.2

commit v6 on v5

--- a/solution.py
+++ b/solution.py
@@ -294,7 +294,7 @@
     )(incoming, down_m, down_o)
 
     side = side_call(0, core, pre, arrived, ())
-    low, high, *side = lax.optimization_barrier((low, high, *side))
+    low, *side = lax.optimization_barrier((low, *side))
     low = added(low, pair(low, 1))
     high = added(high, pair(high, 3))
     high, *side = lax.optimization_barrier((high, *side))

time: 168 us -> 172 us (1.024)
  waiting for transfers between devices: 47.5 us -> 58.9 us
  starting transfers between devices: 71.7 us -> 64.3 us
    all_to_all x1, waiting for transfers between devices: 11.1 us -> 20.5 us  [shards(): lax.all_to_all(sent.reshape(block), EXPERT, 0, 0, tiled=True).reshape(tiles)]
    ppermute x6, starting transfers between devices: 38.7 us -> 29.3 us  [swap(): return lax.ppermute(value, 'core', [(0, 1), (1, 0)])]
    ppermute x4, waiting for transfers between devices: 14 us -> 15.9 us  [pair(): return lax.ppermute(value, 'x', [(i, i ^ mask) for i in range(XS)])]
  transfers between devices with their start and end apart: 13 -> 13, of which waited for: 9 -> 8; matrix products, arithmetic and copies ran while one was open for 6% -> 6% of each run, Pallas kernels for 4% -> 4%
where the time goes in v6:
time: 172 us; the launch traced here: 171 us
  starting transfers between devices  64.3 us (37%)
  waiting for transfers between devices  58.9 us (34%)
  Pallas kernels  16.1 us (9%)
  between operations  14.4 us (8%)
  local copies, waits for them, and re-layouts  12.1 us (7%)
  other arithmetic  5.3 us (3%)
    ppermute x6, starting transfers between devices, swap(): return lax.ppermute(value, 'core', [(0, 1), (1, 0)])  29.3 us
    all_to_all x1, waiting for transfers between devices, shards(): lax.all_to_all(sent.reshape(block), EXPERT, 0, 0, tiled=True).reshape(tiles)  20.5 us
    ppermute x4, waiting for transfers between devices, pair(): return lax.ppermute(value, 'x', [(i, i ^ mask) for i in range(XS)])  15.9 us
    ppermute x4, starting transfers between devices, pair(): return lax.ppermute(value, 'x', [(i, i ^ mask) for i in range(XS)])  12.9 us
    all_to_all x1, starting transfers between devices, shards(): lax.all_to_all(outgoing.reshape(block), EXPERT, 0, 0, tiled=True)  11.3 us
    all_gather x1, waiting for transfers between devices, shards(): pre = lax.all_gather(saved_pre[0], SEQ, axis=0, tiled=True)  10.9 us
    all_to_all x1, starting transfers between devices, shards(): lax.all_to_all(sent.reshape(block), EXPERT, 0, 0, tiled=True).reshape(tiles)  10.8 us
    unnamed x40, local copies, waits for them, and re-layouts  6.99 us
  transfers between devices with their start and end apart: 13, of which 8 were waited for; matrix products, arithmetic and copies ran while one was open for 6% of the time, Pallas kernels for 4%

profile of v6, /device:TPU:1, one launch (start us, length us, event | category | flops | bytes accessed | tf_op | source)
XLA Modules:
  0.0 171.2 jit_solution(4485367646785907777)
XLA Ops:
  7.2 0.0 all-gather.3.cloned.1.call-start
  7.2 0.0 copy-start.12
  7.2 0.9 copy-done.12
  8.1 0.7 copy-done.13
  8.8 0.4 shard_map.105.mine_ref
  9.2 0.0 all-gather.3.cloned.1.call-update
  9.2 8.8 %collective-permute-start = (bf16[128,512]{1,0:T(8,128)(2,1)S(1)}, bf16[128,512]{1,0:T(8,128)(2,1)S(1)}, u32[]{:S(2)}, u32[]{:S(2)}) collective-permute-start(bf16[128,512]{1,0:T(8,128)(2,1)S(1)} %shard_map.105.mine_ref), channel_id=1, source_target_pairs={{0,64},{64,0},{1,65},{65,1},{2,66},{66,2},{3,67},{67,3},{4,68},{68... | collective-permute-start | bytes 393224 | tf_op jit(solution)/shard_map/ppermute | solution.py:226
  18.0 0.0 copy-start.14
  18.1 0.7 copy-done.14
  18.7 0.7 copy-done.15
  19.4 0.7 shard_map.104
  20.1 0.0 collective-permute-done.other_ref
  20.1 0.0 copy-start.19
  20.1 1.8 %shard_map.106 = bf16[640,8,128]{2,1,0:T(8,128)(2,1)} custom-call(bf16[640,128]{1,0:T(8,128)(2,1)S(1)} %get-tuple-element.43.pick_ref, f32[640,128]{1,0:T(8,128)S(1)} %get-tuple-element.44.gate_ref, bf16[128,512]{1,0:T(8,128)(2,1)S(1)} %shard_map.105.mine_ref, bf16[128,512]{1,0:T(8,128)(2,1)S(1)} %collective-permute-done.other_ref), custom_call_target="tpu_custom_call" | custom-call | flops 167772160 | bytes 2097152 | tf_op jit(solution)/shard_map/pallas_call | solution.py:264
  22.0 0.7 copy-done.10
  22.6 11.3 %all-to-all-start = ((bf16[64,80,128]{2,1,0:T(8,128)(2,1)}), bf16[64,80,128]{2,1,0:T(8,128)(2,1)}, u32[]{:S(2)}, u32[]{:S(2)}) async-start(bf16[64,80,128]{2,1,0:T(8,128)(2,1)} %bitcast.8), calls=%async_computation | async-start | bytes 2621440 | tf_op jit(solution)/shard_map/all_to_all | solution.py:273
  33.9 0.2 mul.46
  34.1 0.0 copy-done.16
  34.2 0.7 fusion.1.um_ref
  34.9 0.0 copy-start.3
  34.9 0.0 copy-start.17
  34.9 2.3 %collective-permute-start.2 = (bf16[512,1024]{1,0:T(8,128)(2,1)S(1)}, bf16[512,1024]{1,0:T(8,128)(2,1)S(1)}, u32[]{:S(2)}, u32[]{:S(2)}) collective-permute-start(bf16[512,1024]{1,0:T(8,128)(2,1)S(1)} %fusion.1.um_ref), channel_id=1, source_target_pairs={{0,64},{64,0},{1,65},{65,1},{2,66},{66,2},{3,67},{67,3},{4,68},{68... | collective-permute-start | bytes 3145736 | tf_op jit(solution)/shard_map/ppermute | solution.py:226
  37.2 0.2 mul.42
  37.4 0.7 fusion.2.gm_ref
  38.2 2.1 %collective-permute-start.1 = (bf16[512,1024]{1,0:T(8,128)(2,1)S(1)}, bf16[512,1024]{1,0:T(8,128)(2,1)}, u32[]{:S(2)}, u32[]{:S(2)}) collective-permute-start(bf16[512,1024]{1,0:T(8,128)(2,1)S(1)} %fusion.2.gm_ref), channel_id=1, source_target_pairs={{0,64},{64,0},{1,65},{65,1},{2,66},{66,2},{3,67},{67,3},{4,68},{68... | collective-permute-start | bytes 3145736 | tf_op jit(solution)/shard_map/ppermute | solution.py:226
  40.3 0.1 copy.21
  40.4 0.0 collective-permute-done.2.uo_ref
  40.4 2.5 %collective-permute-done.1.go_ref = bf16[512,1024]{1,0:T(8,128)(2,1)} collective-permute-done((bf16[512,1024]{1,0:T(8,128)(2,1)S(1)}, bf16[512,1024]{1,0:T(8,128)(2,1)}, u32[]{:S(2)}, u32[]{:S(2)}) %collective-permute-start.1) | collective-permute-done | bytes 1048608 | tf_op jit(solution)/shard_map/ppermute | solution.py:226
  43.0 0.3 mul.49
  43.3 1.4 fusion.mine_ref
  44.7 0.0 copy-done.5
  44.7 2.3 %collective-permute-start.3 = (bf16[1024,512]{1,0:T(8,128)(2,1)}, bf16[1024,512]{1,0:T(8,128)(2,1)}, u32[]{:S(2)}, u32[]{:S(2)}) collective-permute-start(bf16[1024,512]{1,0:T(8,128)(2,1)} %fusion.mine_ref), channel_id=1, source_target_pairs={{0,64},{64,0},{1,65},{65,1},{2,66},{66,2},{3,67},{67,3},{4,68},{68... | collective-permute-start | bytes 3145736 | tf_op jit(solution)/shard_map/ppermute | solution.py:226
  47.0 10.9 %all-gather.3.cloned.1.call-done = bf16[1,1280,2,1024]{3,2,0,1:T(2,128)(2,1)} async-done(((bf16[1,160,2,1024]{3,2,0,1:T(2,128)(2,1)}), bf16[1,1280,2,1024]{3,2,0,1:T(2,128)(2,1)}) %all-gather.3.cloned.1.call-update) | async-done | bytes 5242896 | tf_op jit(solution)/shard_map/all_gather | solution.py:257
  57.9 3.5 %constant_dynamic-slice_fusion = bf16[64,10,2,1024]{3,2,1,0:T(2,128)(2,1)S(1)} fusion(bf16[64,20,2,1024]{3,2,1,0:T(2,128)(2,1)} %bitcast.74, s32[]{:T(128)S(6)} %select_n.3), kind=kLoop, calls=%fused_computation.16 | loop fusion | bytes 5242884 | tf_op jit(solution)/shard_map/dynamic_slice | solution.py:282
  61.4 0.8 copy.29
  62.2 5.5 %all-to-all-done = bf16[64,80,128]{2,1,0:T(8,128)(2,1)} async-done(((bf16[64,80,128]{2,1,0:T(8,128)(2,1)}), bf16[64,80,128]{2,1,0:T(8,128)(2,1)}, u32[]{:S(2)}, u32[]{:S(2)}) %all-to-all-start) | async-done | bytes 1310752 | tf_op jit(solution)/shard_map/all_to_all | solution.py:273
  67.8 0.0 collective-permute-done.3.other_ref
  67.8 3.6 %shard_map.107 = (bf16[640,1024]{1,0:T(8,128)(2,1)S(1)}, bf16[320,1024]{1,0:T(8,128)(2,1)S(1)}, bf16[320,1024]{1,0:T(8,128)(2,1)S(1)}) custom-call(bf16[640,8,128]{2,1,0:T(8,128)(2,1)} %bitcast.9.tile_ref, bf16[1024,512]{1,0:T(8,128)(2,1)} %fusion.mine_ref, bf16[1024,512]{1,0:T(8,128)(2,1)} %collective-permute-done.3.other_ref), custom_call_target="tpu_custom_call" | custom-call | flops 1342177280 | bytes 4194304 | tf_op jit(solution)/shard_map/pallas_call | solution.py:289
  71.4 4.4 %collective-permute-start.4 = (bf16[320,1024]{1,0:T(8,128)(2,1)S(1)}, bf16[320,1024]{1,0:T(8,128)(2,1)S(1)}, u32[]{:S(2)}, u32[]{:S(2)}) collective-permute-start(bf16[320,1024]{1,0:T(8,128)(2,1)S(1)} %get-tuple-element.58), channel_id=1, source_target_pairs={{0,384},{128,256},{256,128},{384,0},{1,385},{129,257},{257,129},{3... | collective-permute-start | bytes 1966088 | tf_op jit(solution)/shard_map/ppermute | solution.py:230
  75.8 0.2 shard_map.108
  76.0 1.9 %collective-permute-start.6 = (bf16[320,1024]{1,0:T(8,128)(2,1)S(1)}, bf16[320,1024]{1,0:T(8,128)(2,1)S(1)}, u32[]{:S(2)}, u32[]{:S(2)}) collective-permute-start(bf16[320,1024]{1,0:T(8,128)(2,1)S(1)} %get-tuple-element.74), channel_id=1, source_target_pairs={{0,128},{128,0},{256,384},{384,256},{1,129},{129,1},{257,385},{385... | collective-permute-start | bytes 1966088 | tf_op jit(solution)/shard_map/ppermute | solution.py:230
  78.0 10.5 %collective-permute-done.4 = bf16[320,1024]{1,0:T(8,128)(2,1)S(1)} collective-permute-done((bf16[320,1024]{1,0:T(8,128)(2,1)S(1)}, bf16[320,1024]{1,0:T(8,128)(2,1)S(1)}, u32[]{:S(2)}, u32[]{:S(2)}) %collective-permute-start.4) | collective-permute-done | bytes 655392 | tf_op jit(solution)/shard_map/ppermute | solution.py:230
  88.4 0.2 add_convert_fusion.2.high
  88.7 1.9 %collective-permute-start.8 = (bf16[320,1024]{1,0:T(8,128)(2,1)S(1)}, bf16[320,1024]{1,0:T(8,128)(2,1)S(1)}, u32[]{:S(2)}, u32[]{:S(2)}) collective-permute-start(bf16[320,1024]{1,0:T(8,128)(2,1)S(1)} %add_convert_fusion.2.high), channel_id=1, source_target_pairs={{0,128},{128,0},{256,384},{384,256},{1,129},{129,1},{257,385},{385... | collective-permute-start | bytes 1966088 | tf_op jit(solution)/shard_map/ppermute | solution.py:230
  90.6 0.0 collective-permute-done.6
  90.6 0.2 add_convert_fusion.1.low
  90.9 4.6 %collective-permute-start.7 = (bf16[320,1024]{1,0:T(8,128)(2,1)S(1)}, bf16[320,1024]{1,0:T(8,128)(2,1)S(1)}, u32[]{:S(2)}, u32[]{:S(2)}) collective-permute-start(bf16[320,1024]{1,0:T(8,128)(2,1)S(1)} %add_convert_fusion.1.low), channel_id=1, source_target_pairs={{0,384},{128,256},{256,128},{384,0},{1,385},{129,257},{257,129},{3... | collective-permute-start | bytes 1966088 | tf_op jit(solution)/shard_map/ppermute | solution.py:230
  95.6 4.0 %shard_map.109 = (bf16[640,1024]{1,0:T(8,128)(2,1)S(1)}, bf16[640,1024]{1,0:T(8,128)(2,1)S(1)}, f32[1024,512]{1,0:T(8,128)S(1)}, bf16[1024,512]{1,0:T(8,128)(2,1)S(1)}) custom-call(s32[1]{0:T(128)} %bitcast.core_ref, bf16[2,640,1024]{2,1,0:T(8,128)(2,1)S(1)} %bitcast.63, ...), custom_call_target="tpu_custom_call", output_to_operand_aliasing={{0}: (3, {}), {1}: (4, {}), {2}: (5, {}), {3}: (6, {})} | custom-call | flops 1342177280 | bytes 11534336 | tf_op jit(solution)/shard_map/pallas_call | solution.py:165
  99.6 1.4 copy-done
  100.9 5.4 %collective-permute-done.8.high_in = bf16[320,1024]{1,0:T(8,128)(2,1)S(1)} collective-permute-done((bf16[320,1024]{1,0:T(8,128)(2,1)S(1)}, bf16[320,1024]{1,0:T(8,128)(2,1)S(1)}, u32[]{:S(2)}, u32[]{:S(2)}) %collective-permute-start.8) | collective-permute-done | bytes 655392 | tf_op jit(solution)/shard_map/ppermute | solution.py:230
  106.4 0.0 collective-permute-done.7.low_in
  106.4 0.0 copy-done.9
  106.4 4.4 %shard_map.110 = bf16[640,8,128]{2,1,0:T(8,128)(2,1)S(1)} custom-call(bf16[320,1024]{1,0:T(8,128)(2,1)S(1)} %add_convert_fusion.1.low, bf16[320,1024]{1,0:T(8,128)(2,1)S(1)} %collective-permute-done.7.low_in, bf16[320,1024]{1,0:T(8,128)(2,1)S(1)} %add_convert_fusion.2.high, bf16[320,1024]{1,0:T(8,128)(2,1)S(1)} %collective-permute-done.8.high_in, ...), custom_call_target="tpu_custom_call" | custom-call | flops 2684354560 | bytes 6291456 | tf_op jit(solution)/shard_map/pallas_call | solution.py:302
  110.8 1.0 copy-done.2
  111.8 10.8 %all-to-all-start.1 = ((bf16[64,80,128]{2,1,0:T(8,128)(2,1)}), bf16[64,80,128]{2,1,0:T(8,128)(2,1)S(1)}, u32[]{:S(2)}, u32[]{:S(2)}) async-start(bf16[64,80,128]{2,1,0:T(8,128)(2,1)} %bitcast.65), calls=%async_computation.1 | async-start | bytes 2621440 | tf_op jit(solution)/shard_map/all_to_all | solution.py:315
  122.7 6.0 %collective-permute-start.5 = (bf16[1024,512]{1,0:T(8,128)(2,1)}, bf16[1024,512]{1,0:T(8,128)(2,1)S(1)}, u32[]{:S(2)}, u32[]{:S(2)}) collective-permute-start(bf16[1024,512]{1,0:T(8,128)(2,1)} %copy-done.7), channel_id=1, source_target_pairs={{0,64},{64,0},{1,65},{65,1},{2,66},{66,2},{3,67},{67,3},{4,68},{68... | collective-permute-start | bytes 3145736 | tf_op jit(solution)/shard_map/ppermute | solution.py:226
  128.7 2.5 %collective-permute-done.5 = bf16[1024,512]{1,0:T(8,128)(2,1)S(1)} collective-permute-done((bf16[1024,512]{1,0:T(8,128)(2,1)}, bf16[1024,512]{1,0:T(8,128)(2,1)S(1)}, u32[]{:S(2)}, u32[]{:S(2)}) %collective-permute-start.5) | collective-permute-done | bytes 1048608 | tf_op jit(solution)/shard_map/ppermute | solution.py:226
  131.2 1.3 fusion.3
  132.5 20.5 %all-to-all-done.1 = bf16[64,80,128]{2,1,0:T(8,128)(2,1)S(1)} async-done(((bf16[64,80,128]{2,1,0:T(8,128)(2,1)}), bf16[64,80,128]{2,1,0:T(8,128)(2,1)S(1)}, u32[]{:S(2)}, u32[]{:S(2)}) %all-to-all-start.1) | async-done | bytes 1310752 | tf_op jit(solution)/shard_map/all_to_all | solution.py:315
  153.1 0.9 copy-done.11
  154.0 1.0 shard_map.111
  155.0 7.7 %collective-permute-start.9 = (bf16[128,512]{1,0:T(8,128)(2,1)S(1)}, bf16[128,512]{1,0:T(8,128)(2,1)S(1)}, u32[]{:S(2)}, u32[]{:S(2)}) collective-permute-start(bf16[128,512]{1,0:T(8,128)(2,1)S(1)} %get-tuple-element.82), channel_id=1, source_target_pairs={{0,64},{64,0},{1,65},{65,1},{2,66},{66,2},{3,67},{67,3},{4,68},{68... | collective-permute-start | bytes 393224 | tf_op jit(solution)/shard_map/ppermute | solution.py:226
  162.7 1.0 collective-permute-done.9
  163.7 0.7 fusion.4
  (25 shorter events, 0.0 us)
Async XLA Ops:
  7.2 50.7 %all-gather.3.cloned.1.call-start = ((), (), s32[]{:S(2)}) async-start(), calls=%async_computation.2 | async-start | bytes 5898240 | tf_op jit(solution)/shard_map/all_gather | solution.py:257
  7.2 0.9 copy-start.12
  8.1 0.7 copy-start.13
  9.2 10.9 %collective-permute-start = (bf16[128,512]{1,0:T(8,128)(2,1)S(1)}, bf16[128,512]{1,0:T(8,128)(2,1)S(1)}, u32[]{:S(2)}, u32[]{:S(2)}) collective-permute-start(bf16[128,512]{1,0:T(8,128)(2,1)S(1)} %shard_map.105.mine_ref), channel_id=1, source_target_pairs={{0,64},{64,0},{1,65},{65,1},{2,66},{66,2},{3,67},{67,3},{4,68},{68... | collective-permute-start | bytes 393224 | tf_op jit(solution)/shard_map/ppermute | solution.py:226
  18.0 0.7 copy-start.14
  18.7 0.7 copy-start.15
  20.1 13.8 %copy-start.19 = (f32[3,1,4,8]{3,2,1,0:T(4,128)S(1)}, f32[3,1,4,8]{3,2,1,0:T(4,128)}, u32[]{:S(2)}) copy-start(f32[3,1,4,8]{3,2,1,0:T(4,128)} %param.17) | copy-start | bytes 1156
  21.9 0.7 copy-start.10
  22.6 11.5 %copy-start.16 = (bf16[1,512,1024]{2,1,0:T(8,128)(2,1)S(1)}, bf16[1,512,1024]{2,1,0:T(8,128)(2,1)}, u32[]{:S(2)}) copy-start(bf16[1,512,1024]{2,1,0:T(8,128)(2,1)} %param.15) | copy-start | bytes 3145732
  22.6 45.1 %all-to-all-start = ((bf16[64,80,128]{2,1,0:T(8,128)(2,1)}), bf16[64,80,128]{2,1,0:T(8,128)(2,1)}, u32[]{:S(2)}, u32[]{:S(2)}) async-start(bf16[64,80,128]{2,1,0:T(8,128)(2,1)} %bitcast.8), calls=%async_computation | async-start | bytes 2621440 | tf_op jit(solution)/shard_map/all_to_all | solution.py:273
  34.9 3.3 %copy-start.3 = (bf16[512,1024]{1,0:T(8,128)(2,1)}, bf16[512,1024]{1,0:T(8,128)(2,1)S(1)}, u32[]{:S(2)}) copy-start(bf16[512,1024]{1,0:T(8,128)(2,1)S(1)} %fusion.1.um_ref) | copy-start | bytes 3145732
  34.9 2.6 %copy-start.17 = (bf16[1,512,1024]{2,1,0:T(8,128)(2,1)S(1)}, bf16[1,512,1024]{2,1,0:T(8,128)(2,1)}, u32[]{:S(2)}) copy-start(bf16[1,512,1024]{2,1,0:T(8,128)(2,1)} %param.14) | copy-start | bytes 3145732
  34.9 5.5 %collective-permute-start.2 = (bf16[512,1024]{1,0:T(8,128)(2,1)S(1)}, bf16[512,1024]{1,0:T(8,128)(2,1)S(1)}, u32[]{:S(2)}, u32[]{:S(2)}) collective-permute-start(bf16[512,1024]{1,0:T(8,128)(2,1)S(1)} %fusion.1.um_ref), channel_id=1, source_target_pairs={{0,64},{64,0},{1,65},{65,1},{2,66},{66,2},{3,67},{67,3},{4,68},{68... | collective-permute-start | bytes 3145736 | tf_op jit(solution)/shard_map/ppermute | solution.py:226
  38.2 6.5 %copy-start.5 = (bf16[512,1024]{1,0:T(8,128)(2,1)}, bf16[512,1024]{1,0:T(8,128)(2,1)S(1)}, u32[]{:S(2)}) copy-start(bf16[512,1024]{1,0:T(8,128)(2,1)S(1)} %fusion.2.gm_ref) | copy-start | bytes 3145732
  38.2 4.8 %collective-permute-start.1 = (bf16[512,1024]{1,0:T(8,128)(2,1)S(1)}, bf16[512,1024]{1,0:T(8,128)(2,1)}, u32[]{:S(2)}, u32[]{:S(2)}) collective-permute-start(bf16[512,1024]{1,0:T(8,128)(2,1)S(1)} %fusion.2.gm_ref), channel_id=1, source_target_pairs={{0,64},{64,0},{1,65},{65,1},{2,66},{66,2},{3,67},{67,3},{4,68},{68... | collective-permute-start | bytes 3145736 | tf_op jit(solution)/shard_map/ppermute | solution.py:226
  40.4 2.9 %copy-start.18 = (bf16[1,1024,512]{2,1,0:T(8,128)(2,1)S(1)}, bf16[1,1024,512]{2,1,0:T(8,128)(2,1)}, u32[]{:S(2)}) copy-start(bf16[1,1024,512]{2,1,0:T(8,128)(2,1)} %param.16) | copy-start | bytes 3145732
  40.4 4.3 %copy-start.8 = (bf16[512,1024]{1,0:T(8,128)(2,1)}, bf16[512,1024]{1,0:T(8,128)(2,1)S(1)}, u32[]{:S(2)}) copy-start(bf16[512,1024]{1,0:T(8,128)(2,1)S(1)} %collective-permute-done.2.uo_ref) | copy-start | bytes 3145732
  44.7 23.1 %collective-permute-start.3 = (bf16[1024,512]{1,0:T(8,128)(2,1)}, bf16[1024,512]{1,0:T(8,128)(2,1)}, u32[]{:S(2)}, u32[]{:S(2)}) collective-permute-start(bf16[1024,512]{1,0:T(8,128)(2,1)} %fusion.mine_ref), channel_id=1, source_target_pairs={{0,64},{64,0},{1,65},{65,1},{2,66},{66,2},{3,67},{67,3},{4,68},{68... | collective-permute-start | bytes 3145736 | tf_op jit(solution)/shard_map/ppermute | solution.py:226
  71.4 17.0 %collective-permute-start.4 = (bf16[320,1024]{1,0:T(8,128)(2,1)S(1)}, bf16[320,1024]{1,0:T(8,128)(2,1)S(1)}, u32[]{:S(2)}, u32[]{:S(2)}) collective-permute-start(bf16[320,1024]{1,0:T(8,128)(2,1)S(1)} %get-tuple-element.58), channel_id=1, source_target_pairs={{0,384},{128,256},{256,128},{384,0},{1,385},{129,257},{257,129},{3... | collective-permute-start | bytes 1966088 | tf_op jit(solution)/shard_map/ppermute | solution.py:230
  76.0 14.6 %collective-permute-start.6 = (bf16[320,1024]{1,0:T(8,128)(2,1)S(1)}, bf16[320,1024]{1,0:T(8,128)(2,1)S(1)}, u32[]{:S(2)}, u32[]{:S(2)}) collective-permute-start(bf16[320,1024]{1,0:T(8,128)(2,1)S(1)} %get-tuple-element.74), channel_id=1, source_target_pairs={{0,128},{128,0},{256,384},{384,256},{1,129},{129,1},{257,385},{385... | collective-permute-start | bytes 1966088 | tf_op jit(solution)/shard_map/ppermute | solution.py:230
  88.7 17.7 %collective-permute-start.8 = (bf16[320,1024]{1,0:T(8,128)(2,1)S(1)}, bf16[320,1024]{1,0:T(8,128)(2,1)S(1)}, u32[]{:S(2)}, u32[]{:S(2)}) collective-permute-start(bf16[320,1024]{1,0:T(8,128)(2,1)S(1)} %add_convert_fusion.2.high), channel_id=1, source_target_pairs={{0,128},{128,0},{256,384},{384,256},{1,129},{129,1},{257,385},{385... | collective-permute-start | bytes 1966088 | tf_op jit(solution)/shard_map/ppermute | solution.py:230
  90.9 15.5 %copy-start.4 = (bf16[512,1024]{1,0:T(8,128)(2,1)S(1)}, bf16[512,1024]{1,0:T(8,128)(2,1)}, u32[]{:S(2)}) copy-start(bf16[512,1024]{1,0:T(8,128)(2,1)} %copy-done.3) | copy-start | bytes 3145732
  90.9 15.5 %copy-start.6 = (bf16[512,1024]{1,0:T(8,128)(2,1)S(1)}, bf16[512,1024]{1,0:T(8,128)(2,1)}, u32[]{:S(2)}) copy-start(bf16[512,1024]{1,0:T(8,128)(2,1)} %copy-done.5) | copy-start | bytes 3145732
  90.9 15.5 %copy-start.9 = (bf16[512,1024]{1,0:T(8,128)(2,1)S(1)}, bf16[512,1024]{1,0:T(8,128)(2,1)}, u32[]{:S(2)}) copy-start(bf16[512,1024]{1,0:T(8,128)(2,1)} %copy-done.8) | copy-start | bytes 3145732
  90.9 15.5 %collective-permute-start.7 = (bf16[320,1024]{1,0:T(8,128)(2,1)S(1)}, bf16[320,1024]{1,0:T(8,128)(2,1)S(1)}, u32[]{:S(2)}, u32[]{:S(2)}) collective-permute-start(bf16[320,1024]{1,0:T(8,128)(2,1)S(1)} %add_convert_fusion.1.low), channel_id=1, source_target_pairs={{0,384},{128,256},{256,128},{384,0},{1,385},{129,257},{257,129},{3... | collective-permute-start | bytes 1966088 | tf_op jit(solution)/shard_map/ppermute | solution.py:230
  99.6 1.4 copy-start
  100.9 9.8 %copy-start.7 = (bf16[1024,512]{1,0:T(8,128)(2,1)}, bf16[1024,512]{1,0:T(8,128)(2,1)S(1)}, u32[]{:S(2)}) copy-start(bf16[1024,512]{1,0:T(8,128)(2,1)S(1)} %get-tuple-element.73) | copy-start | bytes 3145732
  110.8 1.1 copy-start.2
  111.8 19.4 %copy-start.1 = (f32[1024,512]{1,0:T(8,128)S(1)}, f32[1024,512]{1,0:T(8,128)}, u32[]{:S(2)}) copy-start(f32[1024,512]{1,0:T(8,128)} %copy-done) | copy-start | bytes 6291460
  111.8 41.2 %all-to-all-start.1 = ((bf16[64,80,128]{2,1,0:T(8,128)(2,1)}), bf16[64,80,128]{2,1,0:T(8,128)(2,1)S(1)}, u32[]{:S(2)}, u32[]{:S(2)}) async-start(bf16[64,80,128]{2,1,0:T(8,128)(2,1)} %bitcast.65), calls=%async_computation.1 | async-start | bytes 2621440 | tf_op jit(solution)/shard_map/all_to_all | solution.py:315
  122.7 8.5 %collective-permute-start.5 = (bf16[1024,512]{1,0:T(8,128)(2,1)}, bf16[1024,512]{1,0:T(8,128)(2,1)S(1)}, u32[]{:S(2)}, u32[]{:S(2)}) collective-permute-start(bf16[1024,512]{1,0:T(8,128)(2,1)} %copy-done.7), channel_id=1, source_target_pairs={{0,64},{64,0},{1,65},{65,1},{2,66},{66,2},{3,67},{67,3},{4,68},{68... | collective-permute-start | bytes 3145736 | tf_op jit(solution)/shard_map/ppermute | solution.py:226
  153.0 0.9 copy-start.11
  155.0 8.7 %collective-permute-start.9 = (bf16[128,512]{1,0:T(8,128)(2,1)S(1)}, bf16[128,512]{1,0:T(8,128)(2,1)S(1)}, u32[]{:S(2)}, u32[]{:S(2)}) collective-permute-start(bf16[128,512]{1,0:T(8,128)(2,1)S(1)} %get-tuple-element.82), channel_id=1, source_target_pairs={{0,64},{64,0},{1,65},{65,1},{2,66},{66,2},{3,67},{67,3},{4,68},{68... | collective-permute-start | bytes 393224 | tf_op jit(solution)/shard_map/ppermute | solution.py:226
Sparse Core Ops, SparseCore 0:
  10.1 47.7 all-gather.2
